TPU v7x, 32 devices: a whole 2x2x4 slice. The times are simulated.
32 devices in a mesh: brick: 16 (over z, x, core), relay: 2 (over y).
Axes of the slice: x: 2, y: 2, z: 4, core: 2. Of those that a mesh axis runs over, the one named last changes fastest.
Arguments:
- target: float32 [8, 128, 1536], P('relay', 'brick'), may hold values from 0.1 to 9, as said below
- frag_brick: int32 [2048, 1], P(('brick', 'relay')), may hold values from 0 to 15; in each aligned block of 64 rows (0 to 63, 64 to 127, ...) at most 8 rows name the same one
- bead_cell: int32 [2048, 128], P(('brick', 'relay')), may hold values from 0 to 49151
- bead_weight: bfloat16 [2048, 128], P(('brick', 'relay')), may hold values from 0.29882812 to 3
- bead_arm: float32 [3, 2048, 128], P(None, ('brick', 'relay')), may hold values from -12 to 12
- frag_angle: float32 [3, 2048], P(None, ('brick', 'relay')), may hold values from -3.140625 to 3.140625
Outputs:
- frag_grad: float32 [6, 2048], P(None, ('brick', 'relay'))
Inputs may be any that keep to these rules, and one draw needn't show every extreme that they name: `frag_brick`: each device's 64 fragments name at most 8 fragments for one strip. `bead_cell`: A bead's voxel numbered (plane * 8 + x) * 1536 + y within the block of its fragment's strip on its owner's relay index. `target`: positive map intensity.
All inputs are finite; a program needn't handle non-finite values.
Results may differ from a plain program's by a relative error of at most 0.0003.
Values may be sent and summed in bfloat16 or wider, within the bound.
No kernel may reach another device: no remote copies, remote signals or barrier semaphores. Data moves between devices by JAX's collectives and lax.ppermute only.
A program may use at most 128 MiB of HBM per device.

v0:
```python
import jax
import jax.numpy as jnp
import numpy as np
from jax import lax
from jax.sharding import PartitionSpec as P

KR = 4


SIGMA = 1.5
EPSILON = 1e-06
HIGHEST = lax.Precision.HIGHEST


def padded_2(value, sides, width):
    for axis, dim in sides:
        size, length = (lax.axis_size(axis), value.shape[dim])
        up = [(i, (i + 1) % size) for i in range(size - 1)]
        down = [(j, i) for i, j in up]
        last = lax.slice_in_dim(value, length - width, length, axis=dim)
        first = lax.slice_in_dim(value, 0, width, axis=dim)
        before = lax.ppermute(last, axis, up)
        after = lax.ppermute(first, axis, down)
        value = jnp.concatenate([before, value, after], axis=dim)
    return value


def kernel_values(half_width, derivative):
    offsets = np.arange(-half_width, half_width + 1) * 1.0
    gaussian = np.exp(-(offsets**2) / (2.0 * SIGMA**2))
    gaussian = gaussian / gaussian.sum()
    if derivative:
        return -offsets / SIGMA**2 * gaussian
    return gaussian


def band_matrix(derivative, out_len, in_len, offset_base):
    taps = kernel_values(KR, derivative)
    out_ids = np.arange(out_len)[:, None]
    in_ids = np.arange(in_len)[None, :]
    offsets = out_ids + offset_base - in_ids
    inside = np.abs(offsets) <= KR
    band_table = np.where(inside, taps[np.clip(offsets + KR, 0, 2 * KR)], 0.0)
    return jnp.asarray(band_table, jnp.float32)


def blur(volume, along_dim, derivative, padded):
    in_len = volume.shape[along_dim]
    out_len = in_len - 2 * KR if padded else in_len
    if along_dim == 1:
        matrix = band_matrix(derivative, out_len, in_len, KR)
        return jnp.einsum(
            "az,kzxy->kaxy", matrix, volume, precision=HIGHEST, preferred_element_type=jnp.float32
        )
    if along_dim == 2:
        matrix = band_matrix(derivative, out_len, in_len, KR)
        return jnp.einsum(
            "ax,kzxy->kzay", matrix, volume, precision=HIGHEST, preferred_element_type=jnp.float32
        )
    tile_len = min(128, in_len)
    tile_count = in_len // tile_len
    widened = jnp.pad(volume, ((0, 0), (0, 0), (0, 0), (KR, KR)))
    windows = jnp.stack(
        [
            lax.slice_in_dim(
                widened, tile_id * tile_len, tile_id * tile_len + tile_len + 2 * KR, axis=3
            )
            for tile_id in range(tile_count)
        ],
        axis=3,
    )
    matrix = band_matrix(derivative, tile_len, tile_len + 2 * KR, KR)
    tiled = jnp.einsum(
        "kzxcj,aj->kzxca", windows, matrix, precision=HIGHEST, preferred_element_type=jnp.float32
    )
    return tiled.reshape(volume.shape)


def widen(stacked):
    return padded_2(stacked, (("brick", 2),), KR)


def deepen(stacked):
    return padded_2(stacked, (("relay", 1),), KR)


def splat(cell_ids, weight_ids, line_count, row_count):
    slot_total = cell_ids.shape[0]
    block_len = min(2048, slot_total)
    line_axis = jnp.arange(line_count, dtype=jnp.int32)
    row_axis = jnp.arange(row_count, dtype=jnp.int32)

    def add_block(block_id, total):
        cell_part = lax.dynamic_slice_in_dim(cell_ids, block_id * block_len, block_len)
        weight_part = lax.dynamic_slice_in_dim(weight_ids, block_id * block_len, block_len)
        line_table = ((cell_part // row_count)[:, None] == line_axis[None, :]).astype(jnp.bfloat16)
        col_table = jnp.where(
            (cell_part % row_count)[:, None] == row_axis[None, :],
            weight_part[:, None],
            jnp.zeros((), jnp.bfloat16),
        )
        return total + lax.dot_general(
            line_table, col_table, (((0,), (0,)), ((), ())), preferred_element_type=jnp.float32
        )

    return lax.fori_loop(
        0, slot_total // block_len, add_block, jnp.zeros((line_count, row_count), jnp.float32)
    )


def correlate(model_map, target, voxel_total):
    cross, model_sq, target_sq = lax.psum(
        (jnp.sum(model_map * target), jnp.sum(model_map * model_map), jnp.sum(target * target)),
        ("brick", "relay"),
    )
    norm_model = jnp.sqrt(model_sq + EPSILON)
    norm_target = jnp.sqrt(target_sq + EPSILON)
    corr = cross / (norm_model * norm_target)
    return voxel_total * (
        target / (norm_model * norm_target) - corr * model_map / (norm_model * norm_model)
    )


def rotate_arms(angles, arms):
    cos_a, sin_a = (jnp.cos(angles[0]), jnp.sin(angles[0]))
    cos_b, sin_b = (jnp.cos(angles[1]), jnp.sin(angles[1]))
    cos_c, sin_c = (jnp.cos(angles[2]), jnp.sin(angles[2]))
    rot_rows = [
        [
            cos_a * cos_b,
            cos_a * sin_b * sin_c - sin_a * cos_c,
            cos_a * sin_b * cos_c + sin_a * sin_c,
        ],
        [
            sin_a * cos_b,
            sin_a * sin_b * sin_c + cos_a * cos_c,
            sin_a * sin_b * cos_c - cos_a * sin_c,
        ],
        [-sin_b, cos_b * sin_c, cos_b * cos_c],
    ]
    return [
        sum((rot_rows[row_id][col_id][:, None] * arms[col_id] for col_id in range(3)))
        for row_id in range(3)
    ]


def fragment_gradient(force, angles, arms):
    lever = rotate_arms(angles, arms)
    torque_x = jnp.sum(lever[1] * force[2] - lever[2] * force[1], axis=1)
    torque_y = jnp.sum(lever[2] * force[0] - lever[0] * force[2], axis=1)
    torque_z = jnp.sum(lever[0] * force[1] - lever[1] * force[0], axis=1)
    return jnp.stack(
        [
            jnp.sum(force[0], axis=1),
            jnp.sum(force[1], axis=1),
            jnp.sum(force[2], axis=1),
            torque_x,
            torque_y,
            torque_z,
        ]
    )


def shards(target, frag_brick, bead_cell, bead_weight, bead_arm, frag_angle):
    brick_count = lax.axis_size("brick")
    relay_count = lax.axis_size("relay")
    frag_count, bead_count = bead_cell.shape
    plane_count, column_count, row_count = target.shape
    voxel_total = float(brick_count * column_count * relay_count * plane_count * row_count)
    most_rows = max(2, 2 * frag_count // brick_count)
    slot_count = brick_count * most_rows
    brick_of = frag_brick[:, 0]
    frag_ids = jnp.arange(frag_count, dtype=jnp.int32)
    same_brick = brick_of[:, None] == brick_of[None, :]
    earlier = frag_ids[None, :] < frag_ids[:, None]
    slot_rank = jnp.sum(jnp.logical_and(same_brick, earlier).astype(jnp.int32), axis=1)
    slot_of = brick_of * most_rows + slot_rank
    send_weight = jnp.zeros((slot_count, bead_count), jnp.bfloat16).at[slot_of].set(bead_weight)
    send_cell = jnp.zeros((slot_count, bead_count), jnp.int32).at[slot_of].set(bead_cell)
    got_weight, got_cell = (
        lax.all_to_all(send_weight, "brick", split_axis=0, concat_axis=0, tiled=True),
        lax.all_to_all(send_cell, "brick", split_axis=0, concat_axis=0, tiled=True),
    )
    cell_ids = got_cell.reshape(-1)
    weight_ids = got_weight.reshape(-1)
    density = splat(cell_ids, weight_ids, plane_count * column_count, row_count)
    density = density.reshape(1, plane_count, column_count, row_count)
    smooth = blur(density, 3, False, False)
    smooth = blur(widen(smooth), 2, False, True)
    model_map = blur(deepen(smooth), 1, False, True)[0]
    residual = correlate(model_map, target, voxel_total)
    widened = deepen(residual[None])
    along_z = blur(widened, 1, False, True)[0]
    slope_z = blur(widened, 1, True, True)[0]
    paired = jnp.stack([along_z, slope_z])
    smooth_y = blur(paired, 3, False, False)
    slope_y = blur(paired[0:1], 3, True, False)
    ready = widen(jnp.concatenate([smooth_y[0:1], slope_y, smooth_y[1:2]], axis=0))
    grad_x = blur(ready[0:1], 2, True, True)
    grad_rest = blur(ready[1:3], 2, False, True)
    grad_fields = jnp.concatenate([grad_x, grad_rest], axis=0).reshape(3, -1)
    sampled = jnp.take(grad_fields, cell_ids, axis=1)
    force = (sampled * weight_ids.astype(jnp.float32)[None, :]).reshape(3, slot_count, bead_count)
    returned = lax.all_to_all(force, "brick", split_axis=1, concat_axis=1, tiled=True)
    own_force = returned[:, slot_of, :]
    return fragment_gradient(own_force, frag_angle, bead_arm)


def solution(mesh):
    placed = (
        P("relay", "brick", None),
        P(("brick", "relay"), None),
        P(("brick", "relay"), None),
        P(("brick", "relay"), None),
        P(None, ("brick", "relay"), None),
        P(None, ("brick", "relay")),
    )
    return jax.shard_map(
        shards, mesh=mesh, in_specs=placed, out_specs=P(None, ("brick", "relay")), check_vma=False
    )
```

profile of v0, /device:TPU:0, one launch (start us, length us, event | category | flops | bytes accessed | tf_op | source)
XLA Modules:
  0.0 238.3 jit_solution(13137674226800955982)
XLA Ops:
  1.6 1.5 scatter_custom_fusion.1
  3.1 7.4 %all-to-all-start.1 = ((bf16[16,8,128]{2,1,0:T(8,128)(2,1)}), bf16[16,8,128]{2,1,0:T(8,128)(2,1)S(1)}, u32[]{:S(2)}, u32[]{:S(2)}) async-start(bf16[16,8,128]{2,1,0:T(8,128)(2,1)} %bitcast.6), calls=%async_computation.1 | async-start | bytes 65536 | tf_op jit(solution)/shard_map/all_to_all | solution.py:181
  10.4 1.5 scatter_custom_fusion
  12.0 5.1 %all-to-all-done.1 = bf16[16,8,128]{2,1,0:T(8,128)(2,1)S(1)} async-done(((bf16[16,8,128]{2,1,0:T(8,128)(2,1)}), bf16[16,8,128]{2,1,0:T(8,128)(2,1)S(1)}, u32[]{:S(2)}, u32[]{:S(2)}) %all-to-all-start.1) | async-done | bytes 32800 | tf_op jit(solution)/shard_map/all_to_all | solution.py:181
  17.1 3.5 %all-to-all-start = ((s32[16,8,128]{2,1,0:T(8,128)}), s32[16,8,128]{2,1,0:T(8,128)S(1)}, u32[]{:S(2)}, u32[]{:S(2)}) async-start(s32[16,8,128]{2,1,0:T(8,128)} %bitcast.3), calls=%async_computation | async-start | bytes 131072 | tf_op jit(solution)/shard_map/all_to_all | solution.py:182
  21.4 6.0 %all-to-all-done = s32[16,8,128]{2,1,0:T(8,128)S(1)} async-done(((s32[16,8,128]{2,1,0:T(8,128)}), s32[16,8,128]{2,1,0:T(8,128)S(1)}, u32[]{:S(2)}, u32[]{:S(2)}) %all-to-all-start) | async-done | bytes 65568 | tf_op jit(solution)/shard_map/all_to_all | solution.py:182
  27.4 16.5 %while.16 = (s32[]{:T(128)}, f32[32,1536]{1,0:T(8,128)S(1)}, s32[16384]{0:T(1024)S(1)}, bf16[16384]{0:T(1024)(128)(2,1)S(1)}, s32[]{:T(128)}, /*index=5*/s32[]{:T(128)}, s32[]{:T(128)}, s32[]{:T(128)}) while((s32[]{:T(128)}, f32[32,1536]{1,0:T(8,128)S(1)}, s32[16384]{0:T(1024)S(1)}, bf16[16384]{0:T(1024)(128)(2,1)S(1)}, s32[]{:T(128)}, ...), condition=%wide.region_4.5_spmd.clone, body=%wide.region_3.4_spmd.clone.sunk | while | flops 207806464 | bytes 446613 | solution.py:106
  27.5 2.0 fusion.111
  29.6 2.0 fusion.111
  31.6 2.0 fusion.111
  33.7 2.0 fusion.111
  35.7 2.0 fusion.111
  37.8 2.0 fusion.111
  39.8 2.0 fusion.111
  41.9 2.0 fusion.111
  46.3 1.5 collective-permute-start
  49.8 1.3 collective-permute-done.1
  51.5 3.4 %collective-permute-start.2 = (f32[1,4,8,1536]{3,2,1,0:T(8,128)S(1)}, f32[1,4,8,1536]{3,2,1,0:T(8,128)S(1)}, u32[]{:S(2)}, u32[]{:S(2)}) collective-permute-start(f32[1,4,8,1536]{3,2,1,0:T(8,128)S(1)} %convolution_bitcast_fusion.5), channel_id=1, source_target_pairs={{0,1},{2,3},{4,5},{6,7},{8,9},{10,11},{12,13},{14,15},{16,17},{18,... | collective-permute-start | bytes 589832 | tf_op jit(solution)/shard_map/ppermute | solution.py:22
  56.3 1.8 collective-permute-done.2
  58.1 4.5 %collective-permute-done.3 = f32[1,4,8,1536]{3,2,1,0:T(8,128)S(1)} collective-permute-done((f32[1,4,8,1536]{3,2,1,0:T(8,128)S(1)}, f32[1,4,8,1536]{3,2,1,0:T(8,128)S(1)}, u32[]{:S(2)}, u32[]{:S(2)}) %collective-permute-start.3) | collective-permute-done | bytes 196640 | tf_op jit(solution)/shard_map/ppermute | solution.py:23
  62.7 1.8 multiply_reduce_fusion
  64.4 42.7 %all-reduce.3 = (f32[]{:T(128)}, f32[]{:T(128)}, f32[]{:T(128)}) all-reduce(f32[]{:T(128)} %get-tuple-element.183, f32[]{:T(128)} %get-tuple-element.182, f32[]{:T(128)} %multiply_reduce_fusion.1), channel_id=1, replica_groups=mesh['brick'=16,'relay'=2] {'brick','relay'}, use_global_device_ids=true, to_apply=%region_6.7 | all-reduce | flops 3 | bytes 24 | tf_op jit(solution)/shard_map/psum | solution.py:112
  109.3 4.4 %collective-permute-start.4 = (f32[1,4,8,1536]{3,1,2,0:T(4,128)S(1)}, f32[1,4,8,1536]{3,1,2,0:T(4,128)S(1)}, u32[]{:S(2)}, u32[]{:S(2)}) collective-permute-start(f32[1,4,8,1536]{3,1,2,0:T(4,128)S(1)} %multiply_bitcast_fusion), channel_id=1, source_target_pairs={{0,1},{2,3},{4,5},{6,7},{8,9},{10,11},{12,13},{14,15},{16,17},{18,... | collective-permute-start | bytes 589832 | tf_op jit(solution)/shard_map/ppermute | solution.py:22
  113.7 1.5 collective-permute-start.5
  115.3 1.6 collective-permute-done.4
  116.9 4.4 %collective-permute-done.5 = f32[1,4,8,1536]{3,1,2,0:T(4,128)S(1)} collective-permute-done((f32[1,4,8,1536]{3,1,2,0:T(4,128)S(1)}, f32[1,4,8,1536]{3,1,2,0:T(4,128)S(1)}, u32[]{:S(2)}, u32[]{:S(2)}) %collective-permute-start.5) | collective-permute-done | bytes 196640 | tf_op jit(solution)/shard_map/ppermute | solution.py:23
  130.6 2.8 %collective-permute-done.7 = f32[3,4,4,1536]{3,2,1,0:T(4,128)S(1)} collective-permute-done((f32[3,4,4,1536]{3,2,1,0:T(4,128)S(1)}, f32[3,4,4,1536]{3,2,1,0:T(4,128)S(1)}, u32[]{:S(2)}, u32[]{:S(2)}) %collective-permute-start.7) | collective-permute-done | bytes 294944 | tf_op jit(solution)/shard_map/ppermute | solution.py:23
  134.5 12.6 %copy.77 = f32[3,4,8,1536]{0,3,2,1:T(8,128)} copy(f32[3,4,8,1536]{3,2,1,0:T(8,128)S(1)} %pad_maximum_fusion.1) | data formatting | bytes 1179648 | tf_op jit(solution)/shard_map/reshape | solution.py:201
  147.2 63.0 %gather_fusion = f32[16384,3]{1,0:T(8,128)} fusion(f32[3,49152]{0,1:T(8,128)} %bitcast.346, s32[16384]{0:T(1024)S(1)} %broadcast_clamp_fusion), kind=kCustom, calls=%fused_computation | custom fusion | bytes 458752 | tf_op jit(solution)/shard_map/jit(_take)/gather | solution.py:202
  210.1 5.5 %copy.70 = f32[3,128,128]{2,0,1:T(4,128)S(1)} copy(f32[3,128,128]{0,2,1:T(8,128)} %bitcast.347) | data formatting | bytes 393216 | tf_op jit(solution)/shard_map/jit(_take)/gather | solution.py:202
  216.4 9.5 %all-to-all-start.2 = ((f32[3,128,128]{2,0,1:T(4,128)}), f32[3,128,128]{2,0,1:T(4,128)S(1)}, u32[]{:S(2)}, u32[]{:S(2)}) async-start(f32[3,128,128]{2,0,1:T(4,128)} %select_multiply_fusion), calls=%async_computation.2 | async-start | bytes 524288 | tf_op jit(solution)/shard_map/all_to_all | solution.py:204
  226.2 9.8 %all-to-all-done.2 = f32[3,128,128]{2,0,1:T(4,128)S(1)} async-done(((f32[3,128,128]{2,0,1:T(4,128)}), f32[3,128,128]{2,0,1:T(4,128)S(1)}, u32[]{:S(2)}, u32[]{:S(2)}) %all-to-all-start.2) | async-done | bytes 196640 | tf_op jit(solution)/shard_map/all_to_all | solution.py:204
  (112 shorter events, 22.3 us)
Async XLA Ops:
  3.1 14.0 %all-to-all-start.1 = ((bf16[16,8,128]{2,1,0:T(8,128)(2,1)}), bf16[16,8,128]{2,1,0:T(8,128)(2,1)S(1)}, u32[]{:S(2)}, u32[]{:S(2)}) async-start(bf16[16,8,128]{2,1,0:T(8,128)(2,1)} %bitcast.6), calls=%async_computation.1 | async-start | bytes 65536 | tf_op jit(solution)/shard_map/all_to_all | solution.py:181
  17.1 10.4 %all-to-all-start = ((s32[16,8,128]{2,1,0:T(8,128)}), s32[16,8,128]{2,1,0:T(8,128)S(1)}, u32[]{:S(2)}, u32[]{:S(2)}) async-start(s32[16,8,128]{2,1,0:T(8,128)} %bitcast.3), calls=%async_computation | async-start | bytes 131072 | tf_op jit(solution)/shard_map/all_to_all | solution.py:182
  27.4 18.2 %copy-start.4 = (f32[128,136,1,1]{0,1,3,2:T(8,128)S(1)}, f32[128,136,1,1]{0,1,3,2:T(8,128)}, u32[]{:S(2)}) copy-start(f32[128,136,1,1]{0,1,3,2:T(8,128)} %constant.136) | copy-start | bytes 208900
  27.4 21.6 %copy-start = (f32[4,8,1536]{2,1,0:T(8,128)S(1)}, f32[4,8,1536]{2,1,0:T(8,128)}, u32[]{:S(2)}) copy-start(f32[4,8,1536]{2,1,0:T(8,128)} %param.17) | copy-start | bytes 589828
  27.4 23.7 %copy-start.7 = (f32[8,16,1]{1,0,2:T(8,128)S(1)}, f32[8,16,1]{1,0,2:T(8,128)}, u32[]{:S(2)}) copy-start(f32[8,16,1]{1,0,2:T(8,128)} %constant.137) | copy-start | bytes 1540
  27.4 35.2 %copy-start.8 = (f32[4,12,1]{1,0,2:T(4,128)S(1)}, f32[4,12,1]{1,0,2:T(4,128)}, u32[]{:S(2)}) copy-start(f32[4,12,1]{1,0,2:T(4,128)} %constant.138) | copy-start | bytes 580
  43.9 79.3 %copy-start.3 = (f32[128,136,1,1]{0,1,3,2:T(8,128)S(1)}, f32[128,136,1,1]{0,1,3,2:T(8,128)}, u32[]{:S(2)}) copy-start(f32[128,136,1,1]{0,1,3,2:T(8,128)} %constant.141) | copy-start | bytes 208900
  43.9 80.1 %copy-start.10 = (f32[4,12,1]{1,0,2:T(4,128)S(1)}, f32[4,12,1]{1,0,2:T(4,128)}, u32[]{:S(2)}) copy-start(f32[4,12,1]{1,0,2:T(4,128)} %constant.139) | copy-start | bytes 580
  46.3 3.5 %collective-permute-start = (f32[1,4,4,1536]{3,2,1,0:T(4,128)S(1)}, f32[1,4,4,1536]{3,2,1,0:T(4,128)S(1)}, u32[]{:S(2)}, u32[]{:S(2)}) collective-permute-start(f32[1,4,4,1536]{3,2,1,0:T(4,128)S(1)} %get-tuple-element.204), channel_id=1, source_target_pairs={{0,2},{2,4},{4,6},{6,8},{8,10},{10,12},{12,14},{14,16},{16,18},{18... | collective-permute-start | bytes 294920 | tf_op jit(solution)/shard_map/ppermute | solution.py:22
  47.8 3.4 %collective-permute-start.1 = (f32[1,4,4,1536]{3,2,1,0:T(4,128)S(1)}, f32[1,4,4,1536]{3,2,1,0:T(4,128)S(1)}, u32[]{:S(2)}, u32[]{:S(2)}) collective-permute-start(f32[1,4,4,1536]{3,2,1,0:T(4,128)S(1)} %get-tuple-element.205), channel_id=1, source_target_pairs={{2,0},{4,2},{6,4},{8,6},{10,8},{12,10},{14,12},{16,14},{18,16},{20... | collective-permute-start | bytes 294920 | tf_op jit(solution)/shard_map/ppermute | solution.py:23
  51.5 6.6 %collective-permute-start.2 = (f32[1,4,8,1536]{3,2,1,0:T(8,128)S(1)}, f32[1,4,8,1536]{3,2,1,0:T(8,128)S(1)}, u32[]{:S(2)}, u32[]{:S(2)}) collective-permute-start(f32[1,4,8,1536]{3,2,1,0:T(8,128)S(1)} %convolution_bitcast_fusion.5), channel_id=1, source_target_pairs={{0,1},{2,3},{4,5},{6,7},{8,9},{10,11},{12,13},{14,15},{16,17},{18,... | collective-permute-start | bytes 589832 | tf_op jit(solution)/shard_map/ppermute | solution.py:22
  55.0 7.6 %collective-permute-start.3 = (f32[1,4,8,1536]{3,2,1,0:T(8,128)S(1)}, f32[1,4,8,1536]{3,2,1,0:T(8,128)S(1)}, u32[]{:S(2)}, u32[]{:S(2)}) collective-permute-start(f32[1,4,8,1536]{3,2,1,0:T(8,128)S(1)} %convolution_bitcast_fusion.5), channel_id=1, source_target_pairs={{1,0},{3,2},{5,4},{7,6},{9,8},{11,10},{13,12},{15,14},{17,16},{19,... | collective-permute-start | bytes 589832 | tf_op jit(solution)/shard_map/ppermute | solution.py:23
  62.7 63.6 %copy-start.2 = (f32[128,136,1,1,1]{0,1,4,3,2:T(8,128)S(1)}, f32[128,136,1,1,1]{0,1,4,3,2:T(8,128)}, u32[]{:S(2)}) copy-start(f32[128,136,1,1,1]{0,1,4,3,2:T(8,128)} %constant.140) | copy-start | bytes 208900
  109.3 7.6 %collective-permute-start.4 = (f32[1,4,8,1536]{3,1,2,0:T(4,128)S(1)}, f32[1,4,8,1536]{3,1,2,0:T(4,128)S(1)}, u32[]{:S(2)}, u32[]{:S(2)}) collective-permute-start(f32[1,4,8,1536]{3,1,2,0:T(4,128)S(1)} %multiply_bitcast_fusion), channel_id=1, source_target_pairs={{0,1},{2,3},{4,5},{6,7},{8,9},{10,11},{12,13},{14,15},{16,17},{18,... | collective-permute-start | bytes 589832 | tf_op jit(solution)/shard_map/ppermute | solution.py:22
  113.7 7.6 %collective-permute-start.5 = (f32[1,4,8,1536]{3,1,2,0:T(4,128)S(1)}, f32[1,4,8,1536]{3,1,2,0:T(4,128)S(1)}, u32[]{:S(2)}, u32[]{:S(2)}) collective-permute-start(f32[1,4,8,1536]{3,1,2,0:T(4,128)S(1)} %multiply_bitcast_fusion), channel_id=1, source_target_pairs={{1,0},{3,2},{5,4},{7,6},{9,8},{11,10},{13,12},{15,14},{17,16},{19,... | collective-permute-start | bytes 589832 | tf_op jit(solution)/shard_map/ppermute | solution.py:23
  124.8 8.6 %copy-start.6 = (f32[8,16,1]{1,0,2:T(8,128)S(1)}, f32[8,16,1]{1,0,2:T(8,128)}, u32[]{:S(2)}) copy-start(f32[8,16,1]{1,0,2:T(8,128)} %constant.142) | copy-start | bytes 1540
  125.0 8.8 %copy-start.5 = (f32[8,16,1,1]{1,0,3,2:T(8,128)S(1)}, f32[8,16,1,1]{1,0,3,2:T(8,128)}, u32[]{:S(2)}) copy-start(f32[8,16,1,1]{1,0,3,2:T(8,128)} %constant.143) | copy-start | bytes 1540
  127.9 2.7 %collective-permute-start.6 = (f32[3,4,4,1536]{3,2,1,0:T(4,128)S(1)}, f32[3,4,4,1536]{3,2,1,0:T(4,128)S(1)}, u32[]{:S(2)}, u32[]{:S(2)}) collective-permute-start(f32[3,4,4,1536]{3,2,1,0:T(4,128)S(1)} %get-tuple-element.200), channel_id=1, source_target_pairs={{0,2},{2,4},{4,6},{6,8},{8,10},{10,12},{12,14},{14,16},{16,18},{18... | collective-permute-start | bytes 884744 | tf_op jit(solution)/shard_map/ppermute | solution.py:22
  129.2 4.1 %collective-permute-start.7 = (f32[3,4,4,1536]{3,2,1,0:T(4,128)S(1)}, f32[3,4,4,1536]{3,2,1,0:T(4,128)S(1)}, u32[]{:S(2)}, u32[]{:S(2)}) collective-permute-start(f32[3,4,4,1536]{3,2,1,0:T(4,128)S(1)} %get-tuple-element.201), channel_id=1, source_target_pairs={{2,0},{4,2},{6,4},{8,6},{10,8},{12,10},{14,12},{16,14},{18,16},{20... | collective-permute-start | bytes 884744 | tf_op jit(solution)/shard_map/ppermute | solution.py:23
  147.2 78.8 %copy-start.9 = (f32[3,64]{1,0:T(4,128)S(1)}, f32[3,64]{1,0:T(4,128)}, u32[]{:S(2)}) copy-start(f32[3,64]{1,0:T(4,128)} %param.22) | copy-start | bytes 2308
  147.2 78.9 %copy-start.1 = (f32[3,64,128]{2,1,0:T(8,128)S(1)}, f32[3,64,128]{2,1,0:T(8,128)}, u32[]{:S(2)}) copy-start(f32[3,64,128]{2,1,0:T(8,128)} %param.21) | copy-start | bytes 294916
  216.4 19.6 %all-to-all-start.2 = ((f32[3,128,128]{2,0,1:T(4,128)}), f32[3,128,128]{2,0,1:T(4,128)S(1)}, u32[]{:S(2)}, u32[]{:S(2)}) async-start(f32[3,128,128]{2,0,1:T(4,128)} %select_multiply_fusion), calls=%async_computation.2 | async-start | bytes 524288 | tf_op jit(solution)/shard_map/all_to_all | solution.py:204
where the time goes:
time: 239 us; the launch traced here: 238 us
  local copies, waits for them, and re-layouts  88.8 us (37%)
  blocking collectives  42.7 us (18%)
  waiting for transfers between devices  37.3 us (16%)
  starting transfers between devices  36.4 us (15%)
  matrix products  23.2 us (10%)
  other arithmetic  6.78 us (3%)
  between operations  2.66 us (1%)
    gather x2, local copies, waits for them, and re-layouts, shards(): sampled = jnp.take(grad_fields, cell_ids, axis=1)  68.5 us
    psum x1, blocking collectives, correlate(): lax.psum((jnp.sum(model_map * target), jnp.sum(model_map * model_map), jn...  42.7 us
    dot_general x8, matrix products, add_block(): lax.dot_general(line_table, col_table, (((0,), (0,)), ((), ())), preferre...  15.8 us
    ppermute x4, waiting for transfers between devices, padded_2(): after = lax.ppermute(first, axis, down)  13 us
    reshape x1, local copies, waits for them, and re-layouts, shards(): grad_fields = jnp.concatenate([grad_x, grad_rest], axis=0).reshape(3, -1)  12.6 us
    ppermute x4, starting transfers between devices, padded_2(): before = lax.ppermute(last, axis, up)  10.7 us
    all_to_all x1, waiting for transfers between devices, shards(): lax.all_to_all(force, 'brick', split_axis=1, concat_axis=1, tiled=True)  9.81 us
    all_to_all x1, starting transfers between devices, shards(): lax.all_to_all(force, 'brick', split_axis=1, concat_axis=1, tiled=True)  9.54 us
  transfers between devices with their start and end apart: 11, of which 9 were waited for; matrix products, arithmetic and copies ran while one was open for 1% of the time, Pallas kernels for 0%

commit v1 on v0

v1 whole, which is shorter than its diff:
```python
import functools

import jax
import jax.numpy as jnp
import numpy as np
from jax import lax
from jax.experimental import pallas as pl
from jax.experimental.pallas import tpu as pltpu
from jax.sharding import PartitionSpec as P

KR = 4
SIGMA = 1.5
EPSILON = 1e-06
HIGHEST = lax.Precision.HIGHEST
LO = 256
WEIGHT_SCALE = 512.0
LEVER_SCALE = 32768.0
LEVER_BIAS = 1 << 20
VMEM_BYTES = 48 << 20
F32 = jnp.float32
BF16 = jnp.bfloat16
I32 = jnp.int32


def taps_of(derivative):
    offsets = np.arange(-KR, KR + 1) * 1.0
    gaussian = np.exp(-(offsets**2) / (2.0 * SIGMA**2))
    gaussian = gaussian / gaussian.sum()
    if derivative:
        return -offsets / SIGMA**2 * gaussian
    return gaussian


def axis_matrix(length, derivative):
    offsets = np.arange(length)[:, None] - np.arange(length)[None, :]
    return np.where(
        np.abs(offsets) <= KR, taps_of(derivative)[np.clip(offsets + KR, 0, 2 * KR)], 0.0
    )


def columns_at(matrix, rows, wanted):
    inside = (wanted >= 0) & (wanted < matrix.shape[1])
    picked = matrix[rows][:, np.clip(wanted, 0, matrix.shape[1] - 1)]
    return np.where(inside[None, :], picked, 0.0)


def unique_tables(tables):
    flat = np.stack([t.reshape(-1) for t in tables])
    kept, inverse = np.unique(np.round(flat, 14), axis=0, return_inverse=True)
    return kept.reshape((-1,) + tables[0].shape), inverse.reshape(-1).astype(np.int32)


def pieces_np(table):
    import ml_dtypes

    high = table.astype(np.float32).astype(ml_dtypes.bfloat16)
    low = (table - high.astype(np.float64)).astype(ml_dtypes.bfloat16)
    return np.concatenate([high, high, low], axis=-1)


def weight_table(z_kinds, x_kinds, z_len, z_count, z_blocks, x_len, x_count, x_parts):
    z_tables = []
    for r in range(z_count):
        wanted = np.concatenate([np.arange(z_len) + z_len * block for block in z_blocks(r)])
        rows = np.arange(z_len) + z_len * r
        z_tables.append(np.stack([columns_at(m, rows, wanted) for m in z_kinds]))
    x_tables = []
    for b in range(x_count):
        wanted = np.concatenate([x_len * b + part for part in x_parts])
        rows = np.arange(x_len) + x_len * b
        x_tables.append(np.stack([columns_at(m, rows, wanted) for m in x_kinds]))
    z_tables, z_inverse = unique_tables(z_tables)
    x_tables, x_inverse = unique_tables(x_tables)
    kinds = len(z_kinds)
    parts, start = [], 0
    for part in x_parts:
        piece = x_tables[:, :, :, start : start + len(part)]
        start += len(part)
        full = np.einsum("rkzi,bkxj->rbkzxij", z_tables, piece)
        parts.append(
            full.reshape(len(z_tables) * len(x_tables), kinds * z_len * x_len, -1)
        )
    table = pieces_np(np.concatenate(parts, axis=-1))
    return table, z_inverse, x_inverse, len(x_tables)


def eye_column(row, eye):
    return jnp.sum(jnp.where(eye, row, jnp.zeros_like(row)), axis=1, keepdims=True)


def pack_kernel(most, lines, row_count, brick_ref, cell_ref, weight_ref, arm_ref, angle_ref, out_ref):
    frags, beads = cell_ref.shape
    slots = out_ref.shape[0]
    sub = lax.broadcasted_iota(I32, (frags, frags), 0)
    lane = lax.broadcasted_iota(I32, (frags, frags), 1)
    eye = sub == lane
    col = brick_ref[...]
    row = jnp.sum(jnp.where(eye, col, 0), axis=0, keepdims=True)
    earlier = jnp.logical_and(col == row, sub < lane)
    rank = jnp.sum(jnp.where(earlier, 1, 0), axis=0, keepdims=True)
    slot = row * most + rank
    place = jnp.where(lax.broadcasted_iota(I32, (slots, frags), 0) == slot, 1.0, 0.0).astype(F32)

    angles = angle_ref[...]
    cos, sin = jnp.cos(angles), jnp.sin(angles)
    cos_a, cos_b, cos_c = cos[0:1], cos[1:2], cos[2:3]
    sin_a, sin_b, sin_c = sin[0:1], sin[1:2], sin[2:3]
    turn = [
        [cos_a * cos_b, cos_a * sin_b * sin_c - sin_a * cos_c, cos_a * sin_b * cos_c + sin_a * sin_c],
        [sin_a * cos_b, sin_a * sin_b * sin_c + cos_a * cos_c, sin_a * sin_b * cos_c - cos_a * sin_c],
        [-sin_b, cos_b * sin_c, cos_b * cos_c],
    ]
    levers = []
    for i in range(3):
        total = eye_column(turn[i][0], eye) * arm_ref[0]
        for j in (1, 2):
            total = total + eye_column(turn[i][j], eye) * arm_ref[j]
        levers.append(jnp.round(total * LEVER_SCALE))

    cell = cell_ref[...]
    line = ((cell.astype(F32) + 0.5) * (1.0 / row_count)).astype(I32)
    y = cell - line * row_count
    code = (((y // LO) * lines + line) * LO + (y % LO)).astype(F32)
    weight = weight_ref[...].astype(F32) * WEIGHT_SCALE
    payload = jnp.concatenate([code, weight] + levers, axis=1)
    placed = jnp.dot(place, payload, precision=HIGHEST, preferred_element_type=F32)
    placed = placed.astype(I32)
    code, weight, lx, ly, lz = [placed[:, k * beads : (k + 1) * beads] for k in range(5)]
    lz = lz + LEVER_BIAS
    out_ref[:, 0:beads] = code | (weight << 16)
    out_ref[:, beads : 2 * beads] = (lx << 11) | (lz >> 10)
    out_ref[:, 2 * beads : 3 * beads] = (ly << 11) | (lz & 1023)


def splat_kernel(lines, rb, got_ref, out_ref, acc_ref):
    slots = got_ref.shape[0]
    beads = got_ref.shape[1] // 3
    his = acc_ref.shape[0]
    acc_ref[...] = jnp.zeros_like(acc_ref)
    hi_iota = lax.broadcasted_iota(I32, (his, beads), 0)
    lo_iota = lax.broadcasted_iota(I32, (LO, beads), 0)

    def body(i, carry):
        word = got_ref[pl.ds(i * rb, rb), 0:beads]
        lo = word & (LO - 1)
        hi = (word >> 8) & 255
        weight = (word >> 16).astype(F32) * (1.0 / WEIGHT_SCALE)
        left, right = [], []
        for q in range(rb):
            left.append(jnp.where(hi_iota == hi[q : q + 1], weight[q : q + 1], 0.0).astype(BF16))
            right.append(jnp.where(lo_iota == lo[q : q + 1], 1.0, 0.0).astype(BF16))
        acc_ref[...] += lax.dot_general(
            jnp.concatenate(left, axis=1),
            jnp.concatenate(right, axis=1),
            (((1,), (1,)), ((), ())),
            preferred_element_type=F32,
        )
        return carry

    lax.fori_loop(0, slots // rb, body, 0)
    for yh in range(his // lines):
        out_ref[:, yh * LO : (yh + 1) * LO] = acc_ref[yh * lines : (yh + 1) * lines, :]


def line_blur(value, derivative):
    taps = taps_of(derivative)
    rows, length = value.shape
    wide = jnp.concatenate([value, jnp.zeros((rows, 128), F32)], axis=1)
    total = None if derivative else float(taps[KR]) * value
    for d in range(1, KR + 1):
        up = pltpu.roll(wide, d, 1)[:, :length]
        down = pltpu.roll(wide, length + 128 - d, 1)[:, :length]
        pair = up - down if derivative else up + down
        term = float(taps[KR + d]) * pair
        total = term if total is None else total + term
    return total


def split(value):
    high = value.astype(BF16)
    low = (value - high.astype(F32)).astype(BF16)
    return high, low


def mix_lines(table_ref, parts):
    value = jnp.concatenate(parts, axis=0)
    high, low = split(value)
    return jnp.dot(
        table_ref[0], jnp.concatenate([high, low, high], axis=0), preferred_element_type=F32
    )


def store_fields(fields, lines, out_ref):
    his = fields[0].shape[1] // LO * lines
    for k, field in enumerate(fields):
        for yh in range(field.shape[1] // LO):
            high, low = split(field[:, yh * LO : (yh + 1) * LO])
            rows = slice(k * his + yh * lines, k * his + (yh + 1) * lines)
            out_ref[rows, 0:LO] = high
            out_ref[rows, LO : 2 * LO] = low


def target_kernel(lines, count, _, table_ref, *refs):
    parts, out_ref = refs[:count], refs[count]
    mixed = mix_lines(table_ref, [ref[...] for ref in parts])
    grad_x = line_blur(mixed[0:lines], False)
    grad_y = line_blur(mixed[lines : 2 * lines], True)
    grad_z = line_blur(mixed[2 * lines : 3 * lines], False)
    store_fields([grad_x, grad_y, grad_z], lines, out_ref)


def model_kernel(lines, count, _, table_ref, target_ref, *refs):
    parts, out_ref, sum_ref = refs[:count], refs[count], refs[count + 1]
    mixed = mix_lines(table_ref, [ref[...] for ref in parts])
    smooth = line_blur(mixed, False)
    model = smooth[3 * lines :]
    target = target_ref[...]
    sums = [jnp.sum(model * target), jnp.sum(model * model), jnp.sum(target * target)]
    lane = lax.broadcasted_iota(I32, sum_ref.shape, 1)
    total = jnp.zeros(sum_ref.shape, F32)
    for k, value in enumerate(sums):
        total = jnp.where(lane == k, value, total)
    sum_ref[...] = total
    grad_x = line_blur(smooth[0:lines], False)
    grad_y = line_blur(smooth[lines : 2 * lines], True)
    grad_z = line_blur(smooth[2 * lines : 3 * lines], False)
    store_fields([grad_x, grad_y, grad_z], lines, out_ref)


def sample_kernel(his, rb, got_ref, field_ref, out_ref, force_ref):
    slots = got_ref.shape[0]
    beads = got_ref.shape[1] // 3
    lo_iota = lax.broadcasted_iota(I32, (LO, beads), 0)
    sub_iota = lax.broadcasted_iota(I32, (8, beads), 0)

    def body(i, carry):
        word = got_ref[pl.ds(i * rb, rb), 0:beads]
        lo = word & (LO - 1)
        hi = (word >> 8) & 255
        picks = [
            jnp.where(lo_iota == lo[q : q + 1], 1.0, 0.0).astype(BF16) for q in range(rb)
        ]
        pick = jnp.concatenate(picks, axis=1)
        sampled = jnp.dot(
            field_ref[...], jnp.concatenate([pick, pick], axis=0), preferred_element_type=F32
        )
        for q in range(rb):
            own = jnp.broadcast_to(hi[q : q + 1], (8, beads))
            group, within = own >> 3, (own & 7) == sub_iota
            found = [jnp.zeros((8, beads), F32)] * 3
            for j in range(his // 8):
                here = group == j
                for k in range(3):
                    rows = slice(k * his + 8 * j, k * his + 8 * j + 8)
                    found[k] = jnp.where(
                        here, sampled[rows, q * beads : (q + 1) * beads], found[k]
                    )
            for k in range(3):
                value = jnp.sum(jnp.where(within, found[k], 0.0), axis=0, keepdims=True)
                force_ref[k, pl.ds(i * rb + q, 1), :] = value
        return carry

    lax.fori_loop(0, slots // rb, body, 0)
    first, second = got_ref[:, beads : 2 * beads], got_ref[:, 2 * beads : 3 * beads]
    weight = (got_ref[:, 0:beads] >> 16).astype(F32) * (1.0 / WEIGHT_SCALE)
    lever_z = (((first & 2047) << 10) | (second & 1023)) - LEVER_BIAS
    levers = [
        v.astype(F32) * (1.0 / LEVER_SCALE) for v in (first >> 11, second >> 11, lever_z)
    ]
    force = [force_ref[k] * weight for k in range(3)]
    terms = force + [
        levers[1] * force[2] - levers[2] * force[1],
        levers[2] * force[0] - levers[0] * force[2],
        levers[0] * force[1] - levers[1] * force[0],
    ]
    lane = lax.broadcasted_iota(I32, out_ref.shape, 1)
    total = jnp.zeros(out_ref.shape, F32)
    for k, term in enumerate(terms):
        total = jnp.where(lane == k, jnp.sum(term, axis=1, keepdims=True), total)
    out_ref[...] = total


def return_kernel(target_ref, model_ref, sum_ref, out_ref):
    lane = lax.broadcasted_iota(I32, out_ref.shape, 1)
    sums = sum_ref[0:1, :]
    for k in range(1, sum_ref.shape[0] // 8):
        sums = sums + sum_ref[8 * k : 8 * k + 1, :]
    total = jnp.where(lane < 6, target_ref[...], 0.0)
    total = jnp.where((lane >= 8) & (lane < 14), pltpu.roll(model_ref[...], 8, 1), total)
    out_ref[...] = jnp.where(lane >= 16, pltpu.roll(sums, 16, 1), total)


def finish_kernel(most, voxel_total, brick_ref, back_ref, out_ref):
    frags = out_ref.shape[1]
    slots = back_ref.shape[0]
    sub = lax.broadcasted_iota(I32, (frags, frags), 0)
    lane = lax.broadcasted_iota(I32, (frags, frags), 1)
    col = brick_ref[...]
    row = jnp.sum(jnp.where(sub == lane, col, 0), axis=0, keepdims=True)
    earlier = jnp.logical_and(col == row, sub < lane)
    rank = jnp.sum(jnp.where(earlier, 1, 0), axis=0, keepdims=True)
    slot = row * most + rank
    place = jnp.where(lax.broadcasted_iota(I32, (slots, frags), 0) == slot, 1.0, 0.0).astype(F32)
    back = back_ref[...]
    first = lax.broadcasted_iota(I32, (slots, 128), 0) % most == 0
    sums = jnp.sum(jnp.where(first, back, 0.0), axis=0, keepdims=True)
    cross, model_sq, target_sq = sums[:, 16:17], sums[:, 17:18], sums[:, 18:19]
    norm_model = jnp.sqrt(model_sq + EPSILON)
    norm_target = jnp.sqrt(target_sq + EPSILON)
    corr = cross / (norm_model * norm_target)
    scale_target = voxel_total / (norm_model * norm_target)
    scale_model = voxel_total * corr / (norm_model * norm_model)
    mine = lax.dot_general(
        back, place, (((0,), (0,)), ((), ())), precision=HIGHEST, preferred_element_type=F32
    )
    out_ref[...] = scale_target * mine[0:6] - scale_model * mine[8:14]


def call(kernel, out_shape, *args, scratch=(), name=None):
    return pl.pallas_call(
        kernel,
        out_shape=out_shape,
        scratch_shapes=list(scratch),
        compiler_params=pltpu.CompilerParams(vmem_limit_bytes=VMEM_BYTES),
        name=name,
    )(*args)


def call_at(kernel, out_shape, index, table, *args, name=None):
    def whole(shape):
        return pl.BlockSpec(shape, lambda i, s: (0,) * len(shape))

    single = not isinstance(out_shape, list)
    outs = [out_shape] if single else out_shape
    specs = [whole(o.shape) for o in outs]
    return pl.pallas_call(
        kernel,
        out_shape=out_shape,
        grid_spec=pltpu.PrefetchScalarGridSpec(
            num_scalar_prefetch=1,
            grid=(1,),
            in_specs=[pl.BlockSpec((1,) + table.shape[1:], lambda i, s: (s[0], 0, 0))]
            + [whole(a.shape) for a in args],
            out_specs=specs[0] if single else specs,
        ),
        compiler_params=pltpu.CompilerParams(vmem_limit_bytes=VMEM_BYTES),
        name=name,
    )(index, table, *args)


def shifted(value, axis, step):
    size = lax.axis_size(axis)
    pairs = [(i, i + step) for i in range(size) if 0 <= i + step < size]
    return lax.ppermute(value, axis, pairs)


def relay_blocks(value, reach):
    size = lax.axis_size("relay")
    if size == 2:
        return [value, lax.ppermute(value, "relay", [(0, 1), (1, 0)])]
    blocks = [value]
    for step in range(1, min(reach, size - 1) + 1):
        blocks += [shifted(value, "relay", step), shifted(value, "relay", -step)]
    return blocks


def relay_order(size, reach):
    if size == 2:
        return lambda r: [r, 1 - r]
    steps = [0]
    for step in range(1, min(reach, size - 1) + 1):
        steps += [-step, step]
    return lambda r: [r + s for s in steps]


def relay_total(value):
    size = lax.axis_size("relay")
    values, moving = [value], value
    for _ in range(size - 1):
        moving = lax.ppermute(moving, "relay", [(i, (i + 1) % size) for i in range(size)])
        values.append(moving)
    return jnp.concatenate(values, axis=0)


def shards(target, frag_brick, bead_cell, bead_weight, bead_arm, frag_angle):
    brick_count, relay_count = lax.axis_size("brick"), lax.axis_size("relay")
    frags, beads = bead_cell.shape
    planes, columns, rows = target.shape
    lines = planes * columns
    his = lines * (rows // LO)
    assert rows % LO == 0 and his <= 256 and columns >= 2 * KR
    voxel_total = float(brick_count * columns * relay_count * planes * rows)
    most = max(2, 2 * frags // brick_count)
    slots = brick_count * most

    z_total, x_total = relay_count * planes, brick_count * columns
    gz, dz = axis_matrix(z_total, False), axis_matrix(z_total, True)
    gx, dx = axis_matrix(x_total, False), axis_matrix(x_total, True)
    reach_one, reach_two = -(-KR // planes), -(-2 * KR // planes)
    target_table, tz, tx, tn = weight_table(
        [gz, gz, dz], [dx, gx, gx], planes, relay_count, relay_order(relay_count, reach_one),
        columns, brick_count,
        [np.arange(columns), np.arange(-KR, 0), np.arange(columns, columns + KR)],
    )
    model_table, mz, mx, mn = weight_table(
        [gz @ gz, gz @ gz, dz @ gz, gz], [dx @ gx, gx @ gx, gx @ gx, gx],
        planes, relay_count, relay_order(relay_count, reach_two), columns, brick_count,
        [np.arange(columns), np.arange(-columns, 0), np.arange(columns, 2 * columns)],
    )
    r, b = lax.axis_index("relay"), lax.axis_index("brick")
    target_index = (jnp.asarray(tz)[r] * tn + jnp.asarray(tx)[b]).reshape(1)
    model_index = (jnp.asarray(mz)[r] * mn + jnp.asarray(mx)[b]).reshape(1)

    target_lines = target.reshape(lines, rows)
    target_blocks = relay_blocks(target, reach_one)
    left_edge = jnp.concatenate([t[:, columns - KR :] for t in target_blocks], axis=0)
    right_edge = jnp.concatenate([t[:, :KR] for t in target_blocks], axis=0)
    from_left = shifted(left_edge.reshape(-1, rows), "brick", 1)
    from_right = shifted(right_edge.reshape(-1, rows), "brick", -1)
    target_parts = [t.reshape(lines, rows) for t in target_blocks] + [from_left, from_right]

    sent = call(
        functools.partial(pack_kernel, most, lines, rows),
        jax.ShapeDtypeStruct((slots, 3 * beads), I32),
        frag_brick, bead_cell, bead_weight, bead_arm, frag_angle,
        name="pack",
    )
    got = lax.all_to_all(sent, "brick", split_axis=0, concat_axis=0, tiled=True)
    density = call(
        functools.partial(splat_kernel, lines, 8),
        jax.ShapeDtypeStruct((lines, rows), F32),
        got,
        scratch=[pltpu.VMEM((his, LO), F32)],
        name="splat",
    )
    blocks = jnp.concatenate(relay_blocks(density, reach_two), axis=0)
    model_parts = [blocks, shifted(blocks, "brick", 1), shifted(blocks, "brick", -1)]

    field_shape = jax.ShapeDtypeStruct((3 * his, 2 * LO), BF16)

    def sample(field, name):
        return call(
            functools.partial(sample_kernel, his, 8),
            jax.ShapeDtypeStruct((slots, 128), F32),
            got, field,
            scratch=[pltpu.VMEM((3, slots, beads), F32)],
            name=name,
        )

    target_field = call_at(
        functools.partial(target_kernel, lines, len(target_parts)),
        field_shape, target_index, jnp.asarray(target_table), *target_parts,
        name="target_fields",
    )
    target_sums = sample(target_field, "target_sample")
    model_field, partial = call_at(
        functools.partial(model_kernel, lines, len(model_parts)),
        [field_shape, jax.ShapeDtypeStruct((8, 128), F32)],
        model_index, jnp.asarray(model_table), target_lines, *model_parts,
        name="model_fields",
    )
    partials = relay_total(partial)
    model_sums = sample(model_field, "model_sample")
    leaving = call(
        return_kernel, jax.ShapeDtypeStruct((slots, 128), F32), target_sums, model_sums, partials,
        name="join",
    )
    back = lax.all_to_all(leaving, "brick", split_axis=0, concat_axis=0, tiled=True)
    return call(
        functools.partial(finish_kernel, most, voxel_total),
        jax.ShapeDtypeStruct((6, frags), F32),
        frag_brick, back,
        name="finish",
    )


def solution(mesh):
    placed = (
        P("relay", "brick", None),
        P(("brick", "relay"), None),
        P(("brick", "relay"), None),
        P(("brick", "relay"), None),
        P(None, ("brick", "relay"), None),
        P(None, ("brick", "relay")),
    )
    return jax.shard_map(
        shards, mesh=mesh, in_specs=placed, out_specs=P(None, ("brick", "relay")), check_vma=False
    )
```

time: 239 us -> 92.8 us (0.39)
  local copies, waits for them, and re-layouts: 88.8 us -> 5.27 us
  Pallas kernels: 0 us -> 39.8 us
  waiting for transfers between devices: 37.3 us -> 10.2 us
  blocking collectives: 42.7 us -> 18.5 us
  matrix products: 23.2 us -> 0 us
  starting transfers between devices: 36.4 us -> 17.5 us
  other arithmetic: 6.78 us -> 0.12 us
    gather x3 -> x0, local copies, waits for them, and re-layouts: 69.1 us -> none  [the longest x2 68.5 us: shards(): sampled = jnp.take(grad_fields, cell_ids, axis=1)]
    psum x1 -> x0, blocking collectives: 42.7 us -> none  [correlate(): lax.psum((jnp.sum(model_map * target), jnp.sum(model_map * model_map), jn...]
    pallas_call x0 -> x8, Pallas kernels: none -> 39.8 us  [the longest x6 34.7 us: call(): pl.pallas_call(kernel, out_shape=out_shape, scratch_shapes=list(scratch),...]
    dot_general x17 -> x0, matrix products: 23.2 us -> none  [the longest x8 15.8 us: add_block(): lax.dot_general(line_table, col_table, (((0,), (0,)), ((), ())), preferre...]
    all_to_all x3 -> x1, waiting for transfers between devices: 20.9 us -> 1.65 us  [shards(): got = lax.all_to_all(sent, 'brick', split_axis=0, concat_axis=0, tiled=True)]
    all_to_all x0 -> x1, blocking collectives: none -> 18.5 us  [shards(): lax.all_to_all(leaving, 'brick', split_axis=0, concat_axis=0, tiled=True)]
    all_to_all x3 -> x1, starting transfers between devices: 20.4 us -> 7.49 us  [shards(): got = lax.all_to_all(sent, 'brick', split_axis=0, concat_axis=0, tiled=True)]
    reshape x4 -> x2, local copies, waits for them, and re-layouts: 12.9 us -> 0.81 us  [the longest x1 0.74 us: shards(): from_left = shifted(left_edge.reshape(-1, rows), 'brick', 1)]
  transfers between devices with their start and end apart: 11 -> 8, of which waited for: 9 -> 3; matrix products, arithmetic and copies ran while one was open for 1% -> 2% of each run, Pallas kernels for 0% -> 35%
where the time goes in v1:
time: 92.8 us; the launch traced here: 92.3 us
  Pallas kernels  39.8 us (43%)
  blocking collectives  18.5 us (20%)
  starting transfers between devices  17.5 us (19%)
  waiting for transfers between devices  10.2 us (11%)
  local copies, waits for them, and re-layouts  5.27 us (6%)
    pallas_call x6, Pallas kernels, call(): pl.pallas_call(kernel, out_shape=out_shape, scratch_shapes=list(scratch),...  34.7 us
    all_to_all x1, blocking collectives, shards(): lax.all_to_all(leaving, 'brick', split_axis=0, concat_axis=0, tiled=True)  18.5 us
    ppermute x2, waiting for transfers between devices, relay_blocks(): return [value, lax.ppermute(value, 'relay', [(0, 1), (1, 0)])]  8.54 us
    all_to_all x1, starting transfers between devices, shards(): got = lax.all_to_all(sent, 'brick', split_axis=0, concat_axis=0, tiled=True)  7.49 us
    ppermute x4, starting transfers between devices, shifted(): return lax.ppermute(value, axis, pairs)  5.26 us
    pallas_call x2, Pallas kernels, call_at(): pl.pallas_call(kernel, out_shape=out_shape, grid_spec=pltpu.PrefetchScala...  5.12 us
    unnamed x17, local copies, waits for them, and re-layouts  3.73 us
    ppermute x2, starting transfers between devices, relay_blocks(): return [value, lax.ppermute(value, 'relay', [(0, 1), (1, 0)])]  3.17 us
  transfers between devices with their start and end apart: 8, of which 3 were waited for; matrix products, arithmetic and copies ran while one was open for 2% of the time, Pallas kernels for 35%

profile of v1, /device:TPU:0, one launch (start us, length us, event | category | flops | bytes accessed | tf_op | source)
XLA Modules:
  0.0 92.3 jit_solution(17782735822923179077)
XLA Ops:
  0.0 0.8 copy.16.brick_ref
  0.8 0.0 copy-done.4
  0.8 0.9 copy-done.3
  1.7 0.7 copy-done.5
  2.4 0.7 copy-done.6
  3.1 1.2 %pack.1 = s32[128,384]{1,0:T(8,128)} custom-call(s32[64,1]{1,0:T(8,128)S(1)} %copy.16.brick_ref, s32[64,128]{1,0:T(8,128)S(1)} %copy-done.4, bf16[64,128]{1,0:T(8,128)(2,1)S(1)} %copy-done.5, f32[3,64,128]{2,1,0:T(8,128)S(1)} %copy-done.3, f32[3,64]{1,0:T(4,128)S(1)} %copy-done.6), custom_call_target="tpu_custom_call" | custom-call | tf_op jit(solution)/shard_map/pack/pallas_call | solution.py:320
  4.3 7.5 %all-to-all-start = ((s32[16,8,384]{2,1,0:T(8,128)}), s32[16,8,384]{2,1,0:T(8,128)S(1)}, u32[]{:S(2)}, u32[]{:S(2)}) async-start(s32[16,8,384]{2,1,0:T(8,128)} %bitcast), calls=%async_computation | async-start | bytes 393216 | tf_op jit(solution)/shard_map/all_to_all | solution.py:428
  11.8 1.6 %collective-permute-start = (f32[4,8,1536]{2,1,0:T(8,128)S(1)}, f32[4,8,1536]{2,1,0:T(8,128)S(1)}, u32[]{:S(2)}, u32[]{:S(2)}) collective-permute-start(f32[4,8,1536]{2,1,0:T(8,128)S(1)} %copy-done), channel_id=1, source_target_pairs={{0,1},{1,0},{2,3},{3,2},{4,5},{5,4},{6,7},{7,6},{8,9},{9,8},{10,11... | collective-permute-start | bytes 589832 | tf_op jit(solution)/shard_map/ppermute | solution.py:360
  13.4 5.7 %collective-permute-done = f32[4,8,1536]{2,1,0:T(8,128)S(1)} collective-permute-done((f32[4,8,1536]{2,1,0:T(8,128)S(1)}, f32[4,8,1536]{2,1,0:T(8,128)S(1)}, u32[]{:S(2)}, u32[]{:S(2)}) %collective-permute-start) | collective-permute-done | bytes 196640 | tf_op jit(solution)/shard_map/ppermute | solution.py:360
  19.1 1.6 %all-to-all-done = s32[16,8,384]{2,1,0:T(8,128)S(1)} async-done(((s32[16,8,384]{2,1,0:T(8,128)}), s32[16,8,384]{2,1,0:T(8,128)S(1)}, u32[]{:S(2)}, u32[]{:S(2)}) %all-to-all-start) | async-done | bytes 196640 | tf_op jit(solution)/shard_map/all_to_all | solution.py:428
  20.8 5.5 %splat.1 = f32[32,1536]{1,0:T(8,128)S(1)} custom-call(s32[128,384]{1,0:T(8,128)S(1)} %bitcast.7), custom_call_target="tpu_custom_call" | custom-call | tf_op jit(solution)/shard_map/splat/pallas_call | solution.py:320
  26.3 1.6 %collective-permute-start.3 = (f32[32,1536]{1,0:T(8,128)S(1)}, f32[32,1536]{1,0:T(8,128)S(1)}, u32[]{:S(2)}, u32[]{:S(2)}) collective-permute-start(f32[32,1536]{1,0:T(8,128)S(1)} %splat.1), channel_id=1, source_target_pairs={{0,1},{1,0},{2,3},{3,2},{4,5},{5,4},{6,7},{7,6},{8,9},{9,8},{10,11... | collective-permute-start | bytes 589832 | tf_op jit(solution)/shard_map/ppermute | solution.py:360
  27.9 0.0 copy-start.1
  27.9 0.7 reshape.29
  28.7 1.4 %collective-permute-start.1 = (f32[32,1536]{1,0:T(8,128)}, f32[32,1536]{1,0:T(8,128)S(1)}, u32[]{:S(2)}, u32[]{:S(2)}) collective-permute-start(f32[32,1536]{1,0:T(8,128)} %reshape.29), channel_id=1, source_target_pairs={{0,2},{2,4},{4,6},{6,8},{8,10},{10,12},{12,14},{14,16},{16,18},{18... | collective-permute-start | bytes 589832 | tf_op jit(solution)/shard_map/ppermute | solution.py:354
  30.0 2.9 %collective-permute-done.3 = f32[32,1536]{1,0:T(8,128)S(1)} collective-permute-done((f32[32,1536]{1,0:T(8,128)S(1)}, f32[32,1536]{1,0:T(8,128)S(1)}, u32[]{:S(2)}, u32[]{:S(2)}) %collective-permute-start.3) | collective-permute-done | bytes 196640 | tf_op jit(solution)/shard_map/ppermute | solution.py:360
  32.9 1.3 %collective-permute-start.4 = (f32[64,1536]{1,0:T(8,128)S(1)}, f32[64,1536]{1,0:T(8,128)S(1)}, u32[]{:S(2)}, u32[]{:S(2)}) collective-permute-start(f32[64,1536]{1,0:T(8,128)S(1)} %pad_maximum_fusion.refs_0_), channel_id=1, source_target_pairs={{0,2},{2,4},{4,6},{6,8},{8,10},{10,12},{12,14},{14,16},{16,18},{18... | collective-permute-start | bytes 1179656 | tf_op jit(solution)/shard_map/ppermute | solution.py:354
  34.2 1.3 %collective-permute-start.5 = (f32[64,1536]{1,0:T(8,128)S(1)}, f32[64,1536]{1,0:T(8,128)S(1)}, u32[]{:S(2)}, u32[]{:S(2)}) collective-permute-start(f32[64,1536]{1,0:T(8,128)S(1)} %pad_maximum_fusion.refs_0_), channel_id=1, source_target_pairs={{2,0},{4,2},{6,4},{8,6},{10,8},{12,10},{14,12},{16,14},{18,16},{20... | collective-permute-start | bytes 1179656 | tf_op jit(solution)/shard_map/ppermute | solution.py:354
  35.6 0.1 reshape.30
  35.7 1.3 %collective-permute-start.2 = (f32[32,1536]{1,0:T(8,128)S(1)}, f32[32,1536]{1,0:T(8,128)S(1)}, u32[]{:S(2)}, u32[]{:S(2)}) collective-permute-start(f32[32,1536]{1,0:T(8,128)S(1)} %reshape.30), channel_id=1, source_target_pairs={{2,0},{4,2},{6,4},{8,6},{10,8},{12,10},{14,12},{16,14},{18,16},{20... | collective-permute-start | bytes 589832 | tf_op jit(solution)/shard_map/ppermute | solution.py:354
  37.0 0.0 copy-start.7
  37.0 0.6 copy-done.7
  37.6 0.7 dynamic_slice.13
  39.0 0.0 copy-start.2
  39.0 3.5 %model_fields.1 = (bf16[576,512]{1,0:T(8,128)(2,1)S(1)}, f32[8,128]{1,0:T(8,128)S(1)}) custom-call(s32[1]{0:T(128)S(6)} %add.18._, bf16[6,128,576]{2,1,0:T(8,128)(2,1)S(1)} %copy-done.1, f32[32,1536]{1,0:T(8,128)S(1)} %bitcast.10, f32[64,1536]{1,0:T(8,128)S(1)} %pad_maximum_fusion.refs_0_, f32[64,1536]{1,0:T(8,128)S(1)} %collective-permute-done.4.refs_1_, ...), custom_call_target="tpu_custom_call" | custom-call | tf_op jit(solution)/shard_map/model_fields/pallas_call | solution.py:336
  42.6 1.6 %collective-permute-start.6 = (f32[8,128]{1,0:T(8,128)S(1)}, f32[8,128]{1,0:T(8,128)S(1)}, u32[]{:S(2)}, u32[]{:S(2)}) collective-permute-start(f32[8,128]{1,0:T(8,128)S(1)} %get-tuple-element.8), channel_id=1, source_target_pairs={{0,1},{1,0},{2,3},{3,2},{4,5},{5,4},{6,7},{7,6},{8,9},{9,8},{10,11... | collective-permute-start | bytes 12296 | tf_op jit(solution)/shard_map/ppermute | solution.py:380
  44.2 1.6 %target_fields.1.field_ref = bf16[576,512]{1,0:T(8,128)(2,1)S(1)} custom-call(s32[1]{0:T(128)S(6)} %add.18._, bf16[6,96,384]{2,1,0:T(8,128)(2,1)S(1)} %copy-done.2, f32[32,1536]{1,0:T(8,128)S(1)} %bitcast.11, f32[32,1536]{1,0:T(8,128)S(1)} %bitcast.12, f32[32,1536]{1,0:T(8,128)S(1)} %collective-permute-done.1.refs_2_, ...), custom_call_target="tpu_custom_call" | custom-call | tf_op jit(solution)/shard_map/target_fields/pallas_call | solution.py:336
  45.8 13.5 %target_sample.1.target_ref = f32[128,128]{1,0:T(8,128)S(1)} custom-call(s32[128,384]{1,0:T(8,128)S(1)} %bitcast.8, bf16[576,512]{1,0:T(8,128)(2,1)S(1)} %target_fields.1.field_ref), custom_call_target="tpu_custom_call" | custom-call | tf_op jit(solution)/shard_map/target_sample/pallas_call | solution.py:320
  59.3 13.5 %model_sample.1.model_ref = f32[128,128]{1,0:T(8,128)S(1)} custom-call(s32[128,384]{1,0:T(8,128)S(1)} %bitcast.9, bf16[576,512]{1,0:T(8,128)(2,1)S(1)} %get-tuple-element.7.field_ref), custom_call_target="tpu_custom_call" | custom-call | tf_op jit(solution)/shard_map/model_sample/pallas_call | solution.py:320
  72.8 0.1 join.1
  72.9 18.5 %all_to_all.22 = f32[16,8,128]{2,1,0:T(8,128)S(1)} all-to-all(f32[16,8,128]{2,1,0:T(8,128)S(1)} %bitcast.13), channel_id=1, replica_groups=mesh['brick'=16,'relay'=2] {'brick'}, dimensions={0} | all-to-all | bytes 131072 | tf_op jit(solution)/shard_map/all_to_all | solution.py:468
  91.4 0.9 finish.1
  (19 shorter events, 0.2 us)
Async XLA Ops:
  0.0 0.8 copy-start.4
  0.8 0.9 copy-start.3
  1.7 0.7 copy-start.5
  2.4 0.7 copy-start.6
  4.3 7.5 %copy-start = (f32[4,8,1536]{2,1,0:T(8,128)S(1)}, f32[4,8,1536]{2,1,0:T(8,128)}, u32[]{:S(2)}) copy-start(f32[4,8,1536]{2,1,0:T(8,128)} %param.12) | copy-start | bytes 589828
  4.3 16.5 %all-to-all-start = ((s32[16,8,384]{2,1,0:T(8,128)}), s32[16,8,384]{2,1,0:T(8,128)S(1)}, u32[]{:S(2)}, u32[]{:S(2)}) async-start(s32[16,8,384]{2,1,0:T(8,128)} %bitcast), calls=%async_computation | async-start | bytes 393216 | tf_op jit(solution)/shard_map/all_to_all | solution.py:428
  11.8 7.3 %collective-permute-start = (f32[4,8,1536]{2,1,0:T(8,128)S(1)}, f32[4,8,1536]{2,1,0:T(8,128)S(1)}, u32[]{:S(2)}, u32[]{:S(2)}) collective-permute-start(f32[4,8,1536]{2,1,0:T(8,128)S(1)} %copy-done), channel_id=1, source_target_pairs={{0,1},{1,0},{2,3},{3,2},{4,5},{5,4},{6,7},{7,6},{8,9},{9,8},{10,11... | collective-permute-start | bytes 589832 | tf_op jit(solution)/shard_map/ppermute | solution.py:360
  26.3 6.6 %collective-permute-start.3 = (f32[32,1536]{1,0:T(8,128)S(1)}, f32[32,1536]{1,0:T(8,128)S(1)}, u32[]{:S(2)}, u32[]{:S(2)}) collective-permute-start(f32[32,1536]{1,0:T(8,128)S(1)} %splat.1), channel_id=1, source_target_pairs={{0,1},{1,0},{2,3},{3,2},{4,5},{5,4},{6,7},{7,6},{8,9},{9,8},{10,11... | collective-permute-start | bytes 589832 | tf_op jit(solution)/shard_map/ppermute | solution.py:360
  27.9 11.1 %copy-start.1 = (bf16[6,128,576]{2,1,0:T(8,128)(2,1)S(1)}, bf16[6,128,576]{2,1,0:T(8,128)(2,1)}, u32[]{:S(2)}) copy-start(bf16[6,128,576]{2,1,0:T(8,128)(2,1)} %constant.28.clone.table_ref) | copy-start | bytes 2654212
  28.7 15.5 %collective-permute-start.1 = (f32[32,1536]{1,0:T(8,128)}, f32[32,1536]{1,0:T(8,128)S(1)}, u32[]{:S(2)}, u32[]{:S(2)}) collective-permute-start(f32[32,1536]{1,0:T(8,128)} %reshape.29), channel_id=1, source_target_pairs={{0,2},{2,4},{4,6},{6,8},{8,10},{10,12},{12,14},{14,16},{16,18},{18... | collective-permute-start | bytes 589832 | tf_op jit(solution)/shard_map/ppermute | solution.py:354
  32.9 6.1 %collective-permute-start.4 = (f32[64,1536]{1,0:T(8,128)S(1)}, f32[64,1536]{1,0:T(8,128)S(1)}, u32[]{:S(2)}, u32[]{:S(2)}) collective-permute-start(f32[64,1536]{1,0:T(8,128)S(1)} %pad_maximum_fusion.refs_0_), channel_id=1, source_target_pairs={{0,2},{2,4},{4,6},{6,8},{8,10},{10,12},{12,14},{14,16},{16,18},{18... | collective-permute-start | bytes 1179656 | tf_op jit(solution)/shard_map/ppermute | solution.py:354
  34.2 4.8 %collective-permute-start.5 = (f32[64,1536]{1,0:T(8,128)S(1)}, f32[64,1536]{1,0:T(8,128)S(1)}, u32[]{:S(2)}, u32[]{:S(2)}) collective-permute-start(f32[64,1536]{1,0:T(8,128)S(1)} %pad_maximum_fusion.refs_0_), channel_id=1, source_target_pairs={{2,0},{4,2},{6,4},{8,6},{10,8},{12,10},{14,12},{16,14},{18,16},{20... | collective-permute-start | bytes 1179656 | tf_op jit(solution)/shard_map/ppermute | solution.py:354
  35.7 8.5 %collective-permute-start.2 = (f32[32,1536]{1,0:T(8,128)S(1)}, f32[32,1536]{1,0:T(8,128)S(1)}, u32[]{:S(2)}, u32[]{:S(2)}) collective-permute-start(f32[32,1536]{1,0:T(8,128)S(1)} %reshape.30), channel_id=1, source_target_pairs={{2,0},{4,2},{6,4},{8,6},{10,8},{12,10},{14,12},{16,14},{18,16},{20... | collective-permute-start | bytes 589832 | tf_op jit(solution)/shard_map/ppermute | solution.py:354
  37.0 0.7 copy-start.7
  39.0 5.1 %copy-start.2 = (bf16[6,96,384]{2,1,0:T(8,128)(2,1)S(1)}, bf16[6,96,384]{2,1,0:T(8,128)(2,1)}, u32[]{:S(2)}) copy-start(bf16[6,96,384]{2,1,0:T(8,128)(2,1)} %constant.27.clone.table_ref) | copy-start | bytes 1327108
  42.6 30.2 %collective-permute-start.6 = (f32[8,128]{1,0:T(8,128)S(1)}, f32[8,128]{1,0:T(8,128)S(1)}, u32[]{:S(2)}, u32[]{:S(2)}) collective-permute-start(f32[8,128]{1,0:T(8,128)S(1)} %get-tuple-element.8), channel_id=1, source_target_pairs={{0,1},{1,0},{2,3},{3,2},{4,5},{5,4},{6,7},{7,6},{8,9},{9,8},{10,11... | collective-permute-start | bytes 12296 | tf_op jit(solution)/shard_map/ppermute | solution.py:380

commit v2 on v1

--- a/solution.py
+++ b/solution.py
@@ -13,6 +13,7 @@
 EPSILON = 1e-06
 HIGHEST = lax.Precision.HIGHEST
 LO = 256
+FIELDS = 16
 WEIGHT_SCALE = 512.0
 LEVER_SCALE = 32768.0
 LEVER_BIAS = 1 << 20
@@ -88,16 +89,31 @@
     return jnp.sum(jnp.where(eye, row, jnp.zeros_like(row)), axis=1, keepdims=True)
 
 
-def pack_kernel(most, lines, row_count, brick_ref, cell_ref, weight_ref, arm_ref, angle_ref, out_ref):
-    frags, beads = cell_ref.shape
-    slots = out_ref.shape[0]
+def slot_row(row, most):
+    frags = row.shape[1]
     sub = lax.broadcasted_iota(I32, (frags, frags), 0)
     lane = lax.broadcasted_iota(I32, (frags, frags), 1)
     eye = sub == lane
-    col = brick_ref[...]
-    row = jnp.sum(jnp.where(eye, col, 0), axis=0, keepdims=True)
-    earlier = jnp.logical_and(col == row, sub < lane)
-    rank = jnp.sum(jnp.where(earlier, 1, 0), axis=0, keepdims=True)
+    earlier = jnp.logical_and(eye_column(row, eye) == row, sub < lane)
+    return jnp.sum(jnp.where(earlier, 1, 0), axis=0, keepdims=True), eye
+
+
+def pack_kernel(
+    most, lines, row_count, brick_ref, angle_ref, cell_in, weight_in, arm_in, out_ref,
+    cell_ref, weight_ref, arm_ref, sems,
+):
+    copies = [
+        pltpu.make_async_copy(source, target, sems.at[k])
+        for k, (source, target) in enumerate(
+            [(cell_in, cell_ref), (weight_in, weight_ref), (arm_in, arm_ref)]
+        )
+    ]
+    for copy in copies:
+        copy.start()
+    frags, beads = cell_ref.shape
+    slots = out_ref.shape[0]
+    row = brick_ref[...]
+    rank, eye = slot_row(row, most)
     slot = row * most + rank
     place = jnp.where(lax.broadcasted_iota(I32, (slots, frags), 0) == slot, 1.0, 0.0).astype(F32)
 
@@ -110,11 +126,14 @@
         [sin_a * cos_b, sin_a * sin_b * sin_c + cos_a * cos_c, sin_a * sin_b * cos_c - cos_a * sin_c],
         [-sin_b, cos_b * sin_c, cos_b * cos_c],
     ]
+    turn = [[eye_column(value, eye) for value in values] for values in turn]
+    for copy in copies:
+        copy.wait()
     levers = []
     for i in range(3):
-        total = eye_column(turn[i][0], eye) * arm_ref[0]
+        total = turn[i][0] * arm_ref[0]
         for j in (1, 2):
-            total = total + eye_column(turn[i][j], eye) * arm_ref[j]
+            total = total + turn[i][j] * arm_ref[j]
         levers.append(jnp.round(total * LEVER_SCALE))
 
     cell = cell_ref[...]
@@ -130,6 +149,20 @@
     out_ref[:, 0:beads] = code | (weight << 16)
     out_ref[:, beads : 2 * beads] = (lx << 11) | (lz >> 10)
     out_ref[:, 2 * beads : 3 * beads] = (ly << 11) | (lz & 1023)
+
+
+def line_blur(value, derivative):
+    taps = taps_of(derivative)
+    rows, length = value.shape
+    wide = jnp.concatenate([value, jnp.zeros((rows, 128), F32)], axis=1)
+    total = None if derivative else float(taps[KR]) * value
+    for d in range(1, KR + 1):
+        up = pltpu.roll(wide, d, 1)[:, :length]
+        down = pltpu.roll(wide, length + 128 - d, 1)[:, :length]
+        pair = up - down if derivative else up + down
+        term = float(taps[KR + d]) * pair
+        total = term if total is None else total + term
+    return total
 
 
 def splat_kernel(lines, rb, got_ref, out_ref, acc_ref):
@@ -158,22 +191,8 @@
         return carry
 
     lax.fori_loop(0, slots // rb, body, 0)
-    for yh in range(his // lines):
-        out_ref[:, yh * LO : (yh + 1) * LO] = acc_ref[yh * lines : (yh + 1) * lines, :]
-
-
-def line_blur(value, derivative):
-    taps = taps_of(derivative)
-    rows, length = value.shape
-    wide = jnp.concatenate([value, jnp.zeros((rows, 128), F32)], axis=1)
-    total = None if derivative else float(taps[KR]) * value
-    for d in range(1, KR + 1):
-        up = pltpu.roll(wide, d, 1)[:, :length]
-        down = pltpu.roll(wide, length + 128 - d, 1)[:, :length]
-        pair = up - down if derivative else up + down
-        term = float(taps[KR + d]) * pair
-        total = term if total is None else total + term
-    return total
+    density = [acc_ref[yh * lines : (yh + 1) * lines, :] for yh in range(his // lines)]
+    out_ref[...] = line_blur(jnp.concatenate(density, axis=1), False)
 
 
 def split(value):
@@ -211,8 +230,7 @@
 
 def model_kernel(lines, count, _, table_ref, target_ref, *refs):
     parts, out_ref, sum_ref = refs[:count], refs[count], refs[count + 1]
-    mixed = mix_lines(table_ref, [ref[...] for ref in parts])
-    smooth = line_blur(mixed, False)
+    smooth = mix_lines(table_ref, [ref[...] for ref in parts])
     model = smooth[3 * lines :]
     target = target_ref[...]
     sums = [jnp.sum(model * target), jnp.sum(model * model), jnp.sum(target * target)]
@@ -280,53 +298,64 @@
     out_ref[...] = total
 
 
-def return_kernel(target_ref, model_ref, sum_ref, out_ref):
+def join_kernel(most, target_ref, model_ref, sum_ref, out_ref):
+    bricks = out_ref.shape[0]
     lane = lax.broadcasted_iota(I32, out_ref.shape, 1)
     sums = sum_ref[0:1, :]
     for k in range(1, sum_ref.shape[0] // 8):
         sums = sums + sum_ref[8 * k : 8 * k + 1, :]
-    total = jnp.where(lane < 6, target_ref[...], 0.0)
-    total = jnp.where((lane >= 8) & (lane < 14), pltpu.roll(model_ref[...], 8, 1), total)
-    out_ref[...] = jnp.where(lane >= 16, pltpu.roll(sums, 16, 1), total)
+    total = jnp.zeros(out_ref.shape, F32)
+    for k in range(most):
+        rows = pl.ds(k, bricks, stride=most)
+        own = jnp.where(lane < 6, target_ref[rows, :], 0.0)
+        own = own + pltpu.roll(jnp.where(lane < 6, model_ref[rows, :], 0.0), 6, 1)
+        if k == 0:
+            own = own + pltpu.roll(jnp.where(lane < 3, sums, 0.0), 12, 1)
+        total = total + (pltpu.roll(own, FIELDS * k, 1) if k else own)
+    out_ref[...] = total
 
 
 def finish_kernel(most, voxel_total, brick_ref, back_ref, out_ref):
     frags = out_ref.shape[1]
-    slots = back_ref.shape[0]
-    sub = lax.broadcasted_iota(I32, (frags, frags), 0)
-    lane = lax.broadcasted_iota(I32, (frags, frags), 1)
-    col = brick_ref[...]
-    row = jnp.sum(jnp.where(sub == lane, col, 0), axis=0, keepdims=True)
-    earlier = jnp.logical_and(col == row, sub < lane)
-    rank = jnp.sum(jnp.where(earlier, 1, 0), axis=0, keepdims=True)
-    slot = row * most + rank
-    place = jnp.where(lax.broadcasted_iota(I32, (slots, frags), 0) == slot, 1.0, 0.0).astype(F32)
+    bricks = back_ref.shape[0]
+    row = brick_ref[...]
+    rank, _ = slot_row(row, most)
+    place = jnp.where(lax.broadcasted_iota(I32, (bricks, frags), 0) == row, 1.0, 0.0).astype(F32)
     back = back_ref[...]
-    first = lax.broadcasted_iota(I32, (slots, 128), 0) % most == 0
-    sums = jnp.sum(jnp.where(first, back, 0.0), axis=0, keepdims=True)
-    cross, model_sq, target_sq = sums[:, 16:17], sums[:, 17:18], sums[:, 18:19]
+    sums = jnp.sum(back, axis=0, keepdims=True)
+    cross, model_sq, target_sq = sums[:, 12:13], sums[:, 13:14], sums[:, 14:15]
     norm_model = jnp.sqrt(model_sq + EPSILON)
     norm_target = jnp.sqrt(target_sq + EPSILON)
     corr = cross / (norm_model * norm_target)
     scale_target = voxel_total / (norm_model * norm_target)
     scale_model = voxel_total * corr / (norm_model * norm_model)
-    mine = lax.dot_general(
+    found = lax.dot_general(
         back, place, (((0,), (0,)), ((), ())), precision=HIGHEST, preferred_element_type=F32
     )
-    out_ref[...] = scale_target * mine[0:6] - scale_model * mine[8:14]
-
-
-def call(kernel, out_shape, *args, scratch=(), name=None):
+    mine = jnp.zeros((FIELDS, frags), F32)
+    for k in range(most):
+        mine = jnp.where(rank == k, found[FIELDS * k : FIELDS * (k + 1)], mine)
+    out_ref[...] = scale_target * mine[0:6] - scale_model * mine[6:12]
+
+
+def cost(macs, nbytes):
+    return pl.CostEstimate(flops=2 * macs, bytes_accessed=nbytes, transcendentals=0)
+
+
+def call(kernel, out_shape, *args, scratch=(), name=None, macs=0, in_specs=None):
+    kwargs = {} if in_specs is None else {"in_specs": in_specs}
     return pl.pallas_call(
         kernel,
         out_shape=out_shape,
         scratch_shapes=list(scratch),
         compiler_params=pltpu.CompilerParams(vmem_limit_bytes=VMEM_BYTES),
+        cost_estimate=cost(macs, 4 * sum(a.size for a in args)),
         name=name,
+        **kwargs,
     )(*args)
 
 
-def call_at(kernel, out_shape, index, table, *args, name=None):
+def call_at(kernel, out_shape, index, table, *args, name=None, macs=0):
     def whole(shape):
         return pl.BlockSpec(shape, lambda i, s: (0,) * len(shape))
 
@@ -344,8 +373,18 @@
             out_specs=specs[0] if single else specs,
         ),
         compiler_params=pltpu.CompilerParams(vmem_limit_bytes=VMEM_BYTES),
+        cost_estimate=cost(macs, 4 * sum(a.size for a in args)),
         name=name,
     )(index, table, *args)
+
+
+def looked_up(values, position):
+    found = jnp.full((), int(values[0]), I32)
+    for i in range(1, len(values)):
+        step = int(values[i]) - int(values[i - 1])
+        if step:
+            found = found + step * (position >= i).astype(I32)
+    return found
 
 
 def shifted(value, axis, step):
@@ -392,6 +431,7 @@
     voxel_total = float(brick_count * columns * relay_count * planes * rows)
     most = max(2, 2 * frags // brick_count)
     slots = brick_count * most
+    assert most * FIELDS <= 128
 
     z_total, x_total = relay_count * planes, brick_count * columns
     gz, dz = axis_matrix(z_total, False), axis_matrix(z_total, True)
@@ -408,8 +448,8 @@
         [np.arange(columns), np.arange(-columns, 0), np.arange(columns, 2 * columns)],
     )
     r, b = lax.axis_index("relay"), lax.axis_index("brick")
-    target_index = (jnp.asarray(tz)[r] * tn + jnp.asarray(tx)[b]).reshape(1)
-    model_index = (jnp.asarray(mz)[r] * mn + jnp.asarray(mx)[b]).reshape(1)
+    target_index = (looked_up(tz, r) * tn + looked_up(tx, b)).reshape(1)
+    model_index = (looked_up(mz, r) * mn + looked_up(mx, b)).reshape(1)
 
     target_lines = target.reshape(lines, rows)
     target_blocks = relay_blocks(target, reach_one)
@@ -417,59 +457,78 @@
     right_edge = jnp.concatenate([t[:, :KR] for t in target_blocks], axis=0)
     from_left = shifted(left_edge.reshape(-1, rows), "brick", 1)
     from_right = shifted(right_edge.reshape(-1, rows), "brick", -1)
-    target_parts = [t.reshape(lines, rows) for t in target_blocks] + [from_left, from_right]
-
+
+    brick_row = frag_brick.reshape(1, frags)
+    vmem, anywhere = pl.BlockSpec(memory_space=pltpu.VMEM), pl.BlockSpec(memory_space=pl.ANY)
     sent = call(
         functools.partial(pack_kernel, most, lines, rows),
         jax.ShapeDtypeStruct((slots, 3 * beads), I32),
-        frag_brick, bead_cell, bead_weight, bead_arm, frag_angle,
+        brick_row, frag_angle, bead_cell, bead_weight, bead_arm,
+        in_specs=[vmem, vmem, anywhere, anywhere, anywhere],
+        scratch=[
+            pltpu.VMEM(bead_cell.shape, I32),
+            pltpu.VMEM(bead_weight.shape, BF16),
+            pltpu.VMEM(bead_arm.shape, F32),
+            pltpu.SemaphoreType.DMA((3,)),
+        ],
         name="pack",
     )
     got = lax.all_to_all(sent, "brick", split_axis=0, concat_axis=0, tiled=True)
-    density = call(
-        functools.partial(splat_kernel, lines, 8),
+    got, from_left, from_right = lax.optimization_barrier((got, from_left, from_right))
+    target_parts = [t.reshape(lines, rows) for t in target_blocks] + [from_left, from_right]
+    smooth = call(
+        functools.partial(splat_kernel, lines, min(32, slots)),
         jax.ShapeDtypeStruct((lines, rows), F32),
         got,
         scratch=[pltpu.VMEM((his, LO), F32)],
         name="splat",
-    )
-    blocks = jnp.concatenate(relay_blocks(density, reach_two), axis=0)
+        macs=slots * beads * his * LO,
+    )
+    blocks = jnp.concatenate(relay_blocks(smooth, reach_two), axis=0)
+    target_field = call_at(
+        functools.partial(target_kernel, lines, len(target_parts)),
+        jax.ShapeDtypeStruct((3 * his, 2 * LO), BF16),
+        target_index, jnp.asarray(target_table), *target_parts,
+        name="target_fields",
+        macs=9 * lines * rows * 128,
+    )
+    blocks, target_field = lax.optimization_barrier((blocks, target_field))
     model_parts = [blocks, shifted(blocks, "brick", 1), shifted(blocks, "brick", -1)]
-
-    field_shape = jax.ShapeDtypeStruct((3 * his, 2 * LO), BF16)
 
     def sample(field, name):
         return call(
-            functools.partial(sample_kernel, his, 8),
+            functools.partial(sample_kernel, his, min(32, slots)),
             jax.ShapeDtypeStruct((slots, 128), F32),
             got, field,
             scratch=[pltpu.VMEM((3, slots, beads), F32)],
             name=name,
+            macs=6 * slots * beads * his * LO,
         )
 
-    target_field = call_at(
-        functools.partial(target_kernel, lines, len(target_parts)),
-        field_shape, target_index, jnp.asarray(target_table), *target_parts,
-        name="target_fields",
-    )
     target_sums = sample(target_field, "target_sample")
+    target_sums, *model_parts = lax.optimization_barrier((target_sums, *model_parts))
     model_field, partial = call_at(
         functools.partial(model_kernel, lines, len(model_parts)),
-        [field_shape, jax.ShapeDtypeStruct((8, 128), F32)],
+        [
+            jax.ShapeDtypeStruct((3 * his, 2 * LO), BF16),
+            jax.ShapeDtypeStruct((8, 128), F32),
+        ],
         model_index, jnp.asarray(model_table), target_lines, *model_parts,
         name="model_fields",
     )
     partials = relay_total(partial)
     model_sums = sample(model_field, "model_sample")
     leaving = call(
-        return_kernel, jax.ShapeDtypeStruct((slots, 128), F32), target_sums, model_sums, partials,
+        functools.partial(join_kernel, most),
+        jax.ShapeDtypeStruct((brick_count, 128), F32),
+        target_sums, model_sums, partials,
         name="join",
     )
     back = lax.all_to_all(leaving, "brick", split_axis=0, concat_axis=0, tiled=True)
     return call(
         functools.partial(finish_kernel, most, voxel_total),
         jax.ShapeDtypeStruct((6, frags), F32),
-        frag_brick, back,
+        brick_row, back,
         name="finish",
     )
 

time: 92.8 us -> 85 us (0.916)
  Pallas kernels: 39.8 us -> 32.1 us
  starting transfers between devices: 17.5 us -> 22.1 us
  blocking collectives: 18.5 us -> 14.2 us
  waiting for transfers between devices: 10.2 us -> 11.9 us
  local copies, waits for them, and re-layouts: 5.27 us -> 3.92 us
    pallas_call x6, Pallas kernels: 34.7 us -> 28.8 us  [call(): pl.pallas_call(kernel, out_shape=out_shape, scratch_shapes=list(scratch),...]
    ppermute x4, starting transfers between devices: 5.26 us -> 9.83 us  [shifted(): return lax.ppermute(value, axis, pairs)]
    all_to_all x1, blocking collectives: 18.5 us -> 14.2 us  [shards(): lax.all_to_all(leaving, 'brick', split_axis=0, concat_axis=0, tiled=True)]
    ppermute x4, waiting for transfers between devices: 0.01 us -> 3.64 us  [shifted(): return lax.ppermute(value, axis, pairs)]
    pallas_call x2, Pallas kernels: 5.12 us -> 3.22 us  [call_at(): pl.pallas_call(kernel, out_shape=out_shape, grid_spec=pltpu.PrefetchScala...]
    all_to_all x1, waiting for transfers between devices: 1.65 us -> 0.01 us  [shards(): got = lax.all_to_all(sent, 'brick', split_axis=0, concat_axis=0, tiled=True)]
    unnamed x17 -> x16, local copies, waits for them, and re-layouts: 3.73 us -> 3.72 us
  transfers between devices with their start and end apart: 8 -> 8, of which waited for: 3 -> 3; matrix products, arithmetic and copies ran while one was open for 2% -> 0% of each run, Pallas kernels for 35% -> 28%
where the time goes in v2:
time: 85 us; the launch traced here: 84.5 us
  Pallas kernels  32.1 us (38%)
  starting transfers between devices  22.1 us (26%)
  blocking collectives  14.2 us (17%)
  waiting for transfers between devices  11.9 us (14%)
  local copies, waits for them, and re-layouts  3.92 us (5%)
    pallas_call x6, Pallas kernels, call(): pl.pallas_call(kernel, out_shape=out_shape, scratch_shapes=list(scratch),...  28.8 us
    all_to_all x1, blocking collectives, shards(): lax.all_to_all(leaving, 'brick', split_axis=0, concat_axis=0, tiled=True)  14.2 us
    ppermute x4, starting transfers between devices, shifted(): return lax.ppermute(value, axis, pairs)  9.83 us
    ppermute x2, waiting for transfers between devices, relay_blocks(): return [value, lax.ppermute(value, 'relay', [(0, 1), (1, 0)])]  8.26 us
    all_to_all x1, starting transfers between devices, shards(): got = lax.all_to_all(sent, 'brick', split_axis=0, concat_axis=0, tiled=True)  7.51 us
    unnamed x16, local copies, waits for them, and re-layouts  3.72 us
    ppermute x4, waiting for transfers between devices, shifted(): return lax.ppermute(value, axis, pairs)  3.64 us
    pallas_call x2, Pallas kernels, call_at(): pl.pallas_call(kernel, out_shape=out_shape, grid_spec=pltpu.PrefetchScala...  3.22 us
  transfers between devices with their start and end apart: 8, of which 3 were waited for; matrix products, arithmetic and copies ran while one was open for 0% of the time, Pallas kernels for 28%

profile of v2, /device:TPU:0, one launch (start us, length us, event | category | flops | bytes accessed | tf_op | source)
XLA Modules:
  0.0 84.5 jit_solution(4629649810723221276)
XLA Ops:
  0.0 0.7 copy-done.7
  0.7 0.9 %copy-done.3 = f32[3,64,128]{2,1,0:T(8,128)S(1)} copy-done((f32[3,64,128]{2,1,0:T(8,128)S(1)}, f32[3,64,128]{2,1,0:T(8,128)}, u32[]{:S(2)}) %copy-start.3) | copy-done | bytes 98328
  1.6 0.8 copy-done.4
  2.3 0.7 copy-done.5
  3.0 0.7 copy-done.6
  3.7 1.5 %pack.1 = s32[128,384]{1,0:T(8,128)} custom-call(s32[1,64]{1,0:T(1,128)S(1)} %bitcast.18, f32[3,64]{1,0:T(4,128)S(1)} %copy-done.6, s32[64,128]{1,0:T(8,128)S(1)} %copy-done.4, bf16[64,128]{1,0:T(8,128)(2,1)S(1)} %copy-done.5, f32[3,64,128]{2,1,0:T(8,128)S(1)} %copy-done.3), custom_call_target="tpu_custom_call" | custom-call | bytes 164864 | tf_op jit(solution)/shard_map/pack/pallas_call | solution.py:347
  5.2 0.0 copy-start
  5.2 7.5 %all-to-all-start = ((s32[16,8,384]{2,1,0:T(8,128)}), s32[16,8,384]{2,1,0:T(8,128)S(1)}, u32[]{:S(2)}, u32[]{:S(2)}) async-start(s32[16,8,384]{2,1,0:T(8,128)} %bitcast.1), calls=%async_computation | async-start | bytes 393216 | tf_op jit(solution)/shard_map/all_to_all | solution.py:476
  12.8 1.6 %collective-permute-start = (f32[4,8,1536]{2,1,0:T(8,128)S(1)}, f32[4,8,1536]{2,1,0:T(8,128)S(1)}, u32[]{:S(2)}, u32[]{:S(2)}) collective-permute-start(f32[4,8,1536]{2,1,0:T(8,128)S(1)} %copy-done), channel_id=1, source_target_pairs={{0,1},{1,0},{2,3},{3,2},{4,5},{5,4},{6,7},{7,6},{8,9},{9,8},{10,11... | collective-permute-start | bytes 589832 | tf_op jit(solution)/shard_map/ppermute | solution.py:399
  14.4 5.7 %collective-permute-done = f32[4,8,1536]{2,1,0:T(8,128)S(1)} collective-permute-done((f32[4,8,1536]{2,1,0:T(8,128)S(1)}, f32[4,8,1536]{2,1,0:T(8,128)S(1)}, u32[]{:S(2)}, u32[]{:S(2)}) %collective-permute-start) | collective-permute-done | bytes 196640 | tf_op jit(solution)/shard_map/ppermute | solution.py:399
  20.2 0.1 reshape.26
  20.3 0.1 reshape.25
  20.4 1.6 %collective-permute-start.1 = (f32[32,1536]{1,0:T(8,128)S(1)}, f32[32,1536]{1,0:T(8,128)S(1)}, u32[]{:S(2)}, u32[]{:S(2)}) collective-permute-start(f32[32,1536]{1,0:T(8,128)S(1)} %reshape.25), channel_id=1, source_target_pairs={{0,2},{2,4},{4,6},{6,8},{8,10},{10,12},{12,14},{14,16},{16,18},{18... | collective-permute-start | bytes 589832 | tf_op jit(solution)/shard_map/ppermute | solution.py:393
  21.9 1.3 %collective-permute-start.2 = (f32[32,1536]{1,0:T(8,128)S(1)}, f32[32,1536]{1,0:T(8,128)S(1)}, u32[]{:S(2)}, u32[]{:S(2)}) collective-permute-start(f32[32,1536]{1,0:T(8,128)S(1)} %reshape.26), channel_id=1, source_target_pairs={{2,0},{4,2},{6,4},{8,6},{10,8},{12,10},{14,12},{16,14},{18,16},{20... | collective-permute-start | bytes 589832 | tf_op jit(solution)/shard_map/ppermute | solution.py:393
  23.2 0.0 all-to-all-done
  23.2 0.0 collective-permute-done.1.refs_2_
  23.3 3.6 %collective-permute-done.2.refs_3_ = f32[32,1536]{1,0:T(8,128)S(1)} collective-permute-done((f32[32,1536]{1,0:T(8,128)S(1)}, f32[32,1536]{1,0:T(8,128)S(1)}, u32[]{:S(2)}, u32[]{:S(2)}) %collective-permute-start.2) | collective-permute-done | bytes 196640 | tf_op jit(solution)/shard_map/ppermute | solution.py:393
  26.9 4.0 %splat.1 = f32[32,1536]{1,0:T(8,128)S(1)} custom-call(s32[128,384]{1,0:T(8,128)S(1)} %bitcast.13), custom_call_target="tpu_custom_call" | custom-call | flops 1610612736 | bytes 196608 | tf_op jit(solution)/shard_map/splat/pallas_call | solution.py:347
  30.9 1.6 %collective-permute-start.3 = (f32[32,1536]{1,0:T(8,128)S(1)}, f32[32,1536]{1,0:T(8,128)S(1)}, u32[]{:S(2)}, u32[]{:S(2)}) collective-permute-start(f32[32,1536]{1,0:T(8,128)S(1)} %splat.1), channel_id=1, source_target_pairs={{0,1},{1,0},{2,3},{3,2},{4,5},{5,4},{6,7},{7,6},{8,9},{9,8},{10,11... | collective-permute-start | bytes 589832 | tf_op jit(solution)/shard_map/ppermute | solution.py:399
  32.4 1.6 %target_fields.1.field_ref = bf16[576,512]{1,0:T(8,128)(2,1)S(1)} custom-call(s32[1]{0:T(128)} %bitcast.3._, bf16[6,96,384]{2,1,0:T(8,128)(2,1)S(1)} %copy-done.2, f32[32,1536]{1,0:T(8,128)S(1)} %bitcast.10, f32[32,1536]{1,0:T(8,128)S(1)} %bitcast.12, f32[32,1536]{1,0:T(8,128)S(1)} %collective-permute-done.1.refs_2_, ...), custom_call_target="tpu_custom_call" | custom-call | flops 113246208 | bytes 786432 | tf_op jit(solution)/shard_map/target_fields/pallas_call | solution.py:365
  34.0 2.6 %collective-permute-done.3 = f32[32,1536]{1,0:T(8,128)S(1)} collective-permute-done((f32[32,1536]{1,0:T(8,128)S(1)}, f32[32,1536]{1,0:T(8,128)S(1)}, u32[]{:S(2)}, u32[]{:S(2)}) %collective-permute-start.3) | collective-permute-done | bytes 196640 | tf_op jit(solution)/shard_map/ppermute | solution.py:399
  36.6 0.0 copy-start.1
  36.6 1.4 %collective-permute-start.5 = (f32[64,1536]{1,0:T(8,128)S(1)}, f32[64,1536]{1,0:T(8,128)S(1)}, u32[]{:S(2)}, u32[]{:S(2)}) collective-permute-start(f32[64,1536]{1,0:T(8,128)S(1)} %pad_maximum_fusion.refs_0_), channel_id=1, source_target_pairs={{2,0},{4,2},{6,4},{8,6},{10,8},{12,10},{14,12},{16,14},{18,16},{20... | collective-permute-start | bytes 1179656 | tf_op jit(solution)/shard_map/ppermute | solution.py:393
  38.1 5.6 %collective-permute-start.4 = (f32[64,1536]{1,0:T(8,128)S(1)}, f32[64,1536]{1,0:T(8,128)S(1)}, u32[]{:S(2)}, u32[]{:S(2)}) collective-permute-start(f32[64,1536]{1,0:T(8,128)S(1)} %pad_maximum_fusion.refs_0_), channel_id=1, source_target_pairs={{0,2},{2,4},{4,6},{6,8},{8,10},{10,12},{12,14},{14,16},{16,18},{18... | collective-permute-start | bytes 1179656 | tf_op jit(solution)/shard_map/ppermute | solution.py:393
  43.6 11.2 %target_sample.1.target_ref = f32[128,128]{1,0:T(8,128)S(1)} custom-call(s32[128,384]{1,0:T(8,128)S(1)} %bitcast.14, bf16[576,512]{1,0:T(8,128)(2,1)S(1)} %target_fields.1.field_ref), custom_call_target="tpu_custom_call" | custom-call | flops 9663676416 | bytes 1376256 | tf_op jit(solution)/shard_map/target_sample/pallas_call | solution.py:347
  54.8 0.0 collective-permute-done.5.refs_2_
  54.8 1.6 %model_fields.1 = (bf16[576,512]{1,0:T(8,128)(2,1)S(1)}, f32[8,128]{1,0:T(8,128)S(1)}) custom-call(s32[1]{0:T(128)} %bitcast.3._, bf16[6,128,576]{2,1,0:T(8,128)(2,1)S(1)} %copy-done.1, f32[32,1536]{1,0:T(8,128)S(1)} %bitcast.11, f32[64,1536]{1,0:T(8,128)S(1)} %pad_maximum_fusion.refs_0_, f32[64,1536]{1,0:T(8,128)S(1)} %collective-permute-done.4.refs_1_, ...), custom_call_target="tpu_custom_call" | custom-call | bytes 1376256 | tf_op jit(solution)/shard_map/model_fields/pallas_call | solution.py:365
  56.5 1.6 %collective-permute-start.6 = (f32[8,128]{1,0:T(8,128)S(1)}, f32[8,128]{1,0:T(8,128)S(1)}, u32[]{:S(2)}, u32[]{:S(2)}) collective-permute-start(f32[8,128]{1,0:T(8,128)S(1)} %get-tuple-element.26), channel_id=1, source_target_pairs={{0,1},{1,0},{2,3},{3,2},{4,5},{5,4},{6,7},{7,6},{8,9},{9,8},{10,11... | collective-permute-start | bytes 12296 | tf_op jit(solution)/shard_map/ppermute | solution.py:419
  58.1 11.2 %model_sample.1.model_ref = f32[128,128]{1,0:T(8,128)S(1)} custom-call(s32[128,384]{1,0:T(8,128)S(1)} %bitcast.15, bf16[576,512]{1,0:T(8,128)(2,1)S(1)} %get-tuple-element.25.field_ref), custom_call_target="tpu_custom_call" | custom-call | flops 9663676416 | bytes 1376256 | tf_op jit(solution)/shard_map/model_sample/pallas_call | solution.py:347
  69.3 0.2 join.1
  69.4 14.2 %all_to_all.23 = f32[16,1,128]{2,1,0:T(1,128)S(1)} all-to-all(f32[16,1,128]{2,1,0:T(1,128)S(1)} %bitcast.16), channel_id=1, replica_groups=mesh['brick'=16,'relay'=2] {'brick'}, dimensions={0} | all-to-all | bytes 16384 | tf_op jit(solution)/shard_map/all_to_all | solution.py:527
  83.6 0.9 %finish.1 = f32[6,64]{1,0:T(8,128)} custom-call(s32[1,64]{1,0:T(1,128)S(1)} %bitcast.19, f32[16,128]{1,0:T(8,128)S(1)} %bitcast.17), custom_call_target="tpu_custom_call" | custom-call | bytes 8448 | tf_op jit(solution)/shard_map/finish/pallas_call | solution.py:347
  (17 shorter events, 0.2 us)
Async XLA Ops:
  0.0 0.7 copy-start.7
  0.7 0.9 %copy-start.3 = (f32[3,64,128]{2,1,0:T(8,128)S(1)}, f32[3,64,128]{2,1,0:T(8,128)}, u32[]{:S(2)}) copy-start(f32[3,64,128]{2,1,0:T(8,128)} %arm_in.1) | copy-start | bytes 294916
  1.5 0.8 copy-start.4
  2.3 0.7 copy-start.5
  3.0 0.7 copy-start.6
  5.2 7.5 %copy-start = (f32[4,8,1536]{2,1,0:T(8,128)S(1)}, f32[4,8,1536]{2,1,0:T(8,128)}, u32[]{:S(2)}) copy-start(f32[4,8,1536]{2,1,0:T(8,128)} %param.8) | copy-start | bytes 589828
  5.2 18.0 %all-to-all-start = ((s32[16,8,384]{2,1,0:T(8,128)}), s32[16,8,384]{2,1,0:T(8,128)S(1)}, u32[]{:S(2)}, u32[]{:S(2)}) async-start(s32[16,8,384]{2,1,0:T(8,128)} %bitcast.1), calls=%async_computation | async-start | bytes 393216 | tf_op jit(solution)/shard_map/all_to_all | solution.py:476
  12.8 7.3 %collective-permute-start = (f32[4,8,1536]{2,1,0:T(8,128)S(1)}, f32[4,8,1536]{2,1,0:T(8,128)S(1)}, u32[]{:S(2)}, u32[]{:S(2)}) collective-permute-start(f32[4,8,1536]{2,1,0:T(8,128)S(1)} %copy-done), channel_id=1, source_target_pairs={{0,1},{1,0},{2,3},{3,2},{4,5},{5,4},{6,7},{7,6},{8,9},{9,8},{10,11... | collective-permute-start | bytes 589832 | tf_op jit(solution)/shard_map/ppermute | solution.py:399
  20.4 2.9 %collective-permute-start.1 = (f32[32,1536]{1,0:T(8,128)S(1)}, f32[32,1536]{1,0:T(8,128)S(1)}, u32[]{:S(2)}, u32[]{:S(2)}) collective-permute-start(f32[32,1536]{1,0:T(8,128)S(1)} %reshape.25), channel_id=1, source_target_pairs={{0,2},{2,4},{4,6},{6,8},{8,10},{10,12},{12,14},{14,16},{16,18},{18... | collective-permute-start | bytes 589832 | tf_op jit(solution)/shard_map/ppermute | solution.py:393
  21.9 4.9 %collective-permute-start.2 = (f32[32,1536]{1,0:T(8,128)S(1)}, f32[32,1536]{1,0:T(8,128)S(1)}, u32[]{:S(2)}, u32[]{:S(2)}) collective-permute-start(f32[32,1536]{1,0:T(8,128)S(1)} %reshape.26), channel_id=1, source_target_pairs={{2,0},{4,2},{6,4},{8,6},{10,8},{12,10},{14,12},{16,14},{18,16},{20... | collective-permute-start | bytes 589832 | tf_op jit(solution)/shard_map/ppermute | solution.py:393
  26.9 5.5 %copy-start.2 = (bf16[6,96,384]{2,1,0:T(8,128)(2,1)S(1)}, bf16[6,96,384]{2,1,0:T(8,128)(2,1)}, u32[]{:S(2)}) copy-start(bf16[6,96,384]{2,1,0:T(8,128)(2,1)} %constant.26.clone.table_ref) | copy-start | bytes 1327108
  30.9 5.7 %collective-permute-start.3 = (f32[32,1536]{1,0:T(8,128)S(1)}, f32[32,1536]{1,0:T(8,128)S(1)}, u32[]{:S(2)}, u32[]{:S(2)}) collective-permute-start(f32[32,1536]{1,0:T(8,128)S(1)} %splat.1), channel_id=1, source_target_pairs={{0,1},{1,0},{2,3},{3,2},{4,5},{5,4},{6,7},{7,6},{8,9},{9,8},{10,11... | collective-permute-start | bytes 589832 | tf_op jit(solution)/shard_map/ppermute | solution.py:399
  36.6 18.2 %copy-start.1 = (bf16[6,128,576]{2,1,0:T(8,128)(2,1)S(1)}, bf16[6,128,576]{2,1,0:T(8,128)(2,1)}, u32[]{:S(2)}) copy-start(bf16[6,128,576]{2,1,0:T(8,128)(2,1)} %constant.27.clone.table_ref) | copy-start | bytes 2654212
  36.6 18.2 %collective-permute-start.5 = (f32[64,1536]{1,0:T(8,128)S(1)}, f32[64,1536]{1,0:T(8,128)S(1)}, u32[]{:S(2)}, u32[]{:S(2)}) collective-permute-start(f32[64,1536]{1,0:T(8,128)S(1)} %pad_maximum_fusion.refs_0_), channel_id=1, source_target_pairs={{2,0},{4,2},{6,4},{8,6},{10,8},{12,10},{14,12},{16,14},{18,16},{20... | collective-permute-start | bytes 1179656 | tf_op jit(solution)/shard_map/ppermute | solution.py:393
  38.1 16.7 %collective-permute-start.4 = (f32[64,1536]{1,0:T(8,128)S(1)}, f32[64,1536]{1,0:T(8,128)S(1)}, u32[]{:S(2)}, u32[]{:S(2)}) collective-permute-start(f32[64,1536]{1,0:T(8,128)S(1)} %pad_maximum_fusion.refs_0_), channel_id=1, source_target_pairs={{0,2},{2,4},{4,6},{6,8},{8,10},{10,12},{12,14},{14,16},{16,18},{18... | collective-permute-start | bytes 1179656 | tf_op jit(solution)/shard_map/ppermute | solution.py:393
  56.5 12.8 %collective-permute-start.6 = (f32[8,128]{1,0:T(8,128)S(1)}, f32[8,128]{1,0:T(8,128)S(1)}, u32[]{:S(2)}, u32[]{:S(2)}) collective-permute-start(f32[8,128]{1,0:T(8,128)S(1)} %get-tuple-element.26), channel_id=1, source_target_pairs={{0,1},{1,0},{2,3},{3,2},{4,5},{5,4},{6,7},{7,6},{8,9},{9,8},{10,11... | collective-permute-start | bytes 12296 | tf_op jit(solution)/shard_map/ppermute | solution.py:419

commit v3 on v2

--- a/solution.py
+++ b/solution.py
@@ -18,6 +18,7 @@
 LEVER_SCALE = 32768.0
 LEVER_BIAS = 1 << 20
 VMEM_BYTES = 48 << 20
+PACK_VMEM_BYTES = 60 << 20
 F32 = jnp.float32
 BF16 = jnp.bfloat16
 I32 = jnp.int32
@@ -245,14 +246,14 @@
     store_fields([grad_x, grad_y, grad_z], lines, out_ref)
 
 
-def sample_kernel(his, rb, got_ref, field_ref, out_ref, force_ref):
-    slots = got_ref.shape[0]
+def sample_kernel(his, rb, start, got_ref, field_ref, out_ref, force_ref):
+    slots = out_ref.shape[0]
     beads = got_ref.shape[1] // 3
     lo_iota = lax.broadcasted_iota(I32, (LO, beads), 0)
     sub_iota = lax.broadcasted_iota(I32, (8, beads), 0)
 
     def body(i, carry):
-        word = got_ref[pl.ds(i * rb, rb), 0:beads]
+        word = got_ref[pl.ds(start + i * rb, rb), 0:beads]
         lo = word & (LO - 1)
         hi = (word >> 8) & 255
         picks = [
@@ -279,8 +280,9 @@
         return carry
 
     lax.fori_loop(0, slots // rb, body, 0)
-    first, second = got_ref[:, beads : 2 * beads], got_ref[:, 2 * beads : 3 * beads]
-    weight = (got_ref[:, 0:beads] >> 16).astype(F32) * (1.0 / WEIGHT_SCALE)
+    rows = slice(start, start + slots)
+    first, second = got_ref[rows, beads : 2 * beads], got_ref[rows, 2 * beads : 3 * beads]
+    weight = (got_ref[rows, 0:beads] >> 16).astype(F32) * (1.0 / WEIGHT_SCALE)
     lever_z = (((first & 2047) << 10) | (second & 1023)) - LEVER_BIAS
     levers = [
         v.astype(F32) * (1.0 / LEVER_SCALE) for v in (first >> 11, second >> 11, lever_z)
@@ -298,7 +300,7 @@
     out_ref[...] = total
 
 
-def join_kernel(most, target_ref, model_ref, sum_ref, out_ref):
+def join_kernel(most, first_ref, second_ref, model_ref, sum_ref, out_ref):
     bricks = out_ref.shape[0]
     lane = lax.broadcasted_iota(I32, out_ref.shape, 1)
     sums = sum_ref[0:1, :]
@@ -306,8 +308,9 @@
         sums = sums + sum_ref[8 * k : 8 * k + 1, :]
     total = jnp.zeros(out_ref.shape, F32)
     for k in range(most):
-        rows = pl.ds(k, bricks, stride=most)
-        own = jnp.where(lane < 6, target_ref[rows, :], 0.0)
+        rows, half = pl.ds(k, bricks, stride=most), pl.ds(k, bricks // 2, stride=most)
+        own = jnp.concatenate([first_ref[half, :], second_ref[half, :]], axis=0)
+        own = jnp.where(lane < 6, own, 0.0)
         own = own + pltpu.roll(jnp.where(lane < 6, model_ref[rows, :], 0.0), 6, 1)
         if k == 0:
             own = own + pltpu.roll(jnp.where(lane < 3, sums, 0.0), 12, 1)
@@ -342,13 +345,15 @@
     return pl.CostEstimate(flops=2 * macs, bytes_accessed=nbytes, transcendentals=0)
 
 
-def call(kernel, out_shape, *args, scratch=(), name=None, macs=0, in_specs=None):
+def call(
+    kernel, out_shape, *args, scratch=(), name=None, macs=0, in_specs=None, vmem=VMEM_BYTES
+):
     kwargs = {} if in_specs is None else {"in_specs": in_specs}
     return pl.pallas_call(
         kernel,
         out_shape=out_shape,
         scratch_shapes=list(scratch),
-        compiler_params=pltpu.CompilerParams(vmem_limit_bytes=VMEM_BYTES),
+        compiler_params=pltpu.CompilerParams(vmem_limit_bytes=vmem),
         cost_estimate=cost(macs, 4 * sum(a.size for a in args)),
         name=name,
         **kwargs,
@@ -459,12 +464,12 @@
     from_right = shifted(right_edge.reshape(-1, rows), "brick", -1)
 
     brick_row = frag_brick.reshape(1, frags)
-    vmem, anywhere = pl.BlockSpec(memory_space=pltpu.VMEM), pl.BlockSpec(memory_space=pl.ANY)
+    vmem, hbm = pl.BlockSpec(memory_space=pltpu.VMEM), pl.BlockSpec(memory_space=pltpu.HBM)
     sent = call(
         functools.partial(pack_kernel, most, lines, rows),
         jax.ShapeDtypeStruct((slots, 3 * beads), I32),
         brick_row, frag_angle, bead_cell, bead_weight, bead_arm,
-        in_specs=[vmem, vmem, anywhere, anywhere, anywhere],
+        in_specs=[vmem, vmem, hbm, hbm, hbm],
         scratch=[
             pltpu.VMEM(bead_cell.shape, I32),
             pltpu.VMEM(bead_weight.shape, BF16),
@@ -472,10 +477,9 @@
             pltpu.SemaphoreType.DMA((3,)),
         ],
         name="pack",
+        vmem=PACK_VMEM_BYTES,
     )
     got = lax.all_to_all(sent, "brick", split_axis=0, concat_axis=0, tiled=True)
-    got, from_left, from_right = lax.optimization_barrier((got, from_left, from_right))
-    target_parts = [t.reshape(lines, rows) for t in target_blocks] + [from_left, from_right]
     smooth = call(
         functools.partial(splat_kernel, lines, min(32, slots)),
         jax.ShapeDtypeStruct((lines, rows), F32),
@@ -484,6 +488,8 @@
         name="splat",
         macs=slots * beads * his * LO,
     )
+    smooth, from_left, from_right = lax.optimization_barrier((smooth, from_left, from_right))
+    target_parts = [t.reshape(lines, rows) for t in target_blocks] + [from_left, from_right]
     blocks = jnp.concatenate(relay_blocks(smooth, reach_two), axis=0)
     target_field = call_at(
         functools.partial(target_kernel, lines, len(target_parts)),
@@ -492,21 +498,25 @@
         name="target_fields",
         macs=9 * lines * rows * 128,
     )
-    blocks, target_field = lax.optimization_barrier((blocks, target_field))
+
+    def sample(field, start, count, name):
+        return call(
+            functools.partial(sample_kernel, his, min(32, count), start),
+            jax.ShapeDtypeStruct((count, 128), F32),
+            got, field,
+            scratch=[pltpu.VMEM((3, count, beads), F32)],
+            name=name,
+            macs=6 * count * beads * his * LO,
+        )
+
+    half = slots // 2
+    target_first = sample(target_field, 0, half, "target_sample_a")
+    blocks, target_first, target_field = lax.optimization_barrier(
+        (blocks, target_first, target_field)
+    )
     model_parts = [blocks, shifted(blocks, "brick", 1), shifted(blocks, "brick", -1)]
-
-    def sample(field, name):
-        return call(
-            functools.partial(sample_kernel, his, min(32, slots)),
-            jax.ShapeDtypeStruct((slots, 128), F32),
-            got, field,
-            scratch=[pltpu.VMEM((3, slots, beads), F32)],
-            name=name,
-            macs=6 * slots * beads * his * LO,
-        )
-
-    target_sums = sample(target_field, "target_sample")
-    target_sums, *model_parts = lax.optimization_barrier((target_sums, *model_parts))
+    target_second = sample(target_field, half, slots - half, "target_sample_b")
+    target_second, *model_parts = lax.optimization_barrier((target_second, *model_parts))
     model_field, partial = call_at(
         functools.partial(model_kernel, lines, len(model_parts)),
         [
@@ -517,11 +527,11 @@
         name="model_fields",
     )
     partials = relay_total(partial)
-    model_sums = sample(model_field, "model_sample")
+    model_sums = sample(model_field, 0, slots, "model_sample")
     leaving = call(
         functools.partial(join_kernel, most),
         jax.ShapeDtypeStruct((brick_count, 128), F32),
-        target_sums, model_sums, partials,
+        target_first, target_second, model_sums, partials,
         name="join",
     )
     back = lax.all_to_all(leaving, "brick", split_axis=0, concat_axis=0, tiled=True)

time: 85 us -> 78.6 us (0.925)
  waiting for transfers between devices: 11.9 us -> 5.7 us
  local copies, waits for them, and re-layouts: 3.92 us -> 0.88 us
  blocking collectives: 14.2 us -> 16.2 us
  Pallas kernels: 32.1 us -> 33.1 us
    ppermute x4, waiting for transfers between devices: 3.64 us -> 0.01 us  [shifted(): return lax.ppermute(value, axis, pairs)]
    unnamed x16 -> x8, local copies, waits for them, and re-layouts: 3.72 us -> 0.68 us
    ppermute x2, waiting for transfers between devices: 8.26 us -> 5.68 us  [relay_blocks(): return [value, lax.ppermute(value, 'relay', [(0, 1), (1, 0)])]]
    all_to_all x1, blocking collectives: 14.2 us -> 16.2 us  [shards(): lax.all_to_all(leaving, 'brick', split_axis=0, concat_axis=0, tiled=True)]
    pallas_call x6 -> x7, Pallas kernels: 28.8 us -> 29.9 us  [call(): pl.pallas_call(kernel, out_shape=out_shape, scratch_shapes=list(scratch),...]
    ppermute x1, starting transfers between devices: 1.59 us -> 0.58 us  [relay_total(): lax.ppermute(moving, 'relay', [(i, (i + 1) % size) for i in range(size)])]
    ppermute x4, starting transfers between devices: 9.83 us -> 10.7 us  [shifted(): return lax.ppermute(value, axis, pairs)]
  transfers between devices with their start and end apart: 8 -> 8, of which waited for: 3 -> 1; matrix products, arithmetic and copies ran while one was open for 0% -> 0% of each run, Pallas kernels for 28% -> 35%
where the time goes in v3:
time: 78.6 us; the launch traced here: 78.2 us
  Pallas kernels  33.1 us (42%)
  starting transfers between devices  22 us (28%)
  blocking collectives  16.2 us (21%)
  waiting for transfers between devices  5.7 us (7%)
  local copies, waits for them, and re-layouts  0.88 us (1%)
    pallas_call x7, Pallas kernels, call(): pl.pallas_call(kernel, out_shape=out_shape, scratch_shapes=list(scratch),...  29.9 us
    all_to_all x1, blocking collectives, shards(): lax.all_to_all(leaving, 'brick', split_axis=0, concat_axis=0, tiled=True)  16.2 us
    ppermute x4, starting transfers between devices, shifted(): return lax.ppermute(value, axis, pairs)  10.7 us
    all_to_all x1, starting transfers between devices, shards(): got = lax.all_to_all(sent, 'brick', split_axis=0, concat_axis=0, tiled=True)  7.5 us
    ppermute x2, waiting for transfers between devices, relay_blocks(): return [value, lax.ppermute(value, 'relay', [(0, 1), (1, 0)])]  5.68 us
    pallas_call x2, Pallas kernels, call_at(): pl.pallas_call(kernel, out_shape=out_shape, grid_spec=pltpu.PrefetchScala...  3.2 us
    ppermute x2, starting transfers between devices, relay_blocks(): return [value, lax.ppermute(value, 'relay', [(0, 1), (1, 0)])]  3.17 us
  transfers between devices with their start and end apart: 8, of which 1 were waited for; matrix products, arithmetic and copies ran while one was open for 0% of the time, Pallas kernels for 35%

profile of v3, /device:TPU:0, one launch (start us, length us, event | category | flops | bytes accessed | tf_op | source)
XLA Modules:
  0.0 78.2 jit_solution(15943559060514581314)
XLA Ops:
  0.0 2.8 %pack.1 = s32[128,384]{1,0:T(8,128)} custom-call(s32[1,64]{1,0:T(1,128)} %bitcast.19, f32[3,64]{1,0:T(4,128)} %angle_ref.1, s32[64,128]{1,0:T(8,128)} %cell_in.1, bf16[64,128]{1,0:T(8,128)(2,1)} %weight_in.1, f32[3,64,128]{2,1,0:T(8,128)} %arm_in.1), custom_call_target="tpu_custom_call" | custom-call | bytes 164864 | tf_op jit(solution)/shard_map/pack/pallas_call | solution.py:352
  2.8 0.0 copy-start
  2.8 7.5 %all-to-all-start = ((s32[16,8,384]{2,1,0:T(8,128)}), s32[16,8,384]{2,1,0:T(8,128)S(1)}, u32[]{:S(2)}, u32[]{:S(2)}) async-start(s32[16,8,384]{2,1,0:T(8,128)} %bitcast.21), calls=%async_computation | async-start | bytes 393216 | tf_op jit(solution)/shard_map/all_to_all | solution.py:482
  10.3 1.6 %collective-permute-start = (f32[4,8,1536]{2,1,0:T(8,128)S(1)}, f32[4,8,1536]{2,1,0:T(8,128)S(1)}, u32[]{:S(2)}, u32[]{:S(2)}) collective-permute-start(f32[4,8,1536]{2,1,0:T(8,128)S(1)} %copy-done), channel_id=1, source_target_pairs={{0,1},{1,0},{2,3},{3,2},{4,5},{5,4},{6,7},{7,6},{8,9},{9,8},{10,11... | collective-permute-start | bytes 589832 | tf_op jit(solution)/shard_map/ppermute | solution.py:404
  11.9 5.7 %collective-permute-done = f32[4,8,1536]{2,1,0:T(8,128)S(1)} collective-permute-done((f32[4,8,1536]{2,1,0:T(8,128)S(1)}, f32[4,8,1536]{2,1,0:T(8,128)S(1)}, u32[]{:S(2)}, u32[]{:S(2)}) %collective-permute-start) | collective-permute-done | bytes 196640 | tf_op jit(solution)/shard_map/ppermute | solution.py:404
  17.7 0.1 reshape.26
  17.8 0.1 reshape.25
  17.9 1.6 %collective-permute-start.1 = (f32[32,1536]{1,0:T(8,128)S(1)}, f32[32,1536]{1,0:T(8,128)S(1)}, u32[]{:S(2)}, u32[]{:S(2)}) collective-permute-start(f32[32,1536]{1,0:T(8,128)S(1)} %reshape.25), channel_id=1, source_target_pairs={{0,2},{2,4},{4,6},{6,8},{8,10},{10,12},{12,14},{14,16},{16,18},{18... | collective-permute-start | bytes 589832 | tf_op jit(solution)/shard_map/ppermute | solution.py:398
  19.5 1.3 %collective-permute-start.2 = (f32[32,1536]{1,0:T(8,128)S(1)}, f32[32,1536]{1,0:T(8,128)S(1)}, u32[]{:S(2)}, u32[]{:S(2)}) collective-permute-start(f32[32,1536]{1,0:T(8,128)S(1)} %reshape.26), channel_id=1, source_target_pairs={{2,0},{4,2},{6,4},{8,6},{10,8},{12,10},{14,12},{16,14},{18,16},{20... | collective-permute-start | bytes 589832 | tf_op jit(solution)/shard_map/ppermute | solution.py:398
  20.8 0.0 all-to-all-done
  20.8 0.0 copy-start.2
  20.8 4.0 %splat.1 = f32[32,1536]{1,0:T(8,128)S(1)} custom-call(s32[128,384]{1,0:T(8,128)S(1)} %bitcast.13), custom_call_target="tpu_custom_call" | custom-call | flops 1610612736 | bytes 196608 | tf_op jit(solution)/shard_map/splat/pallas_call | solution.py:352
  24.8 0.0 collective-permute-done.1.refs_2_
  24.8 0.0 collective-permute-done.2.refs_3_
  24.8 1.6 %collective-permute-start.3 = (f32[32,1536]{1,0:T(8,128)S(1)}, f32[32,1536]{1,0:T(8,128)S(1)}, u32[]{:S(2)}, u32[]{:S(2)}) collective-permute-start(f32[32,1536]{1,0:T(8,128)S(1)} %splat.1), channel_id=1, source_target_pairs={{0,1},{1,0},{2,3},{3,2},{4,5},{5,4},{6,7},{7,6},{8,9},{9,8},{10,11... | collective-permute-start | bytes 589832 | tf_op jit(solution)/shard_map/ppermute | solution.py:404
  26.4 1.6 %target_fields.1.field_ref = bf16[576,512]{1,0:T(8,128)(2,1)S(1)} custom-call(s32[1]{0:T(128)} %bitcast.3._, bf16[6,96,384]{2,1,0:T(8,128)(2,1)S(1)} %copy-done.2, f32[32,1536]{1,0:T(8,128)S(1)} %bitcast.10, f32[32,1536]{1,0:T(8,128)S(1)} %bitcast.12, f32[32,1536]{1,0:T(8,128)S(1)} %collective-permute-done.1.refs_2_, ...), custom_call_target="tpu_custom_call" | custom-call | flops 113246208 | bytes 786432 | tf_op jit(solution)/shard_map/target_fields/pallas_call | solution.py:370
  28.0 5.5 %target_sample_a.1.first_ref = f32[64,128]{1,0:T(8,128)S(1)} custom-call(s32[128,384]{1,0:T(8,128)S(1)} %bitcast.14, bf16[576,512]{1,0:T(8,128)(2,1)S(1)} %target_fields.1.field_ref), custom_call_target="tpu_custom_call" | custom-call | flops 4831838208 | bytes 1376256 | tf_op jit(solution)/shard_map/target_sample_a/pallas_call | solution.py:352
  33.5 0.0 collective-permute-done.3
  33.6 0.0 copy-start.1
  33.6 1.4 %collective-permute-start.5 = (f32[64,1536]{1,0:T(8,128)S(1)}, f32[64,1536]{1,0:T(8,128)S(1)}, u32[]{:S(2)}, u32[]{:S(2)}) collective-permute-start(f32[64,1536]{1,0:T(8,128)S(1)} %pad_maximum_fusion.refs_0_), channel_id=1, source_target_pairs={{2,0},{4,2},{6,4},{8,6},{10,8},{12,10},{14,12},{16,14},{18,16},{20... | collective-permute-start | bytes 1179656 | tf_op jit(solution)/shard_map/ppermute | solution.py:398
  35.0 6.5 %collective-permute-start.4 = (f32[64,1536]{1,0:T(8,128)S(1)}, f32[64,1536]{1,0:T(8,128)S(1)}, u32[]{:S(2)}, u32[]{:S(2)}) collective-permute-start(f32[64,1536]{1,0:T(8,128)S(1)} %pad_maximum_fusion.refs_0_), channel_id=1, source_target_pairs={{0,2},{2,4},{4,6},{6,8},{8,10},{10,12},{12,14},{14,16},{16,18},{18... | collective-permute-start | bytes 1179656 | tf_op jit(solution)/shard_map/ppermute | solution.py:398
  41.5 5.5 %target_sample_b.1.second_ref = f32[64,128]{1,0:T(8,128)S(1)} custom-call(s32[128,384]{1,0:T(8,128)S(1)} %bitcast.15, bf16[576,512]{1,0:T(8,128)(2,1)S(1)} %target_fields.1.field_ref), custom_call_target="tpu_custom_call" | custom-call | flops 4831838208 | bytes 1376256 | tf_op jit(solution)/shard_map/target_sample_b/pallas_call | solution.py:352
  47.0 0.0 collective-permute-done.5.refs_2_
  47.1 0.0 collective-permute-done.4.refs_1_
  47.1 1.6 %model_fields.1 = (bf16[576,512]{1,0:T(8,128)(2,1)S(1)}, f32[8,128]{1,0:T(8,128)S(1)}) custom-call(s32[1]{0:T(128)} %bitcast.3._, bf16[6,128,576]{2,1,0:T(8,128)(2,1)S(1)} %copy-done.1, f32[32,1536]{1,0:T(8,128)S(1)} %bitcast.11, f32[64,1536]{1,0:T(8,128)S(1)} %pad_maximum_fusion.refs_0_, f32[64,1536]{1,0:T(8,128)S(1)} %collective-permute-done.4.refs_1_, ...), custom_call_target="tpu_custom_call" | custom-call | bytes 1376256 | tf_op jit(solution)/shard_map/model_fields/pallas_call | solution.py:370
  48.7 0.6 collective-permute-start.6
  49.3 11.0 %model_sample.1.model_ref = f32[128,128]{1,0:T(8,128)S(1)} custom-call(s32[128,384]{1,0:T(8,128)S(1)} %bitcast.16, bf16[576,512]{1,0:T(8,128)(2,1)S(1)} %get-tuple-element.27.field_ref), custom_call_target="tpu_custom_call" | custom-call | flops 9663676416 | bytes 1376256 | tf_op jit(solution)/shard_map/model_sample/pallas_call | solution.py:352
  60.3 0.0 collective-permute-done.6
  60.3 0.2 join.1
  60.5 16.2 %all_to_all.22 = f32[16,1,128]{2,1,0:T(1,128)S(1)} all-to-all(f32[16,1,128]{2,1,0:T(1,128)S(1)} %bitcast.17), channel_id=1, replica_groups=mesh['brick'=16,'relay'=2] {'brick'}, dimensions={0} | all-to-all | bytes 16384 | tf_op jit(solution)/shard_map/all_to_all | solution.py:537
  76.7 0.7 copy-done.3
  77.4 0.9 %finish.1 = f32[6,64]{1,0:T(8,128)} custom-call(s32[1,64]{1,0:T(1,128)S(1)} %bitcast.20, f32[16,128]{1,0:T(8,128)S(1)} %bitcast.18), custom_call_target="tpu_custom_call" | custom-call | bytes 8448 | tf_op jit(solution)/shard_map/finish/pallas_call | solution.py:352
  (10 shorter events, 0.2 us)
Async XLA Ops:
  2.8 7.5 %copy-start = (f32[4,8,1536]{2,1,0:T(8,128)S(1)}, f32[4,8,1536]{2,1,0:T(8,128)}, u32[]{:S(2)}) copy-start(f32[4,8,1536]{2,1,0:T(8,128)} %param.8) | copy-start | bytes 589828
  2.8 18.0 %all-to-all-start = ((s32[16,8,384]{2,1,0:T(8,128)}), s32[16,8,384]{2,1,0:T(8,128)S(1)}, u32[]{:S(2)}, u32[]{:S(2)}) async-start(s32[16,8,384]{2,1,0:T(8,128)} %bitcast.21), calls=%async_computation | async-start | bytes 393216 | tf_op jit(solution)/shard_map/all_to_all | solution.py:482
  10.3 7.3 %collective-permute-start = (f32[4,8,1536]{2,1,0:T(8,128)S(1)}, f32[4,8,1536]{2,1,0:T(8,128)S(1)}, u32[]{:S(2)}, u32[]{:S(2)}) collective-permute-start(f32[4,8,1536]{2,1,0:T(8,128)S(1)} %copy-done), channel_id=1, source_target_pairs={{0,1},{1,0},{2,3},{3,2},{4,5},{5,4},{6,7},{7,6},{8,9},{9,8},{10,11... | collective-permute-start | bytes 589832 | tf_op jit(solution)/shard_map/ppermute | solution.py:404
  17.9 6.9 %collective-permute-start.1 = (f32[32,1536]{1,0:T(8,128)S(1)}, f32[32,1536]{1,0:T(8,128)S(1)}, u32[]{:S(2)}, u32[]{:S(2)}) collective-permute-start(f32[32,1536]{1,0:T(8,128)S(1)} %reshape.25), channel_id=1, source_target_pairs={{0,2},{2,4},{4,6},{6,8},{8,10},{10,12},{12,14},{14,16},{16,18},{18... | collective-permute-start | bytes 589832 | tf_op jit(solution)/shard_map/ppermute | solution.py:398
  19.5 5.3 %collective-permute-start.2 = (f32[32,1536]{1,0:T(8,128)S(1)}, f32[32,1536]{1,0:T(8,128)S(1)}, u32[]{:S(2)}, u32[]{:S(2)}) collective-permute-start(f32[32,1536]{1,0:T(8,128)S(1)} %reshape.26), channel_id=1, source_target_pairs={{2,0},{4,2},{6,4},{8,6},{10,8},{12,10},{14,12},{16,14},{18,16},{20... | collective-permute-start | bytes 589832 | tf_op jit(solution)/shard_map/ppermute | solution.py:398
  20.8 5.6 %copy-start.2 = (bf16[6,96,384]{2,1,0:T(8,128)(2,1)S(1)}, bf16[6,96,384]{2,1,0:T(8,128)(2,1)}, u32[]{:S(2)}) copy-start(bf16[6,96,384]{2,1,0:T(8,128)(2,1)} %constant.26.clone.table_ref) | copy-start | bytes 1327108
  24.8 8.7 %collective-permute-start.3 = (f32[32,1536]{1,0:T(8,128)S(1)}, f32[32,1536]{1,0:T(8,128)S(1)}, u32[]{:S(2)}, u32[]{:S(2)}) collective-permute-start(f32[32,1536]{1,0:T(8,128)S(1)} %splat.1), channel_id=1, source_target_pairs={{0,1},{1,0},{2,3},{3,2},{4,5},{5,4},{6,7},{7,6},{8,9},{9,8},{10,11... | collective-permute-start | bytes 589832 | tf_op jit(solution)/shard_map/ppermute | solution.py:404
  33.6 13.5 %copy-start.1 = (bf16[6,128,576]{2,1,0:T(8,128)(2,1)S(1)}, bf16[6,128,576]{2,1,0:T(8,128)(2,1)}, u32[]{:S(2)}) copy-start(bf16[6,128,576]{2,1,0:T(8,128)(2,1)} %constant.27.clone.table_ref) | copy-start | bytes 2654212
  33.6 13.5 %collective-permute-start.5 = (f32[64,1536]{1,0:T(8,128)S(1)}, f32[64,1536]{1,0:T(8,128)S(1)}, u32[]{:S(2)}, u32[]{:S(2)}) collective-permute-start(f32[64,1536]{1,0:T(8,128)S(1)} %pad_maximum_fusion.refs_0_), channel_id=1, source_target_pairs={{2,0},{4,2},{6,4},{8,6},{10,8},{12,10},{14,12},{16,14},{18,16},{20... | collective-permute-start | bytes 1179656 | tf_op jit(solution)/shard_map/ppermute | solution.py:398
  35.0 12.0 %collective-permute-start.4 = (f32[64,1536]{1,0:T(8,128)S(1)}, f32[64,1536]{1,0:T(8,128)S(1)}, u32[]{:S(2)}, u32[]{:S(2)}) collective-permute-start(f32[64,1536]{1,0:T(8,128)S(1)} %pad_maximum_fusion.refs_0_), channel_id=1, source_target_pairs={{0,2},{2,4},{4,6},{6,8},{8,10},{10,12},{12,14},{14,16},{16,18},{18... | collective-permute-start | bytes 1179656 | tf_op jit(solution)/shard_map/ppermute | solution.py:398
  48.7 11.6 %collective-permute-start.6 = (f32[8,128]{1,0:T(8,128)S(1)}, f32[8,128]{1,0:T(8,128)S(1)}, u32[]{:S(2)}, u32[]{:S(2)}) collective-permute-start(f32[8,128]{1,0:T(8,128)S(1)} %get-tuple-element.28), channel_id=1, source_target_pairs={{0,1},{1,0},{2,3},{3,2},{4,5},{5,4},{6,7},{7,6},{8,9},{9,8},{10,11... | collective-permute-start | bytes 12296 | tf_op jit(solution)/shard_map/ppermute | solution.py:424
  76.7 0.7 copy-start.3

commit v4 on v3

--- a/solution.py
+++ b/solution.py
@@ -17,6 +17,9 @@
 WEIGHT_SCALE = 512.0
 LEVER_SCALE = 32768.0
 LEVER_BIAS = 1 << 20
+CODE_TOP = 65535
+SCALE_UNIT = 512.0
+SCALE_LANES = 128
 VMEM_BYTES = 48 << 20
 PACK_VMEM_BYTES = 60 << 20
 F32 = jnp.float32
@@ -99,18 +102,17 @@
     return jnp.sum(jnp.where(earlier, 1, 0), axis=0, keepdims=True), eye
 
 
-def pack_kernel(
-    most, lines, row_count, brick_ref, angle_ref, cell_in, weight_in, arm_in, out_ref,
-    cell_ref, weight_ref, arm_ref, sems,
-):
+def pack_kernel(most, lines, row_count, *refs):
+    inputs, (out_ref, place_ref), held, sems = refs[:5], refs[5:7], refs[7:12], refs[12]
     copies = [
         pltpu.make_async_copy(source, target, sems.at[k])
-        for k, (source, target) in enumerate(
-            [(cell_in, cell_ref), (weight_in, weight_ref), (arm_in, arm_ref)]
-        )
+        for k, (source, target) in enumerate(zip(inputs, held))
     ]
     for copy in copies:
         copy.start()
+    brick_ref, angle_ref, cell_ref, weight_ref, arm_ref = held
+    for copy in copies[:2]:
+        copy.wait()
     frags, beads = cell_ref.shape
     slots = out_ref.shape[0]
     row = brick_ref[...]
@@ -128,7 +130,9 @@
         [-sin_b, cos_b * sin_c, cos_b * cos_c],
     ]
     turn = [[eye_column(value, eye) for value in values] for values in turn]
-    for copy in copies:
+    place_ref[0:1, :] = row
+    place_ref[1:2, :] = rank
+    for copy in copies[2:]:
         copy.wait()
     levers = []
     for i in range(3):
@@ -166,7 +170,32 @@
     return total
 
 
-def splat_kernel(lines, rb, got_ref, out_ref, acc_ref):
+def encode(value, out_ref):
+    half, length = value.shape[0] // 2, value.shape[1]
+    top = (jnp.max(value) * SCALE_UNIT).astype(I32) + 1
+    scale = (SCALE_UNIT * CODE_TOP) / top.astype(F32)
+    code = jnp.minimum((value * scale + 0.5).astype(I32), CODE_TOP)
+    out_ref[:, :length] = code[:half] | (code[half:] << 16)
+    out_ref[:, length:] = jnp.full((half, SCALE_LANES), top, I32)
+
+
+def decode(words, count):
+    half, length = words.shape[0] // count, words.shape[1] - SCALE_LANES
+    step = words[:, length : length + 1].astype(F32) * (1.0 / (SCALE_UNIT * CODE_TOP))
+    low = (words[:, :length] & CODE_TOP).astype(F32) * step
+    high = ((words[:, :length] >> 16) & CODE_TOP).astype(F32) * step
+    lines = []
+    for k in range(count):
+        rows = slice(k * half, (k + 1) * half)
+        lines += [low[rows], high[rows]]
+    return lines
+
+
+def encode_kernel(value_ref, out_ref):
+    encode(value_ref[...], out_ref)
+
+
+def splat_kernel(lines, rb, got_ref, out_ref, code_ref, acc_ref):
     slots = got_ref.shape[0]
     beads = got_ref.shape[1] // 3
     his = acc_ref.shape[0]
@@ -193,7 +222,9 @@
 
     lax.fori_loop(0, slots // rb, body, 0)
     density = [acc_ref[yh * lines : (yh + 1) * lines, :] for yh in range(his // lines)]
-    out_ref[...] = line_blur(jnp.concatenate(density, axis=1), False)
+    smooth = line_blur(jnp.concatenate(density, axis=1), False)
+    out_ref[...] = smooth
+    encode(smooth, code_ref)
 
 
 def split(value):
@@ -220,18 +251,27 @@
             out_ref[rows, LO : 2 * LO] = low
 
 
-def target_kernel(lines, count, _, table_ref, *refs):
-    parts, out_ref = refs[:count], refs[count]
-    mixed = mix_lines(table_ref, [ref[...] for ref in parts])
+def window_lines(own_ref, near_refs, left_ref, right_ref):
+    lines = [own_ref[...]]
+    for ref in near_refs:
+        lines += decode(ref[...], 1)
+    for ref in (left_ref, right_ref):
+        lines += decode(ref[...], len(near_refs) + 1)
+    return lines
+
+
+def target_kernel(lines, _, table_ref, own_ref, *refs):
+    *near_refs, left_ref, right_ref, out_ref = refs
+    mixed = mix_lines(table_ref, window_lines(own_ref, near_refs, left_ref, right_ref))
     grad_x = line_blur(mixed[0:lines], False)
     grad_y = line_blur(mixed[lines : 2 * lines], True)
     grad_z = line_blur(mixed[2 * lines : 3 * lines], False)
     store_fields([grad_x, grad_y, grad_z], lines, out_ref)
 
 
-def model_kernel(lines, count, _, table_ref, target_ref, *refs):
-    parts, out_ref, sum_ref = refs[:count], refs[count], refs[count + 1]
-    smooth = mix_lines(table_ref, [ref[...] for ref in parts])
+def model_kernel(lines, _, table_ref, target_ref, own_ref, *refs):
+    *near_refs, left_ref, right_ref, out_ref, sum_ref = refs
+    smooth = mix_lines(table_ref, window_lines(own_ref, near_refs, left_ref, right_ref))
     model = smooth[3 * lines :]
     target = target_ref[...]
     sums = [jnp.sum(model * target), jnp.sum(model * model), jnp.sum(target * target)]
@@ -318,11 +358,10 @@
     out_ref[...] = total
 
 
-def finish_kernel(most, voxel_total, brick_ref, back_ref, out_ref):
+def finish_kernel(most, voxel_total, place_ref, back_ref, out_ref):
     frags = out_ref.shape[1]
     bricks = back_ref.shape[0]
-    row = brick_ref[...]
-    rank, _ = slot_row(row, most)
+    row, rank = place_ref[0:1, :], place_ref[1:2, :]
     place = jnp.where(lax.broadcasted_iota(I32, (bricks, frags), 0) == row, 1.0, 0.0).astype(F32)
     back = back_ref[...]
     sums = jnp.sum(back, axis=0, keepdims=True)
@@ -457,42 +496,43 @@
     model_index = (looked_up(mz, r) * mn + looked_up(mx, b)).reshape(1)
 
     target_lines = target.reshape(lines, rows)
-    target_blocks = relay_blocks(target, reach_one)
-    left_edge = jnp.concatenate([t[:, columns - KR :] for t in target_blocks], axis=0)
-    right_edge = jnp.concatenate([t[:, :KR] for t in target_blocks], axis=0)
-    from_left = shifted(left_edge.reshape(-1, rows), "brick", 1)
-    from_right = shifted(right_edge.reshape(-1, rows), "brick", -1)
-
-    brick_row = frag_brick.reshape(1, frags)
-    vmem, hbm = pl.BlockSpec(memory_space=pltpu.VMEM), pl.BlockSpec(memory_space=pltpu.HBM)
-    sent = call(
+    words = jax.ShapeDtypeStruct((lines // 2, rows + SCALE_LANES), I32)
+    target_blocks = relay_blocks(call(encode_kernel, words, target_lines, name="encode"), reach_one)
+    by_column = [t.reshape(-1, columns, rows + SCALE_LANES) for t in target_blocks]
+    left_edge = jnp.concatenate([t[:, columns - KR :] for t in by_column], axis=0)
+    right_edge = jnp.concatenate([t[:, :KR] for t in by_column], axis=0)
+    from_left = shifted(left_edge.reshape(-1, rows + SCALE_LANES), "brick", 1)
+    from_right = shifted(right_edge.reshape(-1, rows + SCALE_LANES), "brick", -1)
+
+    hbm = pl.BlockSpec(memory_space=pltpu.HBM)
+    packed = [frag_brick.reshape(1, frags), frag_angle, bead_cell, bead_weight, bead_arm]
+    sent, place = call(
         functools.partial(pack_kernel, most, lines, rows),
-        jax.ShapeDtypeStruct((slots, 3 * beads), I32),
-        brick_row, frag_angle, bead_cell, bead_weight, bead_arm,
-        in_specs=[vmem, vmem, hbm, hbm, hbm],
-        scratch=[
-            pltpu.VMEM(bead_cell.shape, I32),
-            pltpu.VMEM(bead_weight.shape, BF16),
-            pltpu.VMEM(bead_arm.shape, F32),
-            pltpu.SemaphoreType.DMA((3,)),
+        [
+            jax.ShapeDtypeStruct((slots, 3 * beads), I32),
+            jax.ShapeDtypeStruct((8, frags), I32),
         ],
+        *packed,
+        in_specs=[hbm] * len(packed),
+        scratch=[pltpu.VMEM(a.shape, a.dtype) for a in packed]
+        + [pltpu.SemaphoreType.DMA((len(packed),))],
         name="pack",
         vmem=PACK_VMEM_BYTES,
     )
     got = lax.all_to_all(sent, "brick", split_axis=0, concat_axis=0, tiled=True)
-    smooth = call(
+    smooth, coded = call(
         functools.partial(splat_kernel, lines, min(32, slots)),
-        jax.ShapeDtypeStruct((lines, rows), F32),
+        [jax.ShapeDtypeStruct((lines, rows), F32), words],
         got,
         scratch=[pltpu.VMEM((his, LO), F32)],
         name="splat",
         macs=slots * beads * his * LO,
     )
-    smooth, from_left, from_right = lax.optimization_barrier((smooth, from_left, from_right))
-    target_parts = [t.reshape(lines, rows) for t in target_blocks] + [from_left, from_right]
-    blocks = jnp.concatenate(relay_blocks(smooth, reach_two), axis=0)
+    coded, from_left, from_right = lax.optimization_barrier((coded, from_left, from_right))
+    target_parts = [target_lines] + target_blocks[1:] + [from_left, from_right]
+    blocks = relay_blocks(coded, reach_two)
     target_field = call_at(
-        functools.partial(target_kernel, lines, len(target_parts)),
+        functools.partial(target_kernel, lines),
         jax.ShapeDtypeStruct((3 * his, 2 * LO), BF16),
         target_index, jnp.asarray(target_table), *target_parts,
         name="target_fields",
@@ -514,11 +554,13 @@
     blocks, target_first, target_field = lax.optimization_barrier(
         (blocks, target_first, target_field)
     )
-    model_parts = [blocks, shifted(blocks, "brick", 1), shifted(blocks, "brick", -1)]
+    beside = jnp.concatenate(blocks, axis=0)
+    model_parts = [smooth] + blocks[1:]
+    model_parts += [shifted(beside, "brick", 1), shifted(beside, "brick", -1)]
     target_second = sample(target_field, half, slots - half, "target_sample_b")
     target_second, *model_parts = lax.optimization_barrier((target_second, *model_parts))
     model_field, partial = call_at(
-        functools.partial(model_kernel, lines, len(model_parts)),
+        functools.partial(model_kernel, lines),
         [
             jax.ShapeDtypeStruct((3 * his, 2 * LO), BF16),
             jax.ShapeDtypeStruct((8, 128), F32),
@@ -538,7 +580,7 @@
     return call(
         functools.partial(finish_kernel, most, voxel_total),
         jax.ShapeDtypeStruct((6, frags), F32),
-        brick_row, back,
+        place, back,
         name="finish",
     )
 

time: 78.6 us -> 69.6 us (0.89)
  blocking collectives: 16.2 us -> 9.99 us
  starting transfers between devices: 22 us -> 19.4 us
    all_to_all x1, blocking collectives: 16.2 us -> 9.99 us  [shards(): lax.all_to_all(leaving, 'brick', split_axis=0, concat_axis=0, tiled=True)]
    ppermute x2, waiting for transfers between devices: 5.68 us -> 0.01 us  [relay_blocks(): return [value, lax.ppermute(value, 'relay', [(0, 1), (1, 0)])]]
    all_to_all x1, waiting for transfers between devices: 0.01 us -> 5.16 us  [shards(): got = lax.all_to_all(sent, 'brick', split_axis=0, concat_axis=0, tiled=True)]
    ppermute x4, starting transfers between devices: 10.7 us -> 8.25 us  [shifted(): return lax.ppermute(value, axis, pairs)]
    all_to_all x1, starting transfers between devices: 7.5 us -> 5.92 us  [shards(): got = lax.all_to_all(sent, 'brick', split_axis=0, concat_axis=0, tiled=True)]
    ppermute x1, starting transfers between devices: 0.58 us -> 1.6 us  [relay_total(): lax.ppermute(moving, 'relay', [(i, (i + 1) % size) for i in range(size)])]
    pallas_call x7 -> x8, Pallas kernels: 29.9 us -> 29.9 us  [call(): pl.pallas_call(kernel, out_shape=out_shape, scratch_shapes=list(scratch),...]
  transfers between devices with their start and end apart: 8 -> 8, of which waited for: 1 -> 1; matrix products, arithmetic and copies ran while one was open for 0% -> 0% of each run, Pallas kernels for 35% -> 44%
where the time goes in v4:
time: 69.6 us; the launch traced here: 69.2 us
  Pallas kernels  33.3 us (48%)
  starting transfers between devices  19.4 us (28%)
  blocking collectives  9.99 us (14%)
  waiting for transfers between devices  5.18 us (7%)
  local copies, waits for them, and re-layouts  1.08 us (2%)
    pallas_call x8, Pallas kernels, call(): pl.pallas_call(kernel, out_shape=out_shape, scratch_shapes=list(scratch),...  29.9 us
    all_to_all x1, blocking collectives, shards(): lax.all_to_all(leaving, 'brick', split_axis=0, concat_axis=0, tiled=True)  9.99 us
    ppermute x4, starting transfers between devices, shifted(): return lax.ppermute(value, axis, pairs)  8.25 us
    all_to_all x1, starting transfers between devices, shards(): got = lax.all_to_all(sent, 'brick', split_axis=0, concat_axis=0, tiled=True)  5.92 us
    all_to_all x1, waiting for transfers between devices, shards(): got = lax.all_to_all(sent, 'brick', split_axis=0, concat_axis=0, tiled=True)  5.16 us
    ppermute x2, starting transfers between devices, relay_blocks(): return [value, lax.ppermute(value, 'relay', [(0, 1), (1, 0)])]  3.59 us
    pallas_call x2, Pallas kernels, call_at(): pl.pallas_call(kernel, out_shape=out_shape, grid_spec=pltpu.PrefetchScala...  3.42 us
    ppermute x1, starting transfers between devices, relay_total(): lax.ppermute(moving, 'relay', [(i, (i + 1) % size) for i in range(size)])  1.6 us
  transfers between devices with their start and end apart: 8, of which 1 were waited for; matrix products, arithmetic and copies ran while one was open for 0% of the time, Pallas kernels for 44%

profile of v4, /device:TPU:0, one launch (start us, length us, event | category | flops | bytes accessed | tf_op | source)
XLA Modules:
  0.0 69.2 jit_solution(5403699321171549503)
XLA Ops:
  0.0 0.9 %copy-done = f32[4,8,1536]{2,1,0:T(8,128)S(1)} copy-done((f32[4,8,1536]{2,1,0:T(8,128)S(1)}, f32[4,8,1536]{2,1,0:T(8,128)}, u32[]{:S(2)}) %copy-start) | copy-done | bytes 196632
  0.9 0.2 encode.1
  1.2 3.0 %collective-permute-start = (s32[16,1664]{1,0:T(8,128)S(1)}, s32[16,1664]{1,0:T(8,128)S(1)}, u32[]{:S(2)}, u32[]{:S(2)}) collective-permute-start(s32[16,1664]{1,0:T(8,128)S(1)} %encode.1), channel_id=1, source_target_pairs={{0,1},{1,0},{2,3},{3,2},{4,5},{5,4},{6,7},{7,6},{8,9},{9,8},{10,11... | collective-permute-start | bytes 319496 | tf_op jit(solution)/shard_map/ppermute | solution.py:443
  4.2 2.2 %pack.1 = (s32[128,384]{1,0:T(8,128)}, s32[8,64]{1,0:T(8,128)}) custom-call(s32[1,64]{1,0:T(1,128)} %bitcast.23, f32[3,64]{1,0:T(4,128)} %refs_1_.1, s32[64,128]{1,0:T(8,128)} %refs_2_.1, bf16[64,128]{1,0:T(8,128)(2,1)} %refs_3_.1, f32[3,64,128]{2,1,0:T(8,128)} %refs_4_.1), custom_call_target="tpu_custom_call" | custom-call | bytes 164864 | tf_op jit(solution)/shard_map/pack/pallas_call | solution.py:391
  6.4 5.9 %all-to-all-start = ((s32[16,8,384]{2,1,0:T(8,128)}), s32[16,8,384]{2,1,0:T(8,128)S(1)}, u32[]{:S(2)}, u32[]{:S(2)}) async-start(s32[16,8,384]{2,1,0:T(8,128)} %bitcast.22), calls=%async_computation | async-start | bytes 393216 | tf_op jit(solution)/shard_map/all_to_all | solution.py:522
  12.3 0.0 collective-permute-done.refs_0_
  12.5 2.3 %collective-permute-start.1 = (s32[16,1664]{1,0:T(8,128)S(1)}, s32[16,1664]{1,0:T(8,128)S(1)}, u32[]{:S(2)}, u32[]{:S(2)}) collective-permute-start(s32[16,1664]{1,0:T(8,128)S(1)} %reshape.30), channel_id=1, source_target_pairs={{0,2},{2,4},{4,6},{6,8},{8,10},{10,12},{12,14},{14,16},{16,18},{18... | collective-permute-start | bytes 319496 | tf_op jit(solution)/shard_map/ppermute | solution.py:437
  14.8 1.3 %collective-permute-start.2 = (s32[16,1664]{1,0:T(8,128)S(1)}, s32[16,1664]{1,0:T(8,128)S(1)}, u32[]{:S(2)}, u32[]{:S(2)}) collective-permute-start(s32[16,1664]{1,0:T(8,128)S(1)} %reshape.31), channel_id=1, source_target_pairs={{2,0},{4,2},{6,4},{8,6},{10,8},{12,10},{14,12},{16,14},{18,16},{20... | collective-permute-start | bytes 319496 | tf_op jit(solution)/shard_map/ppermute | solution.py:437
  16.1 5.2 %all-to-all-done = s32[16,8,384]{2,1,0:T(8,128)S(1)} async-done(((s32[16,8,384]{2,1,0:T(8,128)}), s32[16,8,384]{2,1,0:T(8,128)S(1)}, u32[]{:S(2)}, u32[]{:S(2)}) %all-to-all-start) | async-done | bytes 196640 | tf_op jit(solution)/shard_map/all_to_all | solution.py:522
  21.3 4.2 %splat.1 = (f32[32,1536]{1,0:T(8,128)S(1)}, s32[16,1664]{1,0:T(8,128)S(1)}) custom-call(s32[128,384]{1,0:T(8,128)S(1)} %bitcast.16), custom_call_target="tpu_custom_call" | custom-call | flops 1610612736 | bytes 196608 | tf_op jit(solution)/shard_map/splat/pallas_call | solution.py:391
  25.5 0.0 collective-permute-done.1.refs_1_
  25.5 0.0 collective-permute-done.2.refs_2_
  25.5 0.6 collective-permute-start.3
  26.0 0.0 copy-done.1
  26.0 0.0 copy-done.3
  26.0 1.7 %target_fields.1.field_ref = bf16[576,512]{1,0:T(8,128)(2,1)S(1)} custom-call(s32[1]{0:T(128)} %bitcast.6._, bf16[6,96,384]{2,1,0:T(8,128)(2,1)S(1)} %copy-done.3, f32[32,1536]{1,0:T(8,128)S(1)} %bitcast.12, s32[16,1664]{1,0:T(8,128)S(1)} %collective-permute-done.refs_0_, s32[16,1664]{1,0:T(8,128)S(1)} %collective-permute-done.1.refs_1_, ...), custom_call_target="tpu_custom_call" | custom-call | flops 113246208 | bytes 516096 | tf_op jit(solution)/shard_map/target_fields/pallas_call | solution.py:409
  27.7 5.6 %target_sample_a.1.first_ref = f32[64,128]{1,0:T(8,128)S(1)} custom-call(s32[128,384]{1,0:T(8,128)S(1)} %bitcast.17, bf16[576,512]{1,0:T(8,128)(2,1)S(1)} %target_fields.1.field_ref), custom_call_target="tpu_custom_call" | custom-call | flops 4831838208 | bytes 1376256 | tf_op jit(solution)/shard_map/target_sample_a/pallas_call | solution.py:391
  33.3 0.0 collective-permute-done.3.refs_0_
  33.4 0.0 copy-start.2
  33.4 1.4 %collective-permute-start.5 = (s32[32,1664]{1,0:T(8,128)S(1)}, s32[32,1664]{1,0:T(8,128)S(1)}, u32[]{:S(2)}, u32[]{:S(2)}) collective-permute-start(s32[32,1664]{1,0:T(8,128)S(1)} %constant_dynamic-update-slice_fusion), channel_id=1, source_target_pairs={{2,0},{4,2},{6,4},{8,6},{10,8},{12,10},{14,12},{16,14},{18,16},{20... | collective-permute-start | bytes 638984 | tf_op jit(solution)/shard_map/ppermute | solution.py:437
  34.8 3.2 %collective-permute-start.4 = (s32[32,1664]{1,0:T(8,128)S(1)}, s32[32,1664]{1,0:T(8,128)S(1)}, u32[]{:S(2)}, u32[]{:S(2)}) collective-permute-start(s32[32,1664]{1,0:T(8,128)S(1)} %constant_dynamic-update-slice_fusion), channel_id=1, source_target_pairs={{0,2},{2,4},{4,6},{6,8},{8,10},{10,12},{12,14},{14,16},{16,18},{18... | collective-permute-start | bytes 638984 | tf_op jit(solution)/shard_map/ppermute | solution.py:437
  38.0 5.6 %target_sample_b.1.second_ref = f32[64,128]{1,0:T(8,128)S(1)} custom-call(s32[128,384]{1,0:T(8,128)S(1)} %bitcast.18, bf16[576,512]{1,0:T(8,128)(2,1)S(1)} %target_fields.1.field_ref), custom_call_target="tpu_custom_call" | custom-call | flops 4831838208 | bytes 1376256 | tf_op jit(solution)/shard_map/target_sample_b/pallas_call | solution.py:391
  43.6 0.0 collective-permute-done.5.refs_2_
  43.7 0.0 collective-permute-done.4.refs_1_
  43.7 0.0 copy-done.2
  43.7 1.8 %model_fields.1 = (bf16[576,512]{1,0:T(8,128)(2,1)S(1)}, f32[8,128]{1,0:T(8,128)S(1)}) custom-call(s32[1]{0:T(128)} %bitcast.6._, bf16[6,128,576]{2,1,0:T(8,128)(2,1)S(1)} %copy-done.2, f32[32,1536]{1,0:T(8,128)S(1)} %bitcast.13, f32[32,1536]{1,0:T(8,128)S(1)} %get-tuple-element.35.own_ref, s32[16,1664]{1,0:T(8,128)S(1)} %collective-permute-done.3.refs_0_, ...), custom_call_target="tpu_custom_call" | custom-call | bytes 925696 | tf_op jit(solution)/shard_map/model_fields/pallas_call | solution.py:409
  45.4 1.6 %collective-permute-start.6 = (f32[8,128]{1,0:T(8,128)S(1)}, f32[8,128]{1,0:T(8,128)S(1)}, u32[]{:S(2)}, u32[]{:S(2)}) collective-permute-start(f32[8,128]{1,0:T(8,128)S(1)} %get-tuple-element.40), channel_id=1, source_target_pairs={{0,1},{1,0},{2,3},{3,2},{4,5},{5,4},{6,7},{7,6},{8,9},{9,8},{10,11... | collective-permute-start | bytes 12296 | tf_op jit(solution)/shard_map/ppermute | solution.py:463
  47.0 11.1 %model_sample.1.model_ref = f32[128,128]{1,0:T(8,128)S(1)} custom-call(s32[128,384]{1,0:T(8,128)S(1)} %bitcast.19, bf16[576,512]{1,0:T(8,128)(2,1)S(1)} %get-tuple-element.39.field_ref), custom_call_target="tpu_custom_call" | custom-call | flops 9663676416 | bytes 1376256 | tf_op jit(solution)/shard_map/model_sample/pallas_call | solution.py:391
  58.2 0.0 collective-permute-done.6
  58.2 0.2 join.1
  58.4 10.0 %all_to_all.22 = f32[16,1,128]{2,1,0:T(1,128)S(1)} all-to-all(f32[16,1,128]{2,1,0:T(1,128)S(1)} %bitcast.20), channel_id=1, replica_groups=mesh['brick'=16,'relay'=2] {'brick'}, dimensions={0} | all-to-all | bytes 16384 | tf_op jit(solution)/shard_map/all_to_all | solution.py:579
  68.4 0.9 %finish.1 = f32[6,64]{1,0:T(8,128)} custom-call(s32[8,64]{1,0:T(8,128)S(1)} %copy-done.4, f32[16,128]{1,0:T(8,128)S(1)} %bitcast.21), custom_call_target="tpu_custom_call" | custom-call | bytes 10240 | tf_op jit(solution)/shard_map/finish/pallas_call | solution.py:391
  (14 shorter events, 0.2 us)
Async XLA Ops:
  0.0 0.9 %copy-start = (f32[4,8,1536]{2,1,0:T(8,128)S(1)}, f32[4,8,1536]{2,1,0:T(8,128)}, u32[]{:S(2)}) copy-start(f32[4,8,1536]{2,1,0:T(8,128)} %param.8) | copy-start | bytes 589828
  1.2 11.2 %collective-permute-start = (s32[16,1664]{1,0:T(8,128)S(1)}, s32[16,1664]{1,0:T(8,128)S(1)}, u32[]{:S(2)}, u32[]{:S(2)}) collective-permute-start(s32[16,1664]{1,0:T(8,128)S(1)} %encode.1), channel_id=1, source_target_pairs={{0,1},{1,0},{2,3},{3,2},{4,5},{5,4},{6,7},{7,6},{8,9},{9,8},{10,11... | collective-permute-start | bytes 319496 | tf_op jit(solution)/shard_map/ppermute | solution.py:443
  6.4 14.9 %all-to-all-start = ((s32[16,8,384]{2,1,0:T(8,128)}), s32[16,8,384]{2,1,0:T(8,128)S(1)}, u32[]{:S(2)}, u32[]{:S(2)}) async-start(s32[16,8,384]{2,1,0:T(8,128)} %bitcast.22), calls=%async_computation | async-start | bytes 393216 | tf_op jit(solution)/shard_map/all_to_all | solution.py:522
  12.5 13.0 %collective-permute-start.1 = (s32[16,1664]{1,0:T(8,128)S(1)}, s32[16,1664]{1,0:T(8,128)S(1)}, u32[]{:S(2)}, u32[]{:S(2)}) collective-permute-start(s32[16,1664]{1,0:T(8,128)S(1)} %reshape.30), channel_id=1, source_target_pairs={{0,2},{2,4},{4,6},{6,8},{8,10},{10,12},{12,14},{14,16},{16,18},{18... | collective-permute-start | bytes 319496 | tf_op jit(solution)/shard_map/ppermute | solution.py:437
  14.8 10.6 %collective-permute-start.2 = (s32[16,1664]{1,0:T(8,128)S(1)}, s32[16,1664]{1,0:T(8,128)S(1)}, u32[]{:S(2)}, u32[]{:S(2)}) collective-permute-start(s32[16,1664]{1,0:T(8,128)S(1)} %reshape.31), channel_id=1, source_target_pairs={{2,0},{4,2},{6,4},{8,6},{10,8},{12,10},{14,12},{16,14},{18,16},{20... | collective-permute-start | bytes 319496 | tf_op jit(solution)/shard_map/ppermute | solution.py:437
  21.3 4.8 %copy-start.1 = (f32[4,8,1536]{2,1,0:T(8,128)S(1)}, f32[4,8,1536]{2,1,0:T(8,128)}, u32[]{:S(2)}) copy-start(f32[4,8,1536]{2,1,0:T(8,128)} %param.8) | copy-start | bytes 589828
  21.3 4.8 %copy-start.3 = (bf16[6,96,384]{2,1,0:T(8,128)(2,1)S(1)}, bf16[6,96,384]{2,1,0:T(8,128)(2,1)}, u32[]{:S(2)}) copy-start(bf16[6,96,384]{2,1,0:T(8,128)(2,1)} %constant.26.clone.table_ref) | copy-start | bytes 1327108
  25.5 7.8 %collective-permute-start.3 = (s32[16,1664]{1,0:T(8,128)S(1)}, s32[16,1664]{1,0:T(8,128)S(1)}, u32[]{:S(2)}, u32[]{:S(2)}) collective-permute-start(s32[16,1664]{1,0:T(8,128)S(1)} %get-tuple-element.33), channel_id=1, source_target_pairs={{0,1},{1,0},{2,3},{3,2},{4,5},{5,4},{6,7},{7,6},{8,9},{9,8},{10,11... | collective-permute-start | bytes 319496 | tf_op jit(solution)/shard_map/ppermute | solution.py:443
  33.4 10.3 %copy-start.2 = (bf16[6,128,576]{2,1,0:T(8,128)(2,1)S(1)}, bf16[6,128,576]{2,1,0:T(8,128)(2,1)}, u32[]{:S(2)}) copy-start(bf16[6,128,576]{2,1,0:T(8,128)(2,1)} %constant.27.clone.table_ref) | copy-start | bytes 2654212
  33.4 10.3 %collective-permute-start.5 = (s32[32,1664]{1,0:T(8,128)S(1)}, s32[32,1664]{1,0:T(8,128)S(1)}, u32[]{:S(2)}, u32[]{:S(2)}) collective-permute-start(s32[32,1664]{1,0:T(8,128)S(1)} %constant_dynamic-update-slice_fusion), channel_id=1, source_target_pairs={{2,0},{4,2},{6,4},{8,6},{10,8},{12,10},{14,12},{16,14},{18,16},{20... | collective-permute-start | bytes 638984 | tf_op jit(solution)/shard_map/ppermute | solution.py:437
  34.8 8.9 %collective-permute-start.4 = (s32[32,1664]{1,0:T(8,128)S(1)}, s32[32,1664]{1,0:T(8,128)S(1)}, u32[]{:S(2)}, u32[]{:S(2)}) collective-permute-start(s32[32,1664]{1,0:T(8,128)S(1)} %constant_dynamic-update-slice_fusion), channel_id=1, source_target_pairs={{0,2},{2,4},{4,6},{6,8},{8,10},{10,12},{12,14},{14,16},{16,18},{18... | collective-permute-start | bytes 638984 | tf_op jit(solution)/shard_map/ppermute | solution.py:437
  45.4 12.7 %collective-permute-start.6 = (f32[8,128]{1,0:T(8,128)S(1)}, f32[8,128]{1,0:T(8,128)S(1)}, u32[]{:S(2)}, u32[]{:S(2)}) collective-permute-start(f32[8,128]{1,0:T(8,128)S(1)} %get-tuple-element.40), channel_id=1, source_target_pairs={{0,1},{1,0},{2,3},{3,2},{4,5},{5,4},{6,7},{7,6},{8,9},{9,8},{10,11... | collective-permute-start | bytes 12296 | tf_op jit(solution)/shard_map/ppermute | solution.py:463
  58.4 10.0 %copy-start.4 = (s32[8,64]{1,0:T(8,128)S(1)}, s32[8,64]{1,0:T(8,128)}, u32[]{:S(2)}) copy-start(s32[8,64]{1,0:T(8,128)} %get-tuple-element.23.place_ref) | copy-start | bytes 6148

commit v5 on v4

--- a/solution.py
+++ b/solution.py
@@ -241,9 +241,10 @@
     )
 
 
-def store_fields(fields, lines, out_ref):
+def store_fields(fields, lines, out_ref, exact_ref):
     his = fields[0].shape[1] // LO * lines
     for k, field in enumerate(fields):
+        exact_ref[k * lines : (k + 1) * lines, :] = field
         for yh in range(field.shape[1] // LO):
             high, low = split(field[:, yh * LO : (yh + 1) * LO])
             rows = slice(k * his + yh * lines, k * his + (yh + 1) * lines)
@@ -261,16 +262,16 @@
 
 
 def target_kernel(lines, _, table_ref, own_ref, *refs):
-    *near_refs, left_ref, right_ref, out_ref = refs
+    *near_refs, left_ref, right_ref, out_ref, exact_ref = refs
     mixed = mix_lines(table_ref, window_lines(own_ref, near_refs, left_ref, right_ref))
     grad_x = line_blur(mixed[0:lines], False)
     grad_y = line_blur(mixed[lines : 2 * lines], True)
     grad_z = line_blur(mixed[2 * lines : 3 * lines], False)
-    store_fields([grad_x, grad_y, grad_z], lines, out_ref)
+    store_fields([grad_x, grad_y, grad_z], lines, out_ref, exact_ref)
 
 
 def model_kernel(lines, _, table_ref, target_ref, own_ref, *refs):
-    *near_refs, left_ref, right_ref, out_ref, sum_ref = refs
+    *near_refs, left_ref, right_ref, out_ref, exact_ref, sum_ref = refs
     smooth = mix_lines(table_ref, window_lines(own_ref, near_refs, left_ref, right_ref))
     model = smooth[3 * lines :]
     target = target_ref[...]
@@ -283,27 +284,22 @@
     grad_x = line_blur(smooth[0:lines], False)
     grad_y = line_blur(smooth[lines : 2 * lines], True)
     grad_z = line_blur(smooth[2 * lines : 3 * lines], False)
-    store_fields([grad_x, grad_y, grad_z], lines, out_ref)
-
-
-def sample_kernel(his, rb, start, got_ref, field_ref, out_ref, force_ref):
-    slots = out_ref.shape[0]
-    beads = got_ref.shape[1] // 3
+    store_fields([grad_x, grad_y, grad_z], lines, out_ref, exact_ref)
+
+
+def sample_by_matmul(word, field_ref, his, store):
+    count, beads = word.shape
+    lo, hi = word & (LO - 1), (word >> 8) & 255
     lo_iota = lax.broadcasted_iota(I32, (LO, beads), 0)
-    sub_iota = lax.broadcasted_iota(I32, (8, beads), 0)
-
-    def body(i, carry):
-        word = got_ref[pl.ds(start + i * rb, rb), 0:beads]
-        lo = word & (LO - 1)
-        hi = (word >> 8) & 255
-        picks = [
-            jnp.where(lo_iota == lo[q : q + 1], 1.0, 0.0).astype(BF16) for q in range(rb)
-        ]
-        pick = jnp.concatenate(picks, axis=1)
-        sampled = jnp.dot(
-            field_ref[...], jnp.concatenate([pick, pick], axis=0), preferred_element_type=F32
-        )
-        for q in range(rb):
+    picks = [jnp.where(lo_iota == lo[q : q + 1], 1.0, 0.0).astype(BF16) for q in range(count)]
+    pick = jnp.concatenate(picks, axis=1)
+    sampled = jnp.dot(
+        field_ref[...], jnp.concatenate([pick, pick], axis=0), preferred_element_type=F32
+    )
+
+    def finish():
+        sub_iota = lax.broadcasted_iota(I32, (8, beads), 0)
+        for q in range(count):
             own = jnp.broadcast_to(hi[q : q + 1], (8, beads))
             group, within = own >> 3, (own & 7) == sub_iota
             found = [jnp.zeros((8, beads), F32)] * 3
@@ -311,12 +307,54 @@
                 here = group == j
                 for k in range(3):
                     rows = slice(k * his + 8 * j, k * his + 8 * j + 8)
-                    found[k] = jnp.where(
-                        here, sampled[rows, q * beads : (q + 1) * beads], found[k]
-                    )
+                    part = sampled[rows, q * beads : (q + 1) * beads]
+                    found[k] = jnp.where(here, part, found[k])
+            store(q, [jnp.sum(jnp.where(within, v, 0.0), axis=0, keepdims=True) for v in found])
+
+    return finish
+
+
+def sample_by_lanes(word, exact_ref, lines, store):
+    count, beads = word.shape
+    tiles = exact_ref.shape[1] // 128
+    line_shift, lo_shift = lines.bit_length() - 1, LO.bit_length() - 1
+    sub_iota = lax.broadcasted_iota(I32, (8, beads), 0)
+    for q in range(count):
+        own = jnp.broadcast_to(word[q : q + 1], (8, beads))
+        lo, hi = own & (LO - 1), (own >> lo_shift) & 255
+        line = hi & (lines - 1)
+        group = (line >> 3) * tiles + (hi >> line_shift) * (LO // 128) + (lo >> 7)
+        within, lane = (line & 7) == sub_iota, lo & 127
+        found = [jnp.zeros((8, beads), F32)] * 3
+        for j in range(lines // 8 * tiles):
+            here = group == j
+            first, tile = j // tiles * 8, j % tiles * 128
             for k in range(3):
-                value = jnp.sum(jnp.where(within, found[k], 0.0), axis=0, keepdims=True)
-                force_ref[k, pl.ds(i * rb + q, 1), :] = value
+                table = exact_ref[k * lines + first : k * lines + first + 8, tile : tile + 128]
+                part = jnp.take_along_axis(table, lane, axis=1, mode="promise_in_bounds")
+                found[k] = jnp.where(here, part, found[k])
+        store(q, [jnp.sum(jnp.where(within, v, 0.0), axis=0, keepdims=True) for v in found])
+
+
+def sample_kernel(
+    lines, his, rb, by_lanes, start, got_ref, field_ref, exact_ref, out_ref, force_ref
+):
+    slots = out_ref.shape[0]
+    beads = got_ref.shape[1] // 3
+    by_matmul = rb - by_lanes
+
+    def body(i, carry):
+        def store_from(first):
+            def store(q, values):
+                for k in range(3):
+                    force_ref[k, pl.ds(i * rb + first + q, 1), :] = values[k]
+
+            return store
+
+        word = got_ref[pl.ds(start + i * rb, rb), 0:beads]
+        finish = sample_by_matmul(word[:by_matmul], field_ref, his, store_from(0))
+        sample_by_lanes(word[by_matmul:], exact_ref, lines, store_from(by_matmul))
+        finish()
         return carry
 
     lax.fori_loop(0, slots // rb, body, 0)
@@ -472,6 +510,7 @@
     lines = planes * columns
     his = lines * (rows // LO)
     assert rows % LO == 0 and his <= 256 and columns >= 2 * KR
+    assert beads == 128 and lines & (lines - 1) == 0
     voxel_total = float(brick_count * columns * relay_count * planes * rows)
     most = max(2, 2 * frags // brick_count)
     slots = brick_count * most
@@ -531,19 +570,24 @@
     coded, from_left, from_right = lax.optimization_barrier((coded, from_left, from_right))
     target_parts = [target_lines] + target_blocks[1:] + [from_left, from_right]
     blocks = relay_blocks(coded, reach_two)
+    field_shapes = [
+        jax.ShapeDtypeStruct((3 * his, 2 * LO), BF16),
+        jax.ShapeDtypeStruct((3 * lines, rows), F32),
+    ]
     target_field = call_at(
         functools.partial(target_kernel, lines),
-        jax.ShapeDtypeStruct((3 * his, 2 * LO), BF16),
+        field_shapes,
         target_index, jnp.asarray(target_table), *target_parts,
         name="target_fields",
         macs=9 * lines * rows * 128,
     )
 
     def sample(field, start, count, name):
+        rb = min(32, count)
         return call(
-            functools.partial(sample_kernel, his, min(32, count), start),
+            functools.partial(sample_kernel, lines, his, rb, rb * 5 // 16, start),
             jax.ShapeDtypeStruct((count, 128), F32),
-            got, field,
+            got, *field,
             scratch=[pltpu.VMEM((3, count, beads), F32)],
             name=name,
             macs=6 * count * beads * his * LO,
@@ -559,12 +603,9 @@
     model_parts += [shifted(beside, "brick", 1), shifted(beside, "brick", -1)]
     target_second = sample(target_field, half, slots - half, "target_sample_b")
     target_second, *model_parts = lax.optimization_barrier((target_second, *model_parts))
-    model_field, partial = call_at(
+    *model_field, partial = call_at(
         functools.partial(model_kernel, lines),
-        [
-            jax.ShapeDtypeStruct((3 * his, 2 * LO), BF16),
-            jax.ShapeDtypeStruct((8, 128), F32),
-        ],
+        field_shapes + [jax.ShapeDtypeStruct((8, 128), F32)],
         model_index, jnp.asarray(model_table), target_lines, *model_parts,
         name="model_fields",
     )

time: 69.6 us -> 64.4 us (0.925)
  Pallas kernels: 33.3 us -> 27.2 us
  blocking collectives: 9.99 us -> 10.9 us
    pallas_call x8, Pallas kernels: 29.9 us -> 23.8 us  [call(): pl.pallas_call(kernel, out_shape=out_shape, scratch_shapes=list(scratch),...]
    all_to_all x1, blocking collectives: 9.99 us -> 10.9 us  [shards(): lax.all_to_all(leaving, 'brick', split_axis=0, concat_axis=0, tiled=True)]
  transfers between devices with their start and end apart: 8 -> 8, of which waited for: 1 -> 1; matrix products, arithmetic and copies ran while one was open for 0% -> 0% of each run, Pallas kernels for 44% -> 38%
where the time goes in v5:
time: 64.4 us; the launch traced here: 64 us
  Pallas kernels  27.2 us (42%)
  starting transfers between devices  19.4 us (30%)
  blocking collectives  10.9 us (17%)
  waiting for transfers between devices  5.18 us (8%)
  local copies, waits for them, and re-layouts  1.08 us (2%)
    pallas_call x8, Pallas kernels, call(): pl.pallas_call(kernel, out_shape=out_shape, scratch_shapes=list(scratch),...  23.8 us
    all_to_all x1, blocking collectives, shards(): lax.all_to_all(leaving, 'brick', split_axis=0, concat_axis=0, tiled=True)  10.9 us
    ppermute x4, starting transfers between devices, shifted(): return lax.ppermute(value, axis, pairs)  8.25 us
    all_to_all x1, starting transfers between devices, shards(): got = lax.all_to_all(sent, 'brick', split_axis=0, concat_axis=0, tiled=True)  5.92 us
    all_to_all x1, waiting for transfers between devices, shards(): got = lax.all_to_all(sent, 'brick', split_axis=0, concat_axis=0, tiled=True)  5.16 us
    ppermute x2, starting transfers between devices, relay_blocks(): return [value, lax.ppermute(value, 'relay', [(0, 1), (1, 0)])]  3.59 us
    pallas_call x2, Pallas kernels, call_at(): pl.pallas_call(kernel, out_shape=out_shape, grid_spec=pltpu.PrefetchScala...  3.4 us
    ppermute x1, starting transfers between devices, relay_total(): lax.ppermute(moving, 'relay', [(i, (i + 1) % size) for i in range(size)])  1.6 us
  transfers between devices with their start and end apart: 8, of which 1 were waited for; matrix products, arithmetic and copies ran while one was open for 0% of the time, Pallas kernels for 38%

profile of v5, /device:TPU:0, one launch (start us, length us, event | category | flops | bytes accessed | tf_op | source)
XLA Modules:
  0.0 64.0 jit_solution(6999862804185478578)
XLA Ops:
  0.0 0.9 %copy-done = f32[4,8,1536]{2,1,0:T(8,128)S(1)} copy-done((f32[4,8,1536]{2,1,0:T(8,128)S(1)}, f32[4,8,1536]{2,1,0:T(8,128)}, u32[]{:S(2)}) %copy-start) | copy-done | bytes 196632
  0.9 0.2 encode.1
  1.2 3.0 %collective-permute-start = (s32[16,1664]{1,0:T(8,128)S(1)}, s32[16,1664]{1,0:T(8,128)S(1)}, u32[]{:S(2)}, u32[]{:S(2)}) collective-permute-start(s32[16,1664]{1,0:T(8,128)S(1)} %encode.1), channel_id=1, source_target_pairs={{0,1},{1,0},{2,3},{3,2},{4,5},{5,4},{6,7},{7,6},{8,9},{9,8},{10,11... | collective-permute-start | bytes 319496 | tf_op jit(solution)/shard_map/ppermute | solution.py:481
  4.2 2.1 %pack.1 = (s32[128,384]{1,0:T(8,128)}, s32[8,64]{1,0:T(8,128)}) custom-call(s32[1,64]{1,0:T(1,128)} %bitcast.23, f32[3,64]{1,0:T(4,128)} %refs_1_.1, s32[64,128]{1,0:T(8,128)} %refs_2_.1, bf16[64,128]{1,0:T(8,128)(2,1)} %refs_3_.1, f32[3,64,128]{2,1,0:T(8,128)} %refs_4_.1), custom_call_target="tpu_custom_call" | custom-call | bytes 164864 | tf_op jit(solution)/shard_map/pack/pallas_call | solution.py:429
  6.3 5.9 %all-to-all-start = ((s32[16,8,384]{2,1,0:T(8,128)}), s32[16,8,384]{2,1,0:T(8,128)S(1)}, u32[]{:S(2)}, u32[]{:S(2)}) async-start(s32[16,8,384]{2,1,0:T(8,128)} %bitcast.22), calls=%async_computation | async-start | bytes 393216 | tf_op jit(solution)/shard_map/all_to_all | solution.py:561
  12.3 0.0 collective-permute-done.refs_0_
  12.5 2.3 %collective-permute-start.1 = (s32[16,1664]{1,0:T(8,128)S(1)}, s32[16,1664]{1,0:T(8,128)S(1)}, u32[]{:S(2)}, u32[]{:S(2)}) collective-permute-start(s32[16,1664]{1,0:T(8,128)S(1)} %reshape.30), channel_id=1, source_target_pairs={{0,2},{2,4},{4,6},{6,8},{8,10},{10,12},{12,14},{14,16},{16,18},{18... | collective-permute-start | bytes 319496 | tf_op jit(solution)/shard_map/ppermute | solution.py:475
  14.8 1.3 %collective-permute-start.2 = (s32[16,1664]{1,0:T(8,128)S(1)}, s32[16,1664]{1,0:T(8,128)S(1)}, u32[]{:S(2)}, u32[]{:S(2)}) collective-permute-start(s32[16,1664]{1,0:T(8,128)S(1)} %reshape.31), channel_id=1, source_target_pairs={{2,0},{4,2},{6,4},{8,6},{10,8},{12,10},{14,12},{16,14},{18,16},{20... | collective-permute-start | bytes 319496 | tf_op jit(solution)/shard_map/ppermute | solution.py:475
  16.1 5.2 %all-to-all-done = s32[16,8,384]{2,1,0:T(8,128)S(1)} async-done(((s32[16,8,384]{2,1,0:T(8,128)}), s32[16,8,384]{2,1,0:T(8,128)S(1)}, u32[]{:S(2)}, u32[]{:S(2)}) %all-to-all-start) | async-done | bytes 196640 | tf_op jit(solution)/shard_map/all_to_all | solution.py:561
  21.3 4.2 %splat.1 = (f32[32,1536]{1,0:T(8,128)S(1)}, s32[16,1664]{1,0:T(8,128)S(1)}) custom-call(s32[128,384]{1,0:T(8,128)S(1)} %bitcast.16), custom_call_target="tpu_custom_call" | custom-call | flops 1610612736 | bytes 196608 | tf_op jit(solution)/shard_map/splat/pallas_call | solution.py:429
  25.4 0.0 collective-permute-done.1.refs_1_
  25.5 0.0 collective-permute-done.2.refs_2_
  25.5 0.6 collective-permute-start.3
  26.0 0.0 copy-done.1
  26.0 0.0 copy-done.3
  26.0 1.7 %target_fields.1 = (bf16[576,512]{1,0:T(8,128)(2,1)S(1)}, f32[96,1536]{1,0:T(8,128)S(1)}) custom-call(s32[1]{0:T(128)} %bitcast.6._, bf16[6,96,384]{2,1,0:T(8,128)(2,1)S(1)} %copy-done.3, f32[32,1536]{1,0:T(8,128)S(1)} %bitcast.12, s32[16,1664]{1,0:T(8,128)S(1)} %collective-permute-done.refs_0_, s32[16,1664]{1,0:T(8,128)S(1)} %collective-permute-done.1.refs_1_, ...), custom_call_target="tpu_custom_call" | custom-call | flops 113246208 | bytes 516096 | tf_op jit(solution)/shard_map/target_fields/pallas_call | solution.py:447
  27.7 4.1 %target_sample_a.1.first_ref = f32[64,128]{1,0:T(8,128)S(1)} custom-call(s32[128,384]{1,0:T(8,128)S(1)} %bitcast.17, bf16[576,512]{1,0:T(8,128)(2,1)S(1)} %get-tuple-element.36.field_ref, f32[96,1536]{1,0:T(8,128)S(1)} %get-tuple-element.37.exact_ref), custom_call_target="tpu_custom_call" | custom-call | flops 4831838208 | bytes 1966080 | tf_op jit(solution)/shard_map/target_sample_a/pallas_call | solution.py:429
  31.8 0.0 collective-permute-done.3.refs_0_
  31.8 0.0 copy-start.2
  31.9 1.4 %collective-permute-start.5 = (s32[32,1664]{1,0:T(8,128)S(1)}, s32[32,1664]{1,0:T(8,128)S(1)}, u32[]{:S(2)}, u32[]{:S(2)}) collective-permute-start(s32[32,1664]{1,0:T(8,128)S(1)} %constant_dynamic-update-slice_fusion), channel_id=1, source_target_pairs={{2,0},{4,2},{6,4},{8,6},{10,8},{12,10},{14,12},{16,14},{18,16},{20... | collective-permute-start | bytes 638984 | tf_op jit(solution)/shard_map/ppermute | solution.py:475
  33.3 3.2 %collective-permute-start.4 = (s32[32,1664]{1,0:T(8,128)S(1)}, s32[32,1664]{1,0:T(8,128)S(1)}, u32[]{:S(2)}, u32[]{:S(2)}) collective-permute-start(s32[32,1664]{1,0:T(8,128)S(1)} %constant_dynamic-update-slice_fusion), channel_id=1, source_target_pairs={{0,2},{2,4},{4,6},{6,8},{8,10},{10,12},{12,14},{14,16},{16,18},{18... | collective-permute-start | bytes 638984 | tf_op jit(solution)/shard_map/ppermute | solution.py:475
  36.5 4.1 %target_sample_b.1.second_ref = f32[64,128]{1,0:T(8,128)S(1)} custom-call(s32[128,384]{1,0:T(8,128)S(1)} %bitcast.18, bf16[576,512]{1,0:T(8,128)(2,1)S(1)} %get-tuple-element.36.field_ref, f32[96,1536]{1,0:T(8,128)S(1)} %get-tuple-element.37.exact_ref), custom_call_target="tpu_custom_call" | custom-call | flops 4831838208 | bytes 1966080 | tf_op jit(solution)/shard_map/target_sample_b/pallas_call | solution.py:429
  40.6 0.0 collective-permute-done.5.refs_2_
  40.7 0.0 collective-permute-done.4.refs_1_
  40.7 0.0 copy-done.2
  40.7 1.7 %model_fields.1 = (bf16[576,512]{1,0:T(8,128)(2,1)S(1)}, f32[96,1536]{1,0:T(8,128)S(1)}, f32[8,128]{1,0:T(8,128)S(1)}) custom-call(s32[1]{0:T(128)} %bitcast.6._, bf16[6,128,576]{2,1,0:T(8,128)(2,1)S(1)} %copy-done.2, f32[32,1536]{1,0:T(8,128)S(1)} %bitcast.13, f32[32,1536]{1,0:T(8,128)S(1)} %get-tuple-element.42.own_ref, ...), custom_call_target="tpu_custom_call" | custom-call | bytes 925696 | tf_op jit(solution)/shard_map/model_fields/pallas_call | solution.py:447
  42.4 1.6 %collective-permute-start.6 = (f32[8,128]{1,0:T(8,128)S(1)}, f32[8,128]{1,0:T(8,128)S(1)}, u32[]{:S(2)}, u32[]{:S(2)}) collective-permute-start(f32[8,128]{1,0:T(8,128)S(1)} %get-tuple-element.48), channel_id=1, source_target_pairs={{0,1},{1,0},{2,3},{3,2},{4,5},{5,4},{6,7},{7,6},{8,9},{9,8},{10,11... | collective-permute-start | bytes 12296 | tf_op jit(solution)/shard_map/ppermute | solution.py:501
  44.0 8.1 %model_sample.1.model_ref = f32[128,128]{1,0:T(8,128)S(1)} custom-call(s32[128,384]{1,0:T(8,128)S(1)} %bitcast.19, bf16[576,512]{1,0:T(8,128)(2,1)S(1)} %get-tuple-element.46.field_ref, f32[96,1536]{1,0:T(8,128)S(1)} %get-tuple-element.47.exact_ref), custom_call_target="tpu_custom_call" | custom-call | flops 9663676416 | bytes 1966080 | tf_op jit(solution)/shard_map/model_sample/pallas_call | solution.py:429
  52.1 0.0 collective-permute-done.6
  52.1 0.2 join.1
  52.3 10.9 %all_to_all.22 = f32[16,1,128]{2,1,0:T(1,128)S(1)} all-to-all(f32[16,1,128]{2,1,0:T(1,128)S(1)} %bitcast.20), channel_id=1, replica_groups=mesh['brick'=16,'relay'=2] {'brick'}, dimensions={0} | all-to-all | bytes 16384 | tf_op jit(solution)/shard_map/all_to_all | solution.py:620
  63.2 0.9 %finish.1 = f32[6,64]{1,0:T(8,128)} custom-call(s32[8,64]{1,0:T(8,128)S(1)} %copy-done.4, f32[16,128]{1,0:T(8,128)S(1)} %bitcast.21), custom_call_target="tpu_custom_call" | custom-call | bytes 10240 | tf_op jit(solution)/shard_map/finish/pallas_call | solution.py:429
  (14 shorter events, 0.2 us)
Async XLA Ops:
  0.0 0.9 %copy-start = (f32[4,8,1536]{2,1,0:T(8,128)S(1)}, f32[4,8,1536]{2,1,0:T(8,128)}, u32[]{:S(2)}) copy-start(f32[4,8,1536]{2,1,0:T(8,128)} %param.8) | copy-start | bytes 589828
  1.2 11.2 %collective-permute-start = (s32[16,1664]{1,0:T(8,128)S(1)}, s32[16,1664]{1,0:T(8,128)S(1)}, u32[]{:S(2)}, u32[]{:S(2)}) collective-permute-start(s32[16,1664]{1,0:T(8,128)S(1)} %encode.1), channel_id=1, source_target_pairs={{0,1},{1,0},{2,3},{3,2},{4,5},{5,4},{6,7},{7,6},{8,9},{9,8},{10,11... | collective-permute-start | bytes 319496 | tf_op jit(solution)/shard_map/ppermute | solution.py:481
  6.3 14.9 %all-to-all-start = ((s32[16,8,384]{2,1,0:T(8,128)}), s32[16,8,384]{2,1,0:T(8,128)S(1)}, u32[]{:S(2)}, u32[]{:S(2)}) async-start(s32[16,8,384]{2,1,0:T(8,128)} %bitcast.22), calls=%async_computation | async-start | bytes 393216 | tf_op jit(solution)/shard_map/all_to_all | solution.py:561
  12.5 13.0 %collective-permute-start.1 = (s32[16,1664]{1,0:T(8,128)S(1)}, s32[16,1664]{1,0:T(8,128)S(1)}, u32[]{:S(2)}, u32[]{:S(2)}) collective-permute-start(s32[16,1664]{1,0:T(8,128)S(1)} %reshape.30), channel_id=1, source_target_pairs={{0,2},{2,4},{4,6},{6,8},{8,10},{10,12},{12,14},{14,16},{16,18},{18... | collective-permute-start | bytes 319496 | tf_op jit(solution)/shard_map/ppermute | solution.py:475
  14.8 10.6 %collective-permute-start.2 = (s32[16,1664]{1,0:T(8,128)S(1)}, s32[16,1664]{1,0:T(8,128)S(1)}, u32[]{:S(2)}, u32[]{:S(2)}) collective-permute-start(s32[16,1664]{1,0:T(8,128)S(1)} %reshape.31), channel_id=1, source_target_pairs={{2,0},{4,2},{6,4},{8,6},{10,8},{12,10},{14,12},{16,14},{18,16},{20... | collective-permute-start | bytes 319496 | tf_op jit(solution)/shard_map/ppermute | solution.py:475
  21.3 4.8 %copy-start.1 = (f32[4,8,1536]{2,1,0:T(8,128)S(1)}, f32[4,8,1536]{2,1,0:T(8,128)}, u32[]{:S(2)}) copy-start(f32[4,8,1536]{2,1,0:T(8,128)} %param.8) | copy-start | bytes 589828
  21.3 4.8 %copy-start.3 = (bf16[6,96,384]{2,1,0:T(8,128)(2,1)S(1)}, bf16[6,96,384]{2,1,0:T(8,128)(2,1)}, u32[]{:S(2)}) copy-start(bf16[6,96,384]{2,1,0:T(8,128)(2,1)} %constant.26.clone.table_ref) | copy-start | bytes 1327108
  25.5 6.3 %collective-permute-start.3 = (s32[16,1664]{1,0:T(8,128)S(1)}, s32[16,1664]{1,0:T(8,128)S(1)}, u32[]{:S(2)}, u32[]{:S(2)}) collective-permute-start(s32[16,1664]{1,0:T(8,128)S(1)} %get-tuple-element.40), channel_id=1, source_target_pairs={{0,1},{1,0},{2,3},{3,2},{4,5},{5,4},{6,7},{7,6},{8,9},{9,8},{10,11... | collective-permute-start | bytes 319496 | tf_op jit(solution)/shard_map/ppermute | solution.py:481
  31.8 8.8 %copy-start.2 = (bf16[6,128,576]{2,1,0:T(8,128)(2,1)S(1)}, bf16[6,128,576]{2,1,0:T(8,128)(2,1)}, u32[]{:S(2)}) copy-start(bf16[6,128,576]{2,1,0:T(8,128)(2,1)} %constant.27.clone.table_ref) | copy-start | bytes 2654212
  31.9 8.8 %collective-permute-start.5 = (s32[32,1664]{1,0:T(8,128)S(1)}, s32[32,1664]{1,0:T(8,128)S(1)}, u32[]{:S(2)}, u32[]{:S(2)}) collective-permute-start(s32[32,1664]{1,0:T(8,128)S(1)} %constant_dynamic-update-slice_fusion), channel_id=1, source_target_pairs={{2,0},{4,2},{6,4},{8,6},{10,8},{12,10},{14,12},{16,14},{18,16},{20... | collective-permute-start | bytes 638984 | tf_op jit(solution)/shard_map/ppermute | solution.py:475
  33.3 7.4 %collective-permute-start.4 = (s32[32,1664]{1,0:T(8,128)S(1)}, s32[32,1664]{1,0:T(8,128)S(1)}, u32[]{:S(2)}, u32[]{:S(2)}) collective-permute-start(s32[32,1664]{1,0:T(8,128)S(1)} %constant_dynamic-update-slice_fusion), channel_id=1, source_target_pairs={{0,2},{2,4},{4,6},{6,8},{8,10},{10,12},{12,14},{14,16},{16,18},{18... | collective-permute-start | bytes 638984 | tf_op jit(solution)/shard_map/ppermute | solution.py:475
  42.4 9.7 %collective-permute-start.6 = (f32[8,128]{1,0:T(8,128)S(1)}, f32[8,128]{1,0:T(8,128)S(1)}, u32[]{:S(2)}, u32[]{:S(2)}) collective-permute-start(f32[8,128]{1,0:T(8,128)S(1)} %get-tuple-element.48), channel_id=1, source_target_pairs={{0,1},{1,0},{2,3},{3,2},{4,5},{5,4},{6,7},{7,6},{8,9},{9,8},{10,11... | collective-permute-start | bytes 12296 | tf_op jit(solution)/shard_map/ppermute | solution.py:501
  52.3 10.9 %copy-start.4 = (s32[8,64]{1,0:T(8,128)S(1)}, s32[8,64]{1,0:T(8,128)}, u32[]{:S(2)}) copy-start(s32[8,64]{1,0:T(8,128)} %get-tuple-element.27.place_ref) | copy-start | bytes 6148

commit v6 on v5

--- a/solution.py
+++ b/solution.py
@@ -103,14 +103,15 @@
 
 
 def pack_kernel(most, lines, row_count, *refs):
-    inputs, (out_ref, place_ref), held, sems = refs[:5], refs[5:7], refs[7:12], refs[12]
+    inputs, (out_ref, place_ref, code_ref) = refs[:6], refs[6:9]
+    held, sems = refs[9:15], refs[15]
     copies = [
         pltpu.make_async_copy(source, target, sems.at[k])
         for k, (source, target) in enumerate(zip(inputs, held))
     ]
     for copy in copies:
         copy.start()
-    brick_ref, angle_ref, cell_ref, weight_ref, arm_ref = held
+    brick_ref, angle_ref, cell_ref, weight_ref, arm_ref, target_ref = held
     for copy in copies[:2]:
         copy.wait()
     frags, beads = cell_ref.shape
@@ -134,6 +135,7 @@
     place_ref[1:2, :] = rank
     for copy in copies[2:]:
         copy.wait()
+    encode(target_ref[...], code_ref)
     levers = []
     for i in range(3):
         total = turn[i][0] * arm_ref[0]
@@ -189,10 +191,6 @@
         rows = slice(k * half, (k + 1) * half)
         lines += [low[rows], high[rows]]
     return lines
-
-
-def encode_kernel(value_ref, out_ref):
-    encode(value_ref[...], out_ref)
 
 
 def splat_kernel(lines, rb, got_ref, out_ref, code_ref, acc_ref):
@@ -378,7 +376,8 @@
     out_ref[...] = total
 
 
-def join_kernel(most, first_ref, second_ref, model_ref, sum_ref, out_ref):
+def join_kernel(most, *refs):
+    *target_refs, model_ref, sum_ref, out_ref = refs
     bricks = out_ref.shape[0]
     lane = lax.broadcasted_iota(I32, out_ref.shape, 1)
     sums = sum_ref[0:1, :]
@@ -386,8 +385,9 @@
         sums = sums + sum_ref[8 * k : 8 * k + 1, :]
     total = jnp.zeros(out_ref.shape, F32)
     for k in range(most):
-        rows, half = pl.ds(k, bricks, stride=most), pl.ds(k, bricks // 2, stride=most)
-        own = jnp.concatenate([first_ref[half, :], second_ref[half, :]], axis=0)
+        rows = pl.ds(k, bricks, stride=most)
+        parts = [ref[pl.ds(k, ref.shape[0] // most, stride=most), :] for ref in target_refs]
+        own = jnp.concatenate(parts, axis=0)
         own = jnp.where(lane < 6, own, 0.0)
         own = own + pltpu.roll(jnp.where(lane < 6, model_ref[rows, :], 0.0), 6, 1)
         if k == 0:
@@ -536,20 +536,15 @@
 
     target_lines = target.reshape(lines, rows)
     words = jax.ShapeDtypeStruct((lines // 2, rows + SCALE_LANES), I32)
-    target_blocks = relay_blocks(call(encode_kernel, words, target_lines, name="encode"), reach_one)
-    by_column = [t.reshape(-1, columns, rows + SCALE_LANES) for t in target_blocks]
-    left_edge = jnp.concatenate([t[:, columns - KR :] for t in by_column], axis=0)
-    right_edge = jnp.concatenate([t[:, :KR] for t in by_column], axis=0)
-    from_left = shifted(left_edge.reshape(-1, rows + SCALE_LANES), "brick", 1)
-    from_right = shifted(right_edge.reshape(-1, rows + SCALE_LANES), "brick", -1)
-
     hbm = pl.BlockSpec(memory_space=pltpu.HBM)
     packed = [frag_brick.reshape(1, frags), frag_angle, bead_cell, bead_weight, bead_arm]
-    sent, place = call(
+    packed += [target_lines]
+    sent, place, target_code = call(
         functools.partial(pack_kernel, most, lines, rows),
         [
             jax.ShapeDtypeStruct((slots, 3 * beads), I32),
             jax.ShapeDtypeStruct((8, frags), I32),
+            words,
         ],
         *packed,
         in_specs=[hbm] * len(packed),
@@ -558,9 +553,16 @@
         name="pack",
         vmem=PACK_VMEM_BYTES,
     )
+    target_blocks = relay_blocks(target_code, reach_one)
+    by_column = [t.reshape(-1, columns, rows + SCALE_LANES) for t in target_blocks]
+    left_edge = jnp.concatenate([t[:, columns - KR :] for t in by_column], axis=0)
+    right_edge = jnp.concatenate([t[:, :KR] for t in by_column], axis=0)
+    from_left = shifted(left_edge.reshape(-1, rows + SCALE_LANES), "brick", 1)
+    from_right = shifted(right_edge.reshape(-1, rows + SCALE_LANES), "brick", -1)
+
     got = lax.all_to_all(sent, "brick", split_axis=0, concat_axis=0, tiled=True)
     smooth, coded = call(
-        functools.partial(splat_kernel, lines, min(32, slots)),
+        functools.partial(splat_kernel, lines, min(64, slots)),
         [jax.ShapeDtypeStruct((lines, rows), F32), words],
         got,
         scratch=[pltpu.VMEM((his, LO), F32)],
@@ -593,15 +595,15 @@
             macs=6 * count * beads * his * LO,
         )
 
-    half = slots // 2
-    target_first = sample(target_field, 0, half, "target_sample_a")
+    part = slots // 4
+    target_first = sample(target_field, 0, part, "target_sample_a")
     blocks, target_first, target_field = lax.optimization_barrier(
         (blocks, target_first, target_field)
     )
     beside = jnp.concatenate(blocks, axis=0)
     model_parts = [smooth] + blocks[1:]
     model_parts += [shifted(beside, "brick", 1), shifted(beside, "brick", -1)]
-    target_second = sample(target_field, half, slots - half, "target_sample_b")
+    target_second = sample(target_field, part, slots - part, "target_sample_b")
     target_second, *model_parts = lax.optimization_barrier((target_second, *model_parts))
     *model_field, partial = call_at(
         functools.partial(model_kernel, lines),

time: 64.4 us -> 67.1 us (1.042)
  blocking collectives: 10.9 us -> 14.8 us
  local copies, waits for them, and re-layouts: 1.08 us -> 0.16 us
  starting transfers between devices: 19.4 us -> 20.3 us
  waiting for transfers between devices: 5.18 us -> 4.38 us
    all_to_all x1, waiting for transfers between devices: 5.16 us -> 0.61 us  [shards(): got = lax.all_to_all(sent, 'brick', split_axis=0, concat_axis=0, tiled=True)]
    all_to_all x1, blocking collectives: 10.9 us -> 14.8 us  [shards(): lax.all_to_all(leaving, 'brick', split_axis=0, concat_axis=0, tiled=True)]
    ppermute x2, waiting for transfers between devices: 0.01 us -> 3.76 us  [relay_blocks(): return [value, lax.ppermute(value, 'relay', [(0, 1), (1, 0)])]]
    all_to_all x1, starting transfers between devices: 5.92 us -> 7.51 us  [shards(): got = lax.all_to_all(sent, 'brick', split_axis=0, concat_axis=0, tiled=True)]
    ppermute x1, starting transfers between devices: 1.6 us -> 0.56 us  [relay_total(): lax.ppermute(moving, 'relay', [(i, (i + 1) % size) for i in range(size)])]
    unnamed x11, local copies, waits for them, and re-layouts: 0.95 us -> 0.03 us
    ppermute x4, starting transfers between devices: 8.25 us -> 9.03 us  [shifted(): return lax.ppermute(value, axis, pairs)]
    pallas_call x8 -> x7, Pallas kernels: 23.8 us -> 23.4 us  [call(): pl.pallas_call(kernel, out_shape=out_shape, scratch_shapes=list(scratch),...]
  transfers between devices with their start and end apart: 8 -> 8, of which waited for: 1 -> 2; matrix products, arithmetic and copies ran while one was open for 0% -> 0% of each run, Pallas kernels for 38% -> 33%
where the time goes in v6:
time: 67.1 us; the launch traced here: 66.7 us
  Pallas kernels  26.8 us (40%)
  starting transfers between devices  20.3 us (30%)
  blocking collectives  14.8 us (22%)
  waiting for transfers between devices  4.38 us (7%)
    pallas_call x7, Pallas kernels, call(): pl.pallas_call(kernel, out_shape=out_shape, scratch_shapes=list(scratch),...  23.4 us
    all_to_all x1, blocking collectives, shards(): lax.all_to_all(leaving, 'brick', split_axis=0, concat_axis=0, tiled=True)  14.8 us
    ppermute x4, starting transfers between devices, shifted(): return lax.ppermute(value, axis, pairs)  9.03 us
    all_to_all x1, starting transfers between devices, shards(): got = lax.all_to_all(sent, 'brick', split_axis=0, concat_axis=0, tiled=True)  7.51 us
    ppermute x2, waiting for transfers between devices, relay_blocks(): return [value, lax.ppermute(value, 'relay', [(0, 1), (1, 0)])]  3.76 us
    pallas_call x2, Pallas kernels, call_at(): pl.pallas_call(kernel, out_shape=out_shape, grid_spec=pltpu.PrefetchScala...  3.38 us
    ppermute x2, starting transfers between devices, relay_blocks(): return [value, lax.ppermute(value, 'relay', [(0, 1), (1, 0)])]  3.16 us
  transfers between devices with their start and end apart: 8, of which 2 were waited for; matrix products, arithmetic and copies ran while one was open for 0% of the time, Pallas kernels for 33%

profile of v6, /device:TPU:0, one launch (start us, length us, event | category | flops | bytes accessed | tf_op | source)
XLA Modules:
  0.0 66.7 jit_solution(16839482325473262261)
XLA Ops:
  0.0 2.2 %pack.1 = (s32[128,384]{1,0:T(8,128)}, s32[8,64]{1,0:T(8,128)}, s32[16,1664]{1,0:T(8,128)}) custom-call(s32[1,64]{1,0:T(1,128)} %bitcast.23, f32[3,64]{1,0:T(4,128)} %refs_1_.1, s32[64,128]{1,0:T(8,128)} %refs_2_.1, bf16[64,128]{1,0:T(8,128)(2,1)} %refs_3_.1, f32[3,64,128]{2,1,0:T(8,128)} %refs_4_.1, f32[32,1536]{1,0:T(8,128)} %bitcast.11), custom_call_target="tpu_custom_call" | custom-call | bytes 361472 | tf_op jit(solution)/shard_map/pack/pallas_call | solution.py:429
  2.2 0.0 copy-start.4
  2.3 7.5 %all-to-all-start = ((s32[16,8,384]{2,1,0:T(8,128)}), s32[16,8,384]{2,1,0:T(8,128)S(1)}, u32[]{:S(2)}, u32[]{:S(2)}) async-start(s32[16,8,384]{2,1,0:T(8,128)} %bitcast.21), calls=%async_computation | async-start | bytes 393216 | tf_op jit(solution)/shard_map/all_to_all | solution.py:563
  9.8 0.0 copy-done.4
  9.8 1.6 %collective-permute-start = (s32[16,1664]{1,0:T(8,128)S(1)}, s32[16,1664]{1,0:T(8,128)S(1)}, u32[]{:S(2)}, u32[]{:S(2)}) collective-permute-start(s32[16,1664]{1,0:T(8,128)S(1)} %copy-done.4), channel_id=1, source_target_pairs={{0,1},{1,0},{2,3},{3,2},{4,5},{5,4},{6,7},{7,6},{8,9},{9,8},{10,11... | collective-permute-start | bytes 319496 | tf_op jit(solution)/shard_map/ppermute | solution.py:481
  11.4 3.8 %collective-permute-done.refs_0_ = s32[16,1664]{1,0:T(8,128)S(1)} collective-permute-done((s32[16,1664]{1,0:T(8,128)S(1)}, s32[16,1664]{1,0:T(8,128)S(1)}, u32[]{:S(2)}, u32[]{:S(2)}) %collective-permute-start) | collective-permute-done | bytes 106528 | tf_op jit(solution)/shard_map/ppermute | solution.py:481
  15.3 1.5 %collective-permute-start.1 = (s32[16,1664]{1,0:T(8,128)S(1)}, s32[16,1664]{1,0:T(8,128)S(1)}, u32[]{:S(2)}, u32[]{:S(2)}) collective-permute-start(s32[16,1664]{1,0:T(8,128)S(1)} %reshape.30), channel_id=1, source_target_pairs={{0,2},{2,4},{4,6},{6,8},{8,10},{10,12},{12,14},{14,16},{16,18},{18... | collective-permute-start | bytes 319496 | tf_op jit(solution)/shard_map/ppermute | solution.py:475
  16.9 1.3 %collective-permute-start.2 = (s32[16,1664]{1,0:T(8,128)S(1)}, s32[16,1664]{1,0:T(8,128)S(1)}, u32[]{:S(2)}, u32[]{:S(2)}) collective-permute-start(s32[16,1664]{1,0:T(8,128)S(1)} %reshape.31), channel_id=1, source_target_pairs={{2,0},{4,2},{6,4},{8,6},{10,8},{12,10},{14,12},{16,14},{18,16},{20... | collective-permute-start | bytes 319496 | tf_op jit(solution)/shard_map/ppermute | solution.py:475
  18.2 0.6 all-to-all-done
  18.8 3.8 %splat.1 = (f32[32,1536]{1,0:T(8,128)S(1)}, s32[16,1664]{1,0:T(8,128)S(1)}) custom-call(s32[128,384]{1,0:T(8,128)S(1)} %bitcast.15), custom_call_target="tpu_custom_call" | custom-call | flops 1610612736 | bytes 196608 | tf_op jit(solution)/shard_map/splat/pallas_call | solution.py:429
  22.6 0.0 collective-permute-done.1.refs_1_
  22.6 0.0 collective-permute-done.2.refs_2_
  22.6 1.6 %collective-permute-start.3 = (s32[16,1664]{1,0:T(8,128)S(1)}, s32[16,1664]{1,0:T(8,128)S(1)}, u32[]{:S(2)}, u32[]{:S(2)}) collective-permute-start(s32[16,1664]{1,0:T(8,128)S(1)} %get-tuple-element.42), channel_id=1, source_target_pairs={{0,1},{1,0},{2,3},{3,2},{4,5},{5,4},{6,7},{7,6},{8,9},{9,8},{10,11... | collective-permute-start | bytes 319496 | tf_op jit(solution)/shard_map/ppermute | solution.py:481
  24.2 0.0 copy-done
  24.2 0.0 copy-done.2
  24.2 1.7 %target_fields.1 = (bf16[576,512]{1,0:T(8,128)(2,1)S(1)}, f32[96,1536]{1,0:T(8,128)S(1)}) custom-call(s32[1]{0:T(128)} %bitcast.6._, bf16[6,96,384]{2,1,0:T(8,128)(2,1)S(1)} %copy-done.2, f32[32,1536]{1,0:T(8,128)S(1)} %bitcast.12, s32[16,1664]{1,0:T(8,128)S(1)} %collective-permute-done.refs_0_, s32[16,1664]{1,0:T(8,128)S(1)} %collective-permute-done.1.refs_1_, ...), custom_call_target="tpu_custom_call" | custom-call | flops 113246208 | bytes 516096 | tf_op jit(solution)/shard_map/target_fields/pallas_call | solution.py:447
  25.9 2.0 %target_sample_a.1.refs_0_ = f32[32,128]{1,0:T(8,128)S(1)} custom-call(s32[128,384]{1,0:T(8,128)S(1)} %bitcast.16, bf16[576,512]{1,0:T(8,128)(2,1)S(1)} %get-tuple-element.38.field_ref, f32[96,1536]{1,0:T(8,128)S(1)} %get-tuple-element.39.exact_ref), custom_call_target="tpu_custom_call" | custom-call | flops 2415919104 | bytes 1966080 | tf_op jit(solution)/shard_map/target_sample_a/pallas_call | solution.py:429
  27.9 0.0 collective-permute-done.3.refs_0_
  27.9 0.0 copy-start.1
  27.9 1.4 %collective-permute-start.5 = (s32[32,1664]{1,0:T(8,128)S(1)}, s32[32,1664]{1,0:T(8,128)S(1)}, u32[]{:S(2)}, u32[]{:S(2)}) collective-permute-start(s32[32,1664]{1,0:T(8,128)S(1)} %constant_dynamic-update-slice_fusion), channel_id=1, source_target_pairs={{2,0},{4,2},{6,4},{8,6},{10,8},{12,10},{14,12},{16,14},{18,16},{20... | collective-permute-start | bytes 638984 | tf_op jit(solution)/shard_map/ppermute | solution.py:475
  29.4 4.8 %collective-permute-start.4 = (s32[32,1664]{1,0:T(8,128)S(1)}, s32[32,1664]{1,0:T(8,128)S(1)}, u32[]{:S(2)}, u32[]{:S(2)}) collective-permute-start(s32[32,1664]{1,0:T(8,128)S(1)} %constant_dynamic-update-slice_fusion), channel_id=1, source_target_pairs={{0,2},{2,4},{4,6},{6,8},{8,10},{10,12},{12,14},{14,16},{16,18},{18... | collective-permute-start | bytes 638984 | tf_op jit(solution)/shard_map/ppermute | solution.py:475
  34.2 6.1 %target_sample_b.1.refs_1_ = f32[96,128]{1,0:T(8,128)S(1)} custom-call(s32[128,384]{1,0:T(8,128)S(1)} %bitcast.17, bf16[576,512]{1,0:T(8,128)(2,1)S(1)} %get-tuple-element.38.field_ref, f32[96,1536]{1,0:T(8,128)S(1)} %get-tuple-element.39.exact_ref), custom_call_target="tpu_custom_call" | custom-call | flops 7247757312 | bytes 1966080 | tf_op jit(solution)/shard_map/target_sample_b/pallas_call | solution.py:429
  40.2 0.0 collective-permute-done.5.refs_2_
  40.3 0.0 collective-permute-done.4.refs_1_
  40.3 0.0 copy-done.1
  40.3 1.7 %model_fields.1 = (bf16[576,512]{1,0:T(8,128)(2,1)S(1)}, f32[96,1536]{1,0:T(8,128)S(1)}, f32[8,128]{1,0:T(8,128)S(1)}) custom-call(s32[1]{0:T(128)} %bitcast.6._, bf16[6,128,576]{2,1,0:T(8,128)(2,1)S(1)} %copy-done.1, f32[32,1536]{1,0:T(8,128)S(1)} %bitcast.13, f32[32,1536]{1,0:T(8,128)S(1)} %get-tuple-element.44.own_ref, ...), custom_call_target="tpu_custom_call" | custom-call | bytes 925696 | tf_op jit(solution)/shard_map/model_fields/pallas_call | solution.py:447
  42.0 0.6 collective-permute-start.6
  42.6 8.3 %model_sample.1.refs_2_ = f32[128,128]{1,0:T(8,128)S(1)} custom-call(s32[128,384]{1,0:T(8,128)S(1)} %bitcast.18, bf16[576,512]{1,0:T(8,128)(2,1)S(1)} %get-tuple-element.48.field_ref, f32[96,1536]{1,0:T(8,128)S(1)} %get-tuple-element.49.exact_ref), custom_call_target="tpu_custom_call" | custom-call | flops 9663676416 | bytes 1966080 | tf_op jit(solution)/shard_map/model_sample/pallas_call | solution.py:429
  50.8 0.0 collective-permute-done.6
  50.9 0.2 join.1
  51.0 14.8 %all_to_all.22 = f32[16,1,128]{2,1,0:T(1,128)S(1)} all-to-all(f32[16,1,128]{2,1,0:T(1,128)S(1)} %bitcast.19), channel_id=1, replica_groups=mesh['brick'=16,'relay'=2] {'brick'}, dimensions={0} | all-to-all | bytes 16384 | tf_op jit(solution)/shard_map/all_to_all | solution.py:622
  65.8 0.9 %finish.1 = f32[6,64]{1,0:T(8,128)} custom-call(s32[8,64]{1,0:T(8,128)S(1)} %copy-done.3, f32[16,128]{1,0:T(8,128)S(1)} %bitcast.20), custom_call_target="tpu_custom_call" | custom-call | bytes 10240 | tf_op jit(solution)/shard_map/finish/pallas_call | solution.py:429
  (13 shorter events, 0.2 us)
Async XLA Ops:
  2.2 7.5 %copy-start.4 = (s32[16,1664]{1,0:T(8,128)S(1)}, s32[16,1664]{1,0:T(8,128)}, u32[]{:S(2)}) copy-start(s32[16,1664]{1,0:T(8,128)} %get-tuple-element.31) | copy-start | bytes 319492
  2.3 16.5 %all-to-all-start = ((s32[16,8,384]{2,1,0:T(8,128)}), s32[16,8,384]{2,1,0:T(8,128)S(1)}, u32[]{:S(2)}, u32[]{:S(2)}) async-start(s32[16,8,384]{2,1,0:T(8,128)} %bitcast.21), calls=%async_computation | async-start | bytes 393216 | tf_op jit(solution)/shard_map/all_to_all | solution.py:563
  9.8 5.4 %collective-permute-start = (s32[16,1664]{1,0:T(8,128)S(1)}, s32[16,1664]{1,0:T(8,128)S(1)}, u32[]{:S(2)}, u32[]{:S(2)}) collective-permute-start(s32[16,1664]{1,0:T(8,128)S(1)} %copy-done.4), channel_id=1, source_target_pairs={{0,1},{1,0},{2,3},{3,2},{4,5},{5,4},{6,7},{7,6},{8,9},{9,8},{10,11... | collective-permute-start | bytes 319496 | tf_op jit(solution)/shard_map/ppermute | solution.py:481
  15.3 7.3 %collective-permute-start.1 = (s32[16,1664]{1,0:T(8,128)S(1)}, s32[16,1664]{1,0:T(8,128)S(1)}, u32[]{:S(2)}, u32[]{:S(2)}) collective-permute-start(s32[16,1664]{1,0:T(8,128)S(1)} %reshape.30), channel_id=1, source_target_pairs={{0,2},{2,4},{4,6},{6,8},{8,10},{10,12},{12,14},{14,16},{16,18},{18... | collective-permute-start | bytes 319496 | tf_op jit(solution)/shard_map/ppermute | solution.py:475
  16.9 5.7 %collective-permute-start.2 = (s32[16,1664]{1,0:T(8,128)S(1)}, s32[16,1664]{1,0:T(8,128)S(1)}, u32[]{:S(2)}, u32[]{:S(2)}) collective-permute-start(s32[16,1664]{1,0:T(8,128)S(1)} %reshape.31), channel_id=1, source_target_pairs={{2,0},{4,2},{6,4},{8,6},{10,8},{12,10},{14,12},{16,14},{18,16},{20... | collective-permute-start | bytes 319496 | tf_op jit(solution)/shard_map/ppermute | solution.py:475
  18.8 5.4 %copy-start = (f32[4,8,1536]{2,1,0:T(8,128)S(1)}, f32[4,8,1536]{2,1,0:T(8,128)}, u32[]{:S(2)}) copy-start(f32[4,8,1536]{2,1,0:T(8,128)} %param.8) | copy-start | bytes 589828
  18.8 5.4 %copy-start.2 = (bf16[6,96,384]{2,1,0:T(8,128)(2,1)S(1)}, bf16[6,96,384]{2,1,0:T(8,128)(2,1)}, u32[]{:S(2)}) copy-start(bf16[6,96,384]{2,1,0:T(8,128)(2,1)} %constant.26.clone.table_ref) | copy-start | bytes 1327108
  22.6 5.3 %collective-permute-start.3 = (s32[16,1664]{1,0:T(8,128)S(1)}, s32[16,1664]{1,0:T(8,128)S(1)}, u32[]{:S(2)}, u32[]{:S(2)}) collective-permute-start(s32[16,1664]{1,0:T(8,128)S(1)} %get-tuple-element.42), channel_id=1, source_target_pairs={{0,1},{1,0},{2,3},{3,2},{4,5},{5,4},{6,7},{7,6},{8,9},{9,8},{10,11... | collective-permute-start | bytes 319496 | tf_op jit(solution)/shard_map/ppermute | solution.py:481
  27.9 12.3 %copy-start.1 = (bf16[6,128,576]{2,1,0:T(8,128)(2,1)S(1)}, bf16[6,128,576]{2,1,0:T(8,128)(2,1)}, u32[]{:S(2)}) copy-start(bf16[6,128,576]{2,1,0:T(8,128)(2,1)} %constant.27.clone.table_ref) | copy-start | bytes 2654212
  27.9 12.3 %collective-permute-start.5 = (s32[32,1664]{1,0:T(8,128)S(1)}, s32[32,1664]{1,0:T(8,128)S(1)}, u32[]{:S(2)}, u32[]{:S(2)}) collective-permute-start(s32[32,1664]{1,0:T(8,128)S(1)} %constant_dynamic-update-slice_fusion), channel_id=1, source_target_pairs={{2,0},{4,2},{6,4},{8,6},{10,8},{12,10},{14,12},{16,14},{18,16},{20... | collective-permute-start | bytes 638984 | tf_op jit(solution)/shard_map/ppermute | solution.py:475
  29.4 10.9 %collective-permute-start.4 = (s32[32,1664]{1,0:T(8,128)S(1)}, s32[32,1664]{1,0:T(8,128)S(1)}, u32[]{:S(2)}, u32[]{:S(2)}) collective-permute-start(s32[32,1664]{1,0:T(8,128)S(1)} %constant_dynamic-update-slice_fusion), channel_id=1, source_target_pairs={{0,2},{2,4},{4,6},{6,8},{8,10},{10,12},{12,14},{14,16},{16,18},{18... | collective-permute-start | bytes 638984 | tf_op jit(solution)/shard_map/ppermute | solution.py:475
  42.0 8.8 %collective-permute-start.6 = (f32[8,128]{1,0:T(8,128)S(1)}, f32[8,128]{1,0:T(8,128)S(1)}, u32[]{:S(2)}, u32[]{:S(2)}) collective-permute-start(f32[8,128]{1,0:T(8,128)S(1)} %get-tuple-element.50), channel_id=1, source_target_pairs={{0,1},{1,0},{2,3},{3,2},{4,5},{5,4},{6,7},{7,6},{8,9},{9,8},{10,11... | collective-permute-start | bytes 12296 | tf_op jit(solution)/shard_map/ppermute | solution.py:501
  51.0 14.8 %copy-start.3 = (s32[8,64]{1,0:T(8,128)S(1)}, s32[8,64]{1,0:T(8,128)}, u32[]{:S(2)}) copy-start(s32[8,64]{1,0:T(8,128)} %get-tuple-element.28.place_ref) | copy-start | bytes 6148

commit v7 on v5

--- a/solution.py
+++ b/solution.py
@@ -71,14 +71,14 @@
         z_tables.append(np.stack([columns_at(m, rows, wanted) for m in z_kinds]))
     x_tables = []
     for b in range(x_count):
-        wanted = np.concatenate([x_len * b + part for part in x_parts])
+        wanted = np.concatenate([x_len * b + part for part in x_parts(b)])
         rows = np.arange(x_len) + x_len * b
         x_tables.append(np.stack([columns_at(m, rows, wanted) for m in x_kinds]))
     z_tables, z_inverse = unique_tables(z_tables)
     x_tables, x_inverse = unique_tables(x_tables)
     kinds = len(z_kinds)
     parts, start = [], 0
-    for part in x_parts:
+    for part in x_parts(0):
         piece = x_tables[:, :, :, start : start + len(part)]
         start += len(part)
         full = np.einsum("rkzi,bkxj->rbkzxij", z_tables, piece)
@@ -233,11 +233,14 @@
     return high, low
 
 
-def mix_lines(table_ref, parts):
-    value = jnp.concatenate(parts, axis=0)
+def mix_lines(index_ref, tables_ref, table_ref, sem, lines_of):
+    copy = pltpu.make_async_copy(tables_ref.at[index_ref[0]], table_ref, sem)
+    copy.start()
+    value = jnp.concatenate(lines_of(), axis=0)
     high, low = split(value)
+    copy.wait()
     return jnp.dot(
-        table_ref[0], jnp.concatenate([high, low, high], axis=0), preferred_element_type=F32
+        table_ref[...], jnp.concatenate([high, low, high], axis=0), preferred_element_type=F32
     )
 
 
@@ -252,27 +255,29 @@
             out_ref[rows, LO : 2 * LO] = low
 
 
-def window_lines(own_ref, near_refs, left_ref, right_ref):
+def window_lines(own_ref, near_refs, first_ref, second_ref):
     lines = [own_ref[...]]
     for ref in near_refs:
         lines += decode(ref[...], 1)
-    for ref in (left_ref, right_ref):
+    for ref in (first_ref, second_ref):
         lines += decode(ref[...], len(near_refs) + 1)
     return lines
 
 
-def target_kernel(lines, _, table_ref, own_ref, *refs):
-    *near_refs, left_ref, right_ref, out_ref, exact_ref = refs
-    mixed = mix_lines(table_ref, window_lines(own_ref, near_refs, left_ref, right_ref))
+def target_kernel(lines, index_ref, tables_ref, own_ref, *refs):
+    *near_refs, first_ref, second_ref, out_ref, exact_ref, table_ref, sem = refs
+    window = functools.partial(window_lines, own_ref, near_refs, first_ref, second_ref)
+    mixed = mix_lines(index_ref, tables_ref, table_ref, sem, window)
     grad_x = line_blur(mixed[0:lines], False)
     grad_y = line_blur(mixed[lines : 2 * lines], True)
     grad_z = line_blur(mixed[2 * lines : 3 * lines], False)
     store_fields([grad_x, grad_y, grad_z], lines, out_ref, exact_ref)
 
 
-def model_kernel(lines, _, table_ref, target_ref, own_ref, *refs):
-    *near_refs, left_ref, right_ref, out_ref, exact_ref, sum_ref = refs
-    smooth = mix_lines(table_ref, window_lines(own_ref, near_refs, left_ref, right_ref))
+def model_kernel(lines, index_ref, tables_ref, target_ref, own_ref, *refs):
+    *near_refs, first_ref, second_ref, out_ref, exact_ref, sum_ref, table_ref, sem = refs
+    window = functools.partial(window_lines, own_ref, near_refs, first_ref, second_ref)
+    smooth = mix_lines(index_ref, tables_ref, table_ref, sem, window)
     model = smooth[3 * lines :]
     target = target_ref[...]
     sums = [jnp.sum(model * target), jnp.sum(model * model), jnp.sum(target * target)]
@@ -438,26 +443,17 @@
 
 
 def call_at(kernel, out_shape, index, table, *args, name=None, macs=0):
-    def whole(shape):
-        return pl.BlockSpec(shape, lambda i, s: (0,) * len(shape))
-
-    single = not isinstance(out_shape, list)
-    outs = [out_shape] if single else out_shape
-    specs = [whole(o.shape) for o in outs]
-    return pl.pallas_call(
+    vmem = pl.BlockSpec(memory_space=pltpu.VMEM)
+    return call(
         kernel,
-        out_shape=out_shape,
-        grid_spec=pltpu.PrefetchScalarGridSpec(
-            num_scalar_prefetch=1,
-            grid=(1,),
-            in_specs=[pl.BlockSpec((1,) + table.shape[1:], lambda i, s: (s[0], 0, 0))]
-            + [whole(a.shape) for a in args],
-            out_specs=specs[0] if single else specs,
-        ),
-        compiler_params=pltpu.CompilerParams(vmem_limit_bytes=VMEM_BYTES),
-        cost_estimate=cost(macs, 4 * sum(a.size for a in args)),
+        out_shape,
+        index, table, *args,
+        in_specs=[pl.BlockSpec(memory_space=pltpu.SMEM), pl.BlockSpec(memory_space=pl.ANY)]
+        + [vmem] * len(args),
+        scratch=[pltpu.VMEM(table.shape[1:], table.dtype), pltpu.SemaphoreType.DMA],
         name=name,
-    )(index, table, *args)
+        macs=macs,
+    )
 
 
 def looked_up(values, position):
@@ -473,6 +469,19 @@
     size = lax.axis_size(axis)
     pairs = [(i, i + step) for i in range(size) if 0 <= i + step < size]
     return lax.ppermute(value, axis, pairs)
+
+
+def paired(own, left, right):
+    return lambda b: [own, right, left] if b % 2 == 0 else [own, left, right]
+
+
+def swapped(first, second):
+    size = lax.axis_size("brick")
+    found = []
+    for value, start in ((first, 0), (second, 1)):
+        pairs = [(i, i + 1) for i in range(start, size - 1, 2)]
+        found.append(lax.ppermute(value, "brick", pairs + [(j, i) for i, j in pairs]))
+    return found
 
 
 def relay_blocks(value, reach):
@@ -523,12 +532,12 @@
     target_table, tz, tx, tn = weight_table(
         [gz, gz, dz], [dx, gx, gx], planes, relay_count, relay_order(relay_count, reach_one),
         columns, brick_count,
-        [np.arange(columns), np.arange(-KR, 0), np.arange(columns, columns + KR)],
+        paired(np.arange(columns), np.arange(-KR, 0), np.arange(columns, columns + KR)),
     )
     model_table, mz, mx, mn = weight_table(
         [gz @ gz, gz @ gz, dz @ gz, gz], [dx @ gx, gx @ gx, gx @ gx, gx],
         planes, relay_count, relay_order(relay_count, reach_two), columns, brick_count,
-        [np.arange(columns), np.arange(-columns, 0), np.arange(columns, 2 * columns)],
+        paired(np.arange(columns), np.arange(-columns, 0), np.arange(columns, 2 * columns)),
     )
     r, b = lax.axis_index("relay"), lax.axis_index("brick")
     target_index = (looked_up(tz, r) * tn + looked_up(tx, b)).reshape(1)
@@ -540,8 +549,11 @@
     by_column = [t.reshape(-1, columns, rows + SCALE_LANES) for t in target_blocks]
     left_edge = jnp.concatenate([t[:, columns - KR :] for t in by_column], axis=0)
     right_edge = jnp.concatenate([t[:, :KR] for t in by_column], axis=0)
-    from_left = shifted(left_edge.reshape(-1, rows + SCALE_LANES), "brick", 1)
-    from_right = shifted(right_edge.reshape(-1, rows + SCALE_LANES), "brick", -1)
+    first_edge = jnp.where(b % 2 == 0, left_edge, right_edge)
+    second_edge = jnp.where(b % 2 == 0, right_edge, left_edge)
+    target_near = swapped(
+        first_edge.reshape(-1, rows + SCALE_LANES), second_edge.reshape(-1, rows + SCALE_LANES)
+    )
 
     hbm = pl.BlockSpec(memory_space=pltpu.HBM)
     packed = [frag_brick.reshape(1, frags), frag_angle, bead_cell, bead_weight, bead_arm]
@@ -560,15 +572,15 @@
     )
     got = lax.all_to_all(sent, "brick", split_axis=0, concat_axis=0, tiled=True)
     smooth, coded = call(
-        functools.partial(splat_kernel, lines, min(32, slots)),
+        functools.partial(splat_kernel, lines, min(64, slots)),
         [jax.ShapeDtypeStruct((lines, rows), F32), words],
         got,
         scratch=[pltpu.VMEM((his, LO), F32)],
         name="splat",
         macs=slots * beads * his * LO,
     )
-    coded, from_left, from_right = lax.optimization_barrier((coded, from_left, from_right))
-    target_parts = [target_lines] + target_blocks[1:] + [from_left, from_right]
+    coded, *target_near = lax.optimization_barrier((coded, *target_near))
+    target_parts = [target_lines] + target_blocks[1:] + target_near
     blocks = relay_blocks(coded, reach_two)
     field_shapes = [
         jax.ShapeDtypeStruct((3 * his, 2 * LO), BF16),
@@ -600,7 +612,7 @@
     )
     beside = jnp.concatenate(blocks, axis=0)
     model_parts = [smooth] + blocks[1:]
-    model_parts += [shifted(beside, "brick", 1), shifted(beside, "brick", -1)]
+    model_parts += swapped(beside, beside)
     target_second = sample(target_field, half, slots - half, "target_sample_b")
     target_second, *model_parts = lax.optimization_barrier((target_second, *model_parts))
     *model_field, partial = call_at(

time: 64.4 us -> 62.3 us (0.967)
  starting transfers between devices: 19.4 us -> 14 us
  waiting for transfers between devices: 5.18 us -> 7.61 us
    ppermute x4, starting transfers between devices: 8.25 us -> 2.88 us  [swapped(): lax.ppermute(value, 'brick', pairs + [(j, i) for i, j in pairs])]
    pallas_call x8 -> x10, Pallas kernels: 23.8 us -> 27.5 us  [call(): pl.pallas_call(kernel, out_shape=out_shape, scratch_shapes=list(scratch),...]
    pallas_call x2 -> x0, Pallas kernels: 3.4 us -> none  [call_at(): pl.pallas_call(kernel, out_shape=out_shape, grid_spec=pltpu.PrefetchScala...]
    all_to_all x1, waiting for transfers between devices: 5.16 us -> 7.59 us  [shards(): got = lax.all_to_all(sent, 'brick', split_axis=0, concat_axis=0, tiled=True)]
  transfers between devices with their start and end apart: 8 -> 8, of which waited for: 1 -> 1; matrix products, arithmetic and copies ran while one was open for 0% -> 0% of each run, Pallas kernels for 38% -> 39%
where the time goes in v7:
time: 62.3 us; the launch traced here: 62 us
  Pallas kernels  27.5 us (44%)
  starting transfers between devices  14 us (22%)
  blocking collectives  11.5 us (18%)
  waiting for transfers between devices  7.61 us (12%)
  local copies, waits for them, and re-layouts  1.08 us (2%)
    pallas_call x10, Pallas kernels, call(): pl.pallas_call(kernel, out_shape=out_shape, scratch_shapes=list(scratch),...  27.5 us
    all_to_all x1, blocking collectives, shards(): lax.all_to_all(leaving, 'brick', split_axis=0, concat_axis=0, tiled=True)  11.5 us
    all_to_all x1, waiting for transfers between devices, shards(): got = lax.all_to_all(sent, 'brick', split_axis=0, concat_axis=0, tiled=True)  7.59 us
    all_to_all x1, starting transfers between devices, shards(): got = lax.all_to_all(sent, 'brick', split_axis=0, concat_axis=0, tiled=True)  5.92 us
    ppermute x2, starting transfers between devices, relay_blocks(): return [value, lax.ppermute(value, 'relay', [(0, 1), (1, 0)])]  3.59 us
    ppermute x4, starting transfers between devices, swapped(): lax.ppermute(value, 'brick', pairs + [(j, i) for i, j in pairs])  2.88 us
    ppermute x1, starting transfers between devices, relay_total(): lax.ppermute(moving, 'relay', [(i, (i + 1) % size) for i in range(size)])  1.6 us
  transfers between devices with their start and end apart: 8, of which 1 were waited for; matrix products, arithmetic and copies ran while one was open for 0% of the time, Pallas kernels for 39%

profile of v7, /device:TPU:0, one launch (start us, length us, event | category | flops | bytes accessed | tf_op | source)
XLA Modules:
  0.0 62.0 jit_solution(5554155547846913011)
XLA Ops:
  0.0 0.9 %copy-done = f32[4,8,1536]{2,1,0:T(8,128)S(1)} copy-done((f32[4,8,1536]{2,1,0:T(8,128)S(1)}, f32[4,8,1536]{2,1,0:T(8,128)}, u32[]{:S(2)}) %copy-start) | copy-done | bytes 196632
  0.9 0.2 encode.1
  1.2 3.0 %collective-permute-start = (s32[16,1664]{1,0:T(8,128)S(1)}, s32[16,1664]{1,0:T(8,128)S(1)}, u32[]{:S(2)}, u32[]{:S(2)}) collective-permute-start(s32[16,1664]{1,0:T(8,128)S(1)} %encode.1), channel_id=1, source_target_pairs={{0,1},{1,0},{2,3},{3,2},{4,5},{5,4},{6,7},{7,6},{8,9},{9,8},{10,11... | collective-permute-start | bytes 319496 | tf_op jit(solution)/shard_map/ppermute | solution.py:490
  4.2 2.1 %pack.1 = (s32[128,384]{1,0:T(8,128)}, s32[8,64]{1,0:T(8,128)}) custom-call(s32[1,64]{1,0:T(1,128)} %bitcast.23, f32[3,64]{1,0:T(4,128)} %refs_1_.1, s32[64,128]{1,0:T(8,128)} %refs_2_.1, bf16[64,128]{1,0:T(8,128)(2,1)} %refs_3_.1, f32[3,64,128]{2,1,0:T(8,128)} %refs_4_.1), custom_call_target="tpu_custom_call" | custom-call | bytes 164864 | tf_op jit(solution)/shard_map/pack/pallas_call | solution.py:434
  6.3 5.9 %all-to-all-start = ((s32[16,8,384]{2,1,0:T(8,128)}), s32[16,8,384]{2,1,0:T(8,128)S(1)}, u32[]{:S(2)}, u32[]{:S(2)}) async-start(s32[16,8,384]{2,1,0:T(8,128)} %bitcast.22), calls=%async_computation | async-start | bytes 393216 | tf_op jit(solution)/shard_map/all_to_all | solution.py:573
  12.4 0.0 collective-permute-done.refs_0_
  12.5 0.5 collective-permute-start.1
  13.0 0.7 %collective-permute-start.2 = (s32[16,1664]{1,0:T(8,128)S(1)}, s32[16,1664]{1,0:T(8,128)S(1)}, u32[]{:S(2)}, u32[]{:S(2)}) collective-permute-start(s32[16,1664]{1,0:T(8,128)S(1)} %select_n.34), channel_id=1, source_target_pairs={{2,4},{6,8},{10,12},{14,16},{18,20},{22,24},{26,28},{4,2},{8,6},{1... | collective-permute-start | bytes 319496 | tf_op jit(solution)/shard_map/ppermute | solution.py:483
  13.7 7.6 %all-to-all-done = s32[16,8,384]{2,1,0:T(8,128)S(1)} async-done(((s32[16,8,384]{2,1,0:T(8,128)}), s32[16,8,384]{2,1,0:T(8,128)S(1)}, u32[]{:S(2)}, u32[]{:S(2)}) %all-to-all-start) | async-done | bytes 196640 | tf_op jit(solution)/shard_map/all_to_all | solution.py:573
  21.3 3.8 %splat.1 = (f32[32,1536]{1,0:T(8,128)S(1)}, s32[16,1664]{1,0:T(8,128)S(1)}) custom-call(s32[128,384]{1,0:T(8,128)S(1)} %bitcast.16), custom_call_target="tpu_custom_call" | custom-call | flops 1610612736 | bytes 196608 | tf_op jit(solution)/shard_map/splat/pallas_call | solution.py:434
  25.1 0.0 collective-permute-done.1.refs_1_
  25.1 0.0 collective-permute-done.2.refs_2_
  25.1 0.6 collective-permute-start.3
  25.7 0.0 copy-done.1
  25.7 0.0 copy-done.3
  25.7 1.9 %target_fields.1 = (bf16[576,512]{1,0:T(8,128)(2,1)S(1)}, f32[96,1536]{1,0:T(8,128)S(1)}) custom-call(s32[1]{0:T(128)} %bitcast.6.index_ref, bf16[8,96,384]{2,1,0:T(8,128)(2,1)S(1)} %copy-done.3, f32[32,1536]{1,0:T(8,128)S(1)} %bitcast.12, s32[16,1664]{1,0:T(8,128)S(1)} %collective-permute-done.refs_0_, s32[16,1664]{1,0:T(8,128)S(1)} %collective-permute-done.1.refs_1_, ...), custom_call_target="tpu_custom_call" | custom-call | flops 113246208 | bytes 1695748 | tf_op jit(solution)/shard_map/target_fields/pallas_call | solution.py:434
  27.5 4.1 %target_sample_a.1.first_ref = f32[64,128]{1,0:T(8,128)S(1)} custom-call(s32[128,384]{1,0:T(8,128)S(1)} %bitcast.17, bf16[576,512]{1,0:T(8,128)(2,1)S(1)} %get-tuple-element.36.field_ref, f32[96,1536]{1,0:T(8,128)S(1)} %get-tuple-element.37.exact_ref), custom_call_target="tpu_custom_call" | custom-call | flops 4831838208 | bytes 1966080 | tf_op jit(solution)/shard_map/target_sample_a/pallas_call | solution.py:434
  31.6 0.0 collective-permute-done.3.refs_0_
  31.7 0.0 copy-start.2
  31.7 1.0 %collective-permute-start.5 = (s32[32,1664]{1,0:T(8,128)S(1)}, s32[32,1664]{1,0:T(8,128)S(1)}, u32[]{:S(2)}, u32[]{:S(2)}) collective-permute-start(s32[32,1664]{1,0:T(8,128)S(1)} %constant_dynamic-update-slice_fusion), channel_id=1, source_target_pairs={{2,4},{6,8},{10,12},{14,16},{18,20},{22,24},{26,28},{4,2},{8,6},{1... | collective-permute-start | bytes 638984 | tf_op jit(solution)/shard_map/ppermute | solution.py:483
  32.7 0.8 %collective-permute-start.4 = (s32[32,1664]{1,0:T(8,128)S(1)}, s32[32,1664]{1,0:T(8,128)S(1)}, u32[]{:S(2)}, u32[]{:S(2)}) collective-permute-start(s32[32,1664]{1,0:T(8,128)S(1)} %constant_dynamic-update-slice_fusion), channel_id=1, source_target_pairs={{0,2},{4,6},{8,10},{12,14},{16,18},{20,22},{24,26},{28,30},{2,0},{... | collective-permute-start | bytes 638984 | tf_op jit(solution)/shard_map/ppermute | solution.py:483
  33.5 4.1 %target_sample_b.1.second_ref = f32[64,128]{1,0:T(8,128)S(1)} custom-call(s32[128,384]{1,0:T(8,128)S(1)} %bitcast.18, bf16[576,512]{1,0:T(8,128)(2,1)S(1)} %get-tuple-element.36.field_ref, f32[96,1536]{1,0:T(8,128)S(1)} %get-tuple-element.37.exact_ref), custom_call_target="tpu_custom_call" | custom-call | flops 4831838208 | bytes 1966080 | tf_op jit(solution)/shard_map/target_sample_b/pallas_call | solution.py:434
  37.6 0.0 collective-permute-done.5.refs_2_
  37.6 0.0 collective-permute-done.4.refs_1_
  37.6 0.0 copy-done.2
  37.6 2.2 %model_fields.1 = (bf16[576,512]{1,0:T(8,128)(2,1)S(1)}, f32[96,1536]{1,0:T(8,128)S(1)}, f32[8,128]{1,0:T(8,128)S(1)}) custom-call(s32[1]{0:T(128)} %bitcast.6.index_ref, bf16[8,128,576]{2,1,0:T(8,128)(2,1)S(1)} %copy-done.2, f32[32,1536]{1,0:T(8,128)S(1)} %bitcast.13, f32[32,1536]{1,0:T(8,128)S(1)} %get-tuple-element.42.own_ref, ...), custom_call_target="tpu_custom_call" | custom-call | bytes 3284996 | tf_op jit(solution)/shard_map/model_fields/pallas_call | solution.py:434
  39.8 1.6 %collective-permute-start.6 = (f32[8,128]{1,0:T(8,128)S(1)}, f32[8,128]{1,0:T(8,128)S(1)}, u32[]{:S(2)}, u32[]{:S(2)}) collective-permute-start(f32[8,128]{1,0:T(8,128)S(1)} %get-tuple-element.48), channel_id=1, source_target_pairs={{0,1},{1,0},{2,3},{3,2},{4,5},{5,4},{6,7},{7,6},{8,9},{9,8},{10,11... | collective-permute-start | bytes 12296 | tf_op jit(solution)/shard_map/ppermute | solution.py:510
  41.4 8.1 %model_sample.1.model_ref = f32[128,128]{1,0:T(8,128)S(1)} custom-call(s32[128,384]{1,0:T(8,128)S(1)} %bitcast.19, bf16[576,512]{1,0:T(8,128)(2,1)S(1)} %get-tuple-element.46.field_ref, f32[96,1536]{1,0:T(8,128)S(1)} %get-tuple-element.47.exact_ref), custom_call_target="tpu_custom_call" | custom-call | flops 9663676416 | bytes 1966080 | tf_op jit(solution)/shard_map/model_sample/pallas_call | solution.py:434
  49.5 0.0 collective-permute-done.6
  49.5 0.2 join.1
  49.6 11.5 %all_to_all.22 = f32[16,1,128]{2,1,0:T(1,128)S(1)} all-to-all(f32[16,1,128]{2,1,0:T(1,128)S(1)} %bitcast.20), channel_id=1, replica_groups=mesh['brick'=16,'relay'=2] {'brick'}, dimensions={0} | all-to-all | bytes 16384 | tf_op jit(solution)/shard_map/all_to_all | solution.py:632
  61.1 0.9 %finish.1 = f32[6,64]{1,0:T(8,128)} custom-call(s32[8,64]{1,0:T(8,128)S(1)} %copy-done.4, f32[16,128]{1,0:T(8,128)S(1)} %bitcast.21), custom_call_target="tpu_custom_call" | custom-call | bytes 10240 | tf_op jit(solution)/shard_map/finish/pallas_call | solution.py:434
  (13 shorter events, 0.2 us)
Async XLA Ops:
  0.0 0.9 %copy-start = (f32[4,8,1536]{2,1,0:T(8,128)S(1)}, f32[4,8,1536]{2,1,0:T(8,128)}, u32[]{:S(2)}) copy-start(f32[4,8,1536]{2,1,0:T(8,128)} %param.8) | copy-start | bytes 589828
  1.2 11.2 %collective-permute-start = (s32[16,1664]{1,0:T(8,128)S(1)}, s32[16,1664]{1,0:T(8,128)S(1)}, u32[]{:S(2)}, u32[]{:S(2)}) collective-permute-start(s32[16,1664]{1,0:T(8,128)S(1)} %encode.1), channel_id=1, source_target_pairs={{0,1},{1,0},{2,3},{3,2},{4,5},{5,4},{6,7},{7,6},{8,9},{9,8},{10,11... | collective-permute-start | bytes 319496 | tf_op jit(solution)/shard_map/ppermute | solution.py:490
  6.3 14.9 %all-to-all-start = ((s32[16,8,384]{2,1,0:T(8,128)}), s32[16,8,384]{2,1,0:T(8,128)S(1)}, u32[]{:S(2)}, u32[]{:S(2)}) async-start(s32[16,8,384]{2,1,0:T(8,128)} %bitcast.22), calls=%async_computation | async-start | bytes 393216 | tf_op jit(solution)/shard_map/all_to_all | solution.py:573
  12.5 12.6 %collective-permute-start.1 = (s32[16,1664]{1,0:T(8,128)S(1)}, s32[16,1664]{1,0:T(8,128)S(1)}, u32[]{:S(2)}, u32[]{:S(2)}) collective-permute-start(s32[16,1664]{1,0:T(8,128)S(1)} %select_n.32), channel_id=1, source_target_pairs={{0,2},{4,6},{8,10},{12,14},{16,18},{20,22},{24,26},{28,30},{2,0},{... | collective-permute-start | bytes 319496 | tf_op jit(solution)/shard_map/ppermute | solution.py:483
  13.0 12.1 %collective-permute-start.2 = (s32[16,1664]{1,0:T(8,128)S(1)}, s32[16,1664]{1,0:T(8,128)S(1)}, u32[]{:S(2)}, u32[]{:S(2)}) collective-permute-start(s32[16,1664]{1,0:T(8,128)S(1)} %select_n.34), channel_id=1, source_target_pairs={{2,4},{6,8},{10,12},{14,16},{18,20},{22,24},{26,28},{4,2},{8,6},{1... | collective-permute-start | bytes 319496 | tf_op jit(solution)/shard_map/ppermute | solution.py:483
  21.3 4.4 %copy-start.1 = (f32[4,8,1536]{2,1,0:T(8,128)S(1)}, f32[4,8,1536]{2,1,0:T(8,128)}, u32[]{:S(2)}) copy-start(f32[4,8,1536]{2,1,0:T(8,128)} %param.8) | copy-start | bytes 589828
  21.3 4.4 %copy-start.3 = (bf16[8,96,384]{2,1,0:T(8,128)(2,1)S(1)}, bf16[8,96,384]{2,1,0:T(8,128)(2,1)}, u32[]{:S(2)}) copy-start(bf16[8,96,384]{2,1,0:T(8,128)(2,1)} %constant.68.clone.tables_ref) | copy-start | bytes 1769476
  25.1 6.5 %collective-permute-start.3 = (s32[16,1664]{1,0:T(8,128)S(1)}, s32[16,1664]{1,0:T(8,128)S(1)}, u32[]{:S(2)}, u32[]{:S(2)}) collective-permute-start(s32[16,1664]{1,0:T(8,128)S(1)} %get-tuple-element.40), channel_id=1, source_target_pairs={{0,1},{1,0},{2,3},{3,2},{4,5},{5,4},{6,7},{7,6},{8,9},{9,8},{10,11... | collective-permute-start | bytes 319496 | tf_op jit(solution)/shard_map/ppermute | solution.py:490
  31.7 5.9 %copy-start.2 = (bf16[8,128,576]{2,1,0:T(8,128)(2,1)S(1)}, bf16[8,128,576]{2,1,0:T(8,128)(2,1)}, u32[]{:S(2)}) copy-start(bf16[8,128,576]{2,1,0:T(8,128)(2,1)} %constant.69.clone.tables_ref) | copy-start | bytes 3538948
  31.7 5.9 %collective-permute-start.5 = (s32[32,1664]{1,0:T(8,128)S(1)}, s32[32,1664]{1,0:T(8,128)S(1)}, u32[]{:S(2)}, u32[]{:S(2)}) collective-permute-start(s32[32,1664]{1,0:T(8,128)S(1)} %constant_dynamic-update-slice_fusion), channel_id=1, source_target_pairs={{2,4},{6,8},{10,12},{14,16},{18,20},{22,24},{26,28},{4,2},{8,6},{1... | collective-permute-start | bytes 638984 | tf_op jit(solution)/shard_map/ppermute | solution.py:483
  32.7 4.9 %collective-permute-start.4 = (s32[32,1664]{1,0:T(8,128)S(1)}, s32[32,1664]{1,0:T(8,128)S(1)}, u32[]{:S(2)}, u32[]{:S(2)}) collective-permute-start(s32[32,1664]{1,0:T(8,128)S(1)} %constant_dynamic-update-slice_fusion), channel_id=1, source_target_pairs={{0,2},{4,6},{8,10},{12,14},{16,18},{20,22},{24,26},{28,30},{2,0},{... | collective-permute-start | bytes 638984 | tf_op jit(solution)/shard_map/ppermute | solution.py:483
  39.8 9.7 %collective-permute-start.6 = (f32[8,128]{1,0:T(8,128)S(1)}, f32[8,128]{1,0:T(8,128)S(1)}, u32[]{:S(2)}, u32[]{:S(2)}) collective-permute-start(f32[8,128]{1,0:T(8,128)S(1)} %get-tuple-element.48), channel_id=1, source_target_pairs={{0,1},{1,0},{2,3},{3,2},{4,5},{5,4},{6,7},{7,6},{8,9},{9,8},{10,11... | collective-permute-start | bytes 12296 | tf_op jit(solution)/shard_map/ppermute | solution.py:510
  41.4 19.8 %copy-start.4 = (s32[8,64]{1,0:T(8,128)S(1)}, s32[8,64]{1,0:T(8,128)}, u32[]{:S(2)}) copy-start(s32[8,64]{1,0:T(8,128)} %get-tuple-element.27.place_ref) | copy-start | bytes 6148

commit v8 on v6

--- a/solution.py
+++ b/solution.py
@@ -71,14 +71,14 @@
         z_tables.append(np.stack([columns_at(m, rows, wanted) for m in z_kinds]))
     x_tables = []
     for b in range(x_count):
-        wanted = np.concatenate([x_len * b + part for part in x_parts])
+        wanted = np.concatenate([x_len * b + part for part in x_parts(b)])
         rows = np.arange(x_len) + x_len * b
         x_tables.append(np.stack([columns_at(m, rows, wanted) for m in x_kinds]))
     z_tables, z_inverse = unique_tables(z_tables)
     x_tables, x_inverse = unique_tables(x_tables)
     kinds = len(z_kinds)
     parts, start = [], 0
-    for part in x_parts:
+    for part in x_parts(0):
         piece = x_tables[:, :, :, start : start + len(part)]
         start += len(part)
         full = np.einsum("rkzi,bkxj->rbkzxij", z_tables, piece)
@@ -250,18 +250,18 @@
             out_ref[rows, LO : 2 * LO] = low
 
 
-def window_lines(own_ref, near_refs, left_ref, right_ref):
+def window_lines(own_ref, near_refs, first_ref, second_ref):
     lines = [own_ref[...]]
     for ref in near_refs:
         lines += decode(ref[...], 1)
-    for ref in (left_ref, right_ref):
+    for ref in (first_ref, second_ref):
         lines += decode(ref[...], len(near_refs) + 1)
     return lines
 
 
 def target_kernel(lines, _, table_ref, own_ref, *refs):
-    *near_refs, left_ref, right_ref, out_ref, exact_ref = refs
-    mixed = mix_lines(table_ref, window_lines(own_ref, near_refs, left_ref, right_ref))
+    *near_refs, first_ref, second_ref, out_ref, exact_ref = refs
+    mixed = mix_lines(table_ref, window_lines(own_ref, near_refs, first_ref, second_ref))
     grad_x = line_blur(mixed[0:lines], False)
     grad_y = line_blur(mixed[lines : 2 * lines], True)
     grad_z = line_blur(mixed[2 * lines : 3 * lines], False)
@@ -269,8 +269,8 @@
 
 
 def model_kernel(lines, _, table_ref, target_ref, own_ref, *refs):
-    *near_refs, left_ref, right_ref, out_ref, exact_ref, sum_ref = refs
-    smooth = mix_lines(table_ref, window_lines(own_ref, near_refs, left_ref, right_ref))
+    *near_refs, first_ref, second_ref, out_ref, exact_ref, sum_ref = refs
+    smooth = mix_lines(table_ref, window_lines(own_ref, near_refs, first_ref, second_ref))
     model = smooth[3 * lines :]
     target = target_ref[...]
     sums = [jnp.sum(model * target), jnp.sum(model * model), jnp.sum(target * target)]
@@ -376,8 +376,7 @@
     out_ref[...] = total
 
 
-def join_kernel(most, *refs):
-    *target_refs, model_ref, sum_ref, out_ref = refs
+def join_kernel(most, first_ref, second_ref, model_ref, sum_ref, out_ref):
     bricks = out_ref.shape[0]
     lane = lax.broadcasted_iota(I32, out_ref.shape, 1)
     sums = sum_ref[0:1, :]
@@ -385,9 +384,8 @@
         sums = sums + sum_ref[8 * k : 8 * k + 1, :]
     total = jnp.zeros(out_ref.shape, F32)
     for k in range(most):
-        rows = pl.ds(k, bricks, stride=most)
-        parts = [ref[pl.ds(k, ref.shape[0] // most, stride=most), :] for ref in target_refs]
-        own = jnp.concatenate(parts, axis=0)
+        rows, half = pl.ds(k, bricks, stride=most), pl.ds(k, bricks // 2, stride=most)
+        own = jnp.concatenate([first_ref[half, :], second_ref[half, :]], axis=0)
         own = jnp.where(lane < 6, own, 0.0)
         own = own + pltpu.roll(jnp.where(lane < 6, model_ref[rows, :], 0.0), 6, 1)
         if k == 0:
@@ -475,6 +473,19 @@
     return lax.ppermute(value, axis, pairs)
 
 
+def paired(own, left, right):
+    return lambda b: [own, right, left] if b % 2 == 0 else [own, left, right]
+
+
+def swapped(first, second):
+    size = lax.axis_size("brick")
+    found = []
+    for value, start in ((first, 0), (second, 1)):
+        pairs = [(i, i + 1) for i in range(start, size - 1, 2)]
+        found.append(lax.ppermute(value, "brick", pairs + [(j, i) for i, j in pairs]))
+    return found
+
+
 def relay_blocks(value, reach):
     size = lax.axis_size("relay")
     if size == 2:
@@ -523,12 +534,12 @@
     target_table, tz, tx, tn = weight_table(
         [gz, gz, dz], [dx, gx, gx], planes, relay_count, relay_order(relay_count, reach_one),
         columns, brick_count,
-        [np.arange(columns), np.arange(-KR, 0), np.arange(columns, columns + KR)],
+        paired(np.arange(columns), np.arange(-KR, 0), np.arange(columns, columns + KR)),
     )
     model_table, mz, mx, mn = weight_table(
         [gz @ gz, gz @ gz, dz @ gz, gz], [dx @ gx, gx @ gx, gx @ gx, gx],
         planes, relay_count, relay_order(relay_count, reach_two), columns, brick_count,
-        [np.arange(columns), np.arange(-columns, 0), np.arange(columns, 2 * columns)],
+        paired(np.arange(columns), np.arange(-columns, 0), np.arange(columns, 2 * columns)),
     )
     r, b = lax.axis_index("relay"), lax.axis_index("brick")
     target_index = (looked_up(tz, r) * tn + looked_up(tx, b)).reshape(1)
@@ -557,8 +568,11 @@
     by_column = [t.reshape(-1, columns, rows + SCALE_LANES) for t in target_blocks]
     left_edge = jnp.concatenate([t[:, columns - KR :] for t in by_column], axis=0)
     right_edge = jnp.concatenate([t[:, :KR] for t in by_column], axis=0)
-    from_left = shifted(left_edge.reshape(-1, rows + SCALE_LANES), "brick", 1)
-    from_right = shifted(right_edge.reshape(-1, rows + SCALE_LANES), "brick", -1)
+    first_edge = jnp.where(b % 2 == 0, left_edge, right_edge)
+    second_edge = jnp.where(b % 2 == 0, right_edge, left_edge)
+    target_near = swapped(
+        first_edge.reshape(-1, rows + SCALE_LANES), second_edge.reshape(-1, rows + SCALE_LANES)
+    )
 
     got = lax.all_to_all(sent, "brick", split_axis=0, concat_axis=0, tiled=True)
     smooth, coded = call(
@@ -569,8 +583,8 @@
         name="splat",
         macs=slots * beads * his * LO,
     )
-    coded, from_left, from_right = lax.optimization_barrier((coded, from_left, from_right))
-    target_parts = [target_lines] + target_blocks[1:] + [from_left, from_right]
+    coded, *target_near = lax.optimization_barrier((coded, *target_near))
+    target_parts = [target_lines] + target_blocks[1:] + target_near
     blocks = relay_blocks(coded, reach_two)
     field_shapes = [
         jax.ShapeDtypeStruct((3 * his, 2 * LO), BF16),
@@ -595,15 +609,15 @@
             macs=6 * count * beads * his * LO,
         )
 
-    part = slots // 4
-    target_first = sample(target_field, 0, part, "target_sample_a")
+    half = slots // 2
+    target_first = sample(target_field, 0, half, "target_sample_a")
     blocks, target_first, target_field = lax.optimization_barrier(
         (blocks, target_first, target_field)
     )
     beside = jnp.concatenate(blocks, axis=0)
     model_parts = [smooth] + blocks[1:]
-    model_parts += [shifted(beside, "brick", 1), shifted(beside, "brick", -1)]
-    target_second = sample(target_field, part, slots - part, "target_sample_b")
+    model_parts += swapped(beside, beside)
+    target_second = sample(target_field, half, slots - half, "target_sample_b")
     target_second, *model_parts = lax.optimization_barrier((target_second, *model_parts))
     *model_field, partial = call_at(
         functools.partial(model_kernel, lines),

time: 67.1 us -> 61.8 us (0.921)
  starting transfers between devices: 20.3 us -> 15.1 us
  blocking collectives: 14.8 us -> 12.8 us
  waiting for transfers between devices: 4.38 us -> 5.46 us
  local copies, waits for them, and re-layouts: 0.16 us -> 1.12 us
    ppermute x4, starting transfers between devices: 9.03 us -> 3.96 us  [swapped(): lax.ppermute(value, 'brick', pairs + [(j, i) for i, j in pairs])]
    all_to_all x1, blocking collectives: 14.8 us -> 12.8 us  [shards(): lax.all_to_all(leaving, 'brick', split_axis=0, concat_axis=0, tiled=True)]
    all_to_all x1, waiting for transfers between devices: 0.61 us -> 2.58 us  [shards(): got = lax.all_to_all(sent, 'brick', split_axis=0, concat_axis=0, tiled=True)]
    slice x2, local copies, waits for them, and re-layouts: 0.04 us -> 1 us  [shards(): t[:, columns - KR:]]
    ppermute x2, waiting for transfers between devices: 3.76 us -> 2.87 us  [relay_blocks(): return [value, lax.ppermute(value, 'relay', [(0, 1), (1, 0)])]]
  transfers between devices with their start and end apart: 8 -> 8, of which waited for: 2 -> 2; matrix products, arithmetic and copies ran while one was open for 0% -> 2% of each run, Pallas kernels for 33% -> 35%
where the time goes in v8:
time: 61.8 us; the launch traced here: 61.5 us
  Pallas kernels  26.7 us (43%)
  starting transfers between devices  15.1 us (24%)
  blocking collectives  12.8 us (21%)
  waiting for transfers between devices  5.46 us (9%)
  local copies, waits for them, and re-layouts  1.12 us (2%)
    pallas_call x7, Pallas kernels, call(): pl.pallas_call(kernel, out_shape=out_shape, scratch_shapes=list(scratch),...  23.3 us
    all_to_all x1, blocking collectives, shards(): lax.all_to_all(leaving, 'brick', split_axis=0, concat_axis=0, tiled=True)  12.8 us
    all_to_all x1, starting transfers between devices, shards(): got = lax.all_to_all(sent, 'brick', split_axis=0, concat_axis=0, tiled=True)  7.38 us
    ppermute x4, starting transfers between devices, swapped(): lax.ppermute(value, 'brick', pairs + [(j, i) for i, j in pairs])  3.96 us
    pallas_call x2, Pallas kernels, call_at(): pl.pallas_call(kernel, out_shape=out_shape, grid_spec=pltpu.PrefetchScala...  3.4 us
    ppermute x2, starting transfers between devices, relay_blocks(): return [value, lax.ppermute(value, 'relay', [(0, 1), (1, 0)])]  3.15 us
    ppermute x2, waiting for transfers between devices, relay_blocks(): return [value, lax.ppermute(value, 'relay', [(0, 1), (1, 0)])]  2.87 us
    all_to_all x1, waiting for transfers between devices, shards(): got = lax.all_to_all(sent, 'brick', split_axis=0, concat_axis=0, tiled=True)  2.58 us
  transfers between devices with their start and end apart: 8, of which 2 were waited for; matrix products, arithmetic and copies ran while one was open for 2% of the time, Pallas kernels for 35%

profile of v8, /device:TPU:0, one launch (start us, length us, event | category | flops | bytes accessed | tf_op | source)
XLA Modules:
  0.0 61.5 jit_solution(15764207000145927645)
XLA Ops:
  0.0 2.2 %pack.1 = (s32[128,384]{1,0:T(8,128)}, s32[8,64]{1,0:T(8,128)}, s32[16,1664]{1,0:T(8,128)}) custom-call(s32[1,64]{1,0:T(1,128)} %bitcast.23, f32[3,64]{1,0:T(4,128)} %refs_1_.1, s32[64,128]{1,0:T(8,128)} %refs_2_.1, bf16[64,128]{1,0:T(8,128)(2,1)} %refs_3_.1, f32[3,64,128]{2,1,0:T(8,128)} %refs_4_.1, f32[32,1536]{1,0:T(8,128)} %bitcast.11), custom_call_target="tpu_custom_call" | custom-call | bytes 361472 | tf_op jit(solution)/shard_map/pack/pallas_call | solution.py:427
  2.2 7.4 %all-to-all-start = ((s32[16,8,384]{2,1,0:T(8,128)}), s32[16,8,384]{2,1,0:T(8,128)S(1)}, u32[]{:S(2)}, u32[]{:S(2)}) async-start(s32[16,8,384]{2,1,0:T(8,128)} %bitcast.21), calls=%async_computation | async-start | bytes 393216 | tf_op jit(solution)/shard_map/all_to_all | solution.py:577
  9.6 1.6 %collective-permute-start = (s32[16,1664]{1,0:T(8,128)}, s32[16,1664]{1,0:T(8,128)S(1)}, u32[]{:S(2)}, u32[]{:S(2)}) collective-permute-start(s32[16,1664]{1,0:T(8,128)} %get-tuple-element.31), channel_id=1, source_target_pairs={{0,1},{1,0},{2,3},{3,2},{4,5},{5,4},{6,7},{7,6},{8,9},{9,8},{10,11... | collective-permute-start | bytes 319496 | tf_op jit(solution)/shard_map/ppermute | solution.py:492
  11.2 1.0 %fusion.2 = (s32[2,4,1664]{2,1,0:T(4,128)S(1)}, s32[2,4,1664]{2,1,0:T(4,128)S(1)}) fusion(s32[2,8,1664]{2,1,0:T(8,128)} %bitcast.22), kind=kLoop, calls=%fused_computation.7 | loop fusion | bytes 212992 | tf_op jit(solution)/shard_map/slice | solution.py:569
  12.3 2.9 %collective-permute-done.refs_0_ = s32[16,1664]{1,0:T(8,128)S(1)} collective-permute-done((s32[16,1664]{1,0:T(8,128)}, s32[16,1664]{1,0:T(8,128)S(1)}, u32[]{:S(2)}, u32[]{:S(2)}) %collective-permute-start) | collective-permute-done | bytes 106528 | tf_op jit(solution)/shard_map/ppermute | solution.py:492
  15.3 0.1 collective-permute-start.1
  15.4 0.7 %collective-permute-start.2 = (s32[16,1664]{1,0:T(8,128)S(1)}, s32[16,1664]{1,0:T(8,128)S(1)}, u32[]{:S(2)}, u32[]{:S(2)}) collective-permute-start(s32[16,1664]{1,0:T(8,128)S(1)} %select_n.34), channel_id=1, source_target_pairs={{2,4},{6,8},{10,12},{14,16},{18,20},{22,24},{26,28},{4,2},{8,6},{1... | collective-permute-start | bytes 319496 | tf_op jit(solution)/shard_map/ppermute | solution.py:485
  16.0 2.6 %all-to-all-done = s32[16,8,384]{2,1,0:T(8,128)S(1)} async-done(((s32[16,8,384]{2,1,0:T(8,128)}), s32[16,8,384]{2,1,0:T(8,128)S(1)}, u32[]{:S(2)}, u32[]{:S(2)}) %all-to-all-start) | async-done | bytes 196640 | tf_op jit(solution)/shard_map/all_to_all | solution.py:577
  18.6 3.8 %splat.1 = (f32[32,1536]{1,0:T(8,128)S(1)}, s32[16,1664]{1,0:T(8,128)S(1)}) custom-call(s32[128,384]{1,0:T(8,128)S(1)} %bitcast.15), custom_call_target="tpu_custom_call" | custom-call | flops 1610612736 | bytes 196608 | tf_op jit(solution)/shard_map/splat/pallas_call | solution.py:427
  22.5 0.0 collective-permute-done.1.refs_1_
  22.5 0.0 collective-permute-done.2.refs_2_
  22.5 1.6 %collective-permute-start.3 = (s32[16,1664]{1,0:T(8,128)S(1)}, s32[16,1664]{1,0:T(8,128)S(1)}, u32[]{:S(2)}, u32[]{:S(2)}) collective-permute-start(s32[16,1664]{1,0:T(8,128)S(1)} %get-tuple-element.42), channel_id=1, source_target_pairs={{0,1},{1,0},{2,3},{3,2},{4,5},{5,4},{6,7},{7,6},{8,9},{9,8},{10,11... | collective-permute-start | bytes 319496 | tf_op jit(solution)/shard_map/ppermute | solution.py:492
  24.1 0.0 copy-done
  24.1 0.0 copy-done.2
  24.1 1.7 %target_fields.1 = (bf16[576,512]{1,0:T(8,128)(2,1)S(1)}, f32[96,1536]{1,0:T(8,128)S(1)}) custom-call(s32[1]{0:T(128)} %bitcast.6._, bf16[8,96,384]{2,1,0:T(8,128)(2,1)S(1)} %copy-done.2, f32[32,1536]{1,0:T(8,128)S(1)} %bitcast.12, s32[16,1664]{1,0:T(8,128)S(1)} %collective-permute-done.refs_0_, s32[16,1664]{1,0:T(8,128)S(1)} %collective-permute-done.1.refs_1_, ...), custom_call_target="tpu_custom_call" | custom-call | flops 113246208 | bytes 516096 | tf_op jit(solution)/shard_map/target_fields/pallas_call | solution.py:445
  25.7 4.1 %target_sample_a.1.first_ref = f32[64,128]{1,0:T(8,128)S(1)} custom-call(s32[128,384]{1,0:T(8,128)S(1)} %bitcast.16, bf16[576,512]{1,0:T(8,128)(2,1)S(1)} %get-tuple-element.38.field_ref, f32[96,1536]{1,0:T(8,128)S(1)} %get-tuple-element.39.exact_ref), custom_call_target="tpu_custom_call" | custom-call | flops 4831838208 | bytes 1966080 | tf_op jit(solution)/shard_map/target_sample_a/pallas_call | solution.py:427
  29.8 0.0 collective-permute-done.3.refs_0_
  29.9 0.0 copy-start.1
  29.9 1.0 %collective-permute-start.5 = (s32[32,1664]{1,0:T(8,128)S(1)}, s32[32,1664]{1,0:T(8,128)S(1)}, u32[]{:S(2)}, u32[]{:S(2)}) collective-permute-start(s32[32,1664]{1,0:T(8,128)S(1)} %constant_dynamic-update-slice_fusion), channel_id=1, source_target_pairs={{2,4},{6,8},{10,12},{14,16},{18,20},{22,24},{26,28},{4,2},{8,6},{1... | collective-permute-start | bytes 638984 | tf_op jit(solution)/shard_map/ppermute | solution.py:485
  30.9 2.2 %collective-permute-start.4 = (s32[32,1664]{1,0:T(8,128)S(1)}, s32[32,1664]{1,0:T(8,128)S(1)}, u32[]{:S(2)}, u32[]{:S(2)}) collective-permute-start(s32[32,1664]{1,0:T(8,128)S(1)} %constant_dynamic-update-slice_fusion), channel_id=1, source_target_pairs={{0,2},{4,6},{8,10},{12,14},{16,18},{20,22},{24,26},{28,30},{2,0},{... | collective-permute-start | bytes 638984 | tf_op jit(solution)/shard_map/ppermute | solution.py:485
  33.1 4.1 %target_sample_b.1.second_ref = f32[64,128]{1,0:T(8,128)S(1)} custom-call(s32[128,384]{1,0:T(8,128)S(1)} %bitcast.17, bf16[576,512]{1,0:T(8,128)(2,1)S(1)} %get-tuple-element.38.field_ref, f32[96,1536]{1,0:T(8,128)S(1)} %get-tuple-element.39.exact_ref), custom_call_target="tpu_custom_call" | custom-call | flops 4831838208 | bytes 1966080 | tf_op jit(solution)/shard_map/target_sample_b/pallas_call | solution.py:427
  37.2 0.0 collective-permute-done.5.refs_2_
  37.2 0.0 collective-permute-done.4.refs_1_
  37.3 0.0 copy-done.1
  37.3 1.7 %model_fields.1 = (bf16[576,512]{1,0:T(8,128)(2,1)S(1)}, f32[96,1536]{1,0:T(8,128)S(1)}, f32[8,128]{1,0:T(8,128)S(1)}) custom-call(s32[1]{0:T(128)} %bitcast.6._, bf16[8,128,576]{2,1,0:T(8,128)(2,1)S(1)} %copy-done.1, f32[32,1536]{1,0:T(8,128)S(1)} %bitcast.13, f32[32,1536]{1,0:T(8,128)S(1)} %get-tuple-element.44.own_ref, ...), custom_call_target="tpu_custom_call" | custom-call | bytes 925696 | tf_op jit(solution)/shard_map/model_fields/pallas_call | solution.py:445
  39.0 0.6 collective-permute-start.6
  39.6 8.1 %model_sample.1.model_ref = f32[128,128]{1,0:T(8,128)S(1)} custom-call(s32[128,384]{1,0:T(8,128)S(1)} %bitcast.18, bf16[576,512]{1,0:T(8,128)(2,1)S(1)} %get-tuple-element.48.field_ref, f32[96,1536]{1,0:T(8,128)S(1)} %get-tuple-element.49.exact_ref), custom_call_target="tpu_custom_call" | custom-call | flops 9663676416 | bytes 1966080 | tf_op jit(solution)/shard_map/model_sample/pallas_call | solution.py:427
  47.7 0.0 collective-permute-done.6
  47.7 0.2 join.1
  47.8 12.8 %all_to_all.22 = f32[16,1,128]{2,1,0:T(1,128)S(1)} all-to-all(f32[16,1,128]{2,1,0:T(1,128)S(1)} %bitcast.19), channel_id=1, replica_groups=mesh['brick'=16,'relay'=2] {'brick'}, dimensions={0} | all-to-all | bytes 16384 | tf_op jit(solution)/shard_map/all_to_all | solution.py:636
  60.6 0.0 copy-done.3
  60.6 0.9 %finish.1 = f32[6,64]{1,0:T(8,128)} custom-call(s32[8,64]{1,0:T(8,128)S(1)} %copy-done.3, f32[16,128]{1,0:T(8,128)S(1)} %bitcast.20), custom_call_target="tpu_custom_call" | custom-call | bytes 10240 | tf_op jit(solution)/shard_map/finish/pallas_call | solution.py:427
  (10 shorter events, 0.2 us)
Async XLA Ops:
  2.2 16.4 %all-to-all-start = ((s32[16,8,384]{2,1,0:T(8,128)}), s32[16,8,384]{2,1,0:T(8,128)S(1)}, u32[]{:S(2)}, u32[]{:S(2)}) async-start(s32[16,8,384]{2,1,0:T(8,128)} %bitcast.21), calls=%async_computation | async-start | bytes 393216 | tf_op jit(solution)/shard_map/all_to_all | solution.py:577
  9.6 5.5 %collective-permute-start = (s32[16,1664]{1,0:T(8,128)}, s32[16,1664]{1,0:T(8,128)S(1)}, u32[]{:S(2)}, u32[]{:S(2)}) collective-permute-start(s32[16,1664]{1,0:T(8,128)} %get-tuple-element.31), channel_id=1, source_target_pairs={{0,1},{1,0},{2,3},{3,2},{4,5},{5,4},{6,7},{7,6},{8,9},{9,8},{10,11... | collective-permute-start | bytes 319496 | tf_op jit(solution)/shard_map/ppermute | solution.py:492
  15.3 7.2 %collective-permute-start.1 = (s32[16,1664]{1,0:T(8,128)S(1)}, s32[16,1664]{1,0:T(8,128)S(1)}, u32[]{:S(2)}, u32[]{:S(2)}) collective-permute-start(s32[16,1664]{1,0:T(8,128)S(1)} %select_n.32), channel_id=1, source_target_pairs={{0,2},{4,6},{8,10},{12,14},{16,18},{20,22},{24,26},{28,30},{2,0},{... | collective-permute-start | bytes 319496 | tf_op jit(solution)/shard_map/ppermute | solution.py:485
  15.4 7.1 %collective-permute-start.2 = (s32[16,1664]{1,0:T(8,128)S(1)}, s32[16,1664]{1,0:T(8,128)S(1)}, u32[]{:S(2)}, u32[]{:S(2)}) collective-permute-start(s32[16,1664]{1,0:T(8,128)S(1)} %select_n.34), channel_id=1, source_target_pairs={{2,4},{6,8},{10,12},{14,16},{18,20},{22,24},{26,28},{4,2},{8,6},{1... | collective-permute-start | bytes 319496 | tf_op jit(solution)/shard_map/ppermute | solution.py:485
  18.6 5.4 %copy-start = (f32[4,8,1536]{2,1,0:T(8,128)S(1)}, f32[4,8,1536]{2,1,0:T(8,128)}, u32[]{:S(2)}) copy-start(f32[4,8,1536]{2,1,0:T(8,128)} %param.8) | copy-start | bytes 589828
  18.6 5.4 %copy-start.2 = (bf16[8,96,384]{2,1,0:T(8,128)(2,1)S(1)}, bf16[8,96,384]{2,1,0:T(8,128)(2,1)}, u32[]{:S(2)}) copy-start(bf16[8,96,384]{2,1,0:T(8,128)(2,1)} %constant.68.clone.table_ref) | copy-start | bytes 1769476
  22.5 7.4 %collective-permute-start.3 = (s32[16,1664]{1,0:T(8,128)S(1)}, s32[16,1664]{1,0:T(8,128)S(1)}, u32[]{:S(2)}, u32[]{:S(2)}) collective-permute-start(s32[16,1664]{1,0:T(8,128)S(1)} %get-tuple-element.42), channel_id=1, source_target_pairs={{0,1},{1,0},{2,3},{3,2},{4,5},{5,4},{6,7},{7,6},{8,9},{9,8},{10,11... | collective-permute-start | bytes 319496 | tf_op jit(solution)/shard_map/ppermute | solution.py:492
  29.9 7.4 %copy-start.1 = (bf16[8,128,576]{2,1,0:T(8,128)(2,1)S(1)}, bf16[8,128,576]{2,1,0:T(8,128)(2,1)}, u32[]{:S(2)}) copy-start(bf16[8,128,576]{2,1,0:T(8,128)(2,1)} %constant.69.clone.table_ref) | copy-start | bytes 3538948
  29.9 7.4 %collective-permute-start.5 = (s32[32,1664]{1,0:T(8,128)S(1)}, s32[32,1664]{1,0:T(8,128)S(1)}, u32[]{:S(2)}, u32[]{:S(2)}) collective-permute-start(s32[32,1664]{1,0:T(8,128)S(1)} %constant_dynamic-update-slice_fusion), channel_id=1, source_target_pairs={{2,4},{6,8},{10,12},{14,16},{18,20},{22,24},{26,28},{4,2},{8,6},{1... | collective-permute-start | bytes 638984 | tf_op jit(solution)/shard_map/ppermute | solution.py:485
  30.9 6.4 %collective-permute-start.4 = (s32[32,1664]{1,0:T(8,128)S(1)}, s32[32,1664]{1,0:T(8,128)S(1)}, u32[]{:S(2)}, u32[]{:S(2)}) collective-permute-start(s32[32,1664]{1,0:T(8,128)S(1)} %constant_dynamic-update-slice_fusion), channel_id=1, source_target_pairs={{0,2},{4,6},{8,10},{12,14},{16,18},{20,22},{24,26},{28,30},{2,0},{... | collective-permute-start | bytes 638984 | tf_op jit(solution)/shard_map/ppermute | solution.py:485
  39.0 8.7 %collective-permute-start.6 = (f32[8,128]{1,0:T(8,128)S(1)}, f32[8,128]{1,0:T(8,128)S(1)}, u32[]{:S(2)}, u32[]{:S(2)}) collective-permute-start(f32[8,128]{1,0:T(8,128)S(1)} %get-tuple-element.50), channel_id=1, source_target_pairs={{0,1},{1,0},{2,3},{3,2},{4,5},{5,4},{6,7},{7,6},{8,9},{9,8},{10,11... | collective-permute-start | bytes 12296 | tf_op jit(solution)/shard_map/ppermute | solution.py:512
  39.6 21.0 %copy-start.3 = (s32[8,64]{1,0:T(8,128)S(1)}, s32[8,64]{1,0:T(8,128)}, u32[]{:S(2)}) copy-start(s32[8,64]{1,0:T(8,128)} %get-tuple-element.28.place_ref) | copy-start | bytes 6148

commit v9 on v8

--- a/solution.py
+++ b/solution.py
@@ -376,7 +376,8 @@
     out_ref[...] = total
 
 
-def join_kernel(most, first_ref, second_ref, model_ref, sum_ref, out_ref):
+def join_kernel(most, *refs):
+    *target_refs, model_ref, sum_ref, out_ref = refs
     bricks = out_ref.shape[0]
     lane = lax.broadcasted_iota(I32, out_ref.shape, 1)
     sums = sum_ref[0:1, :]
@@ -384,8 +385,9 @@
         sums = sums + sum_ref[8 * k : 8 * k + 1, :]
     total = jnp.zeros(out_ref.shape, F32)
     for k in range(most):
-        rows, half = pl.ds(k, bricks, stride=most), pl.ds(k, bricks // 2, stride=most)
-        own = jnp.concatenate([first_ref[half, :], second_ref[half, :]], axis=0)
+        rows = pl.ds(k, bricks, stride=most)
+        parts = [ref[pl.ds(k, ref.shape[0] // most, stride=most), :] for ref in target_refs]
+        own = jnp.concatenate(parts, axis=0)
         own = jnp.where(lane < 6, own, 0.0)
         own = own + pltpu.roll(jnp.where(lane < 6, model_ref[rows, :], 0.0), 6, 1)
         if k == 0:
@@ -609,15 +611,15 @@
             macs=6 * count * beads * his * LO,
         )
 
-    half = slots // 2
-    target_first = sample(target_field, 0, half, "target_sample_a")
+    part = slots // 4
+    target_first = sample(target_field, 0, part, "target_sample_a")
     blocks, target_first, target_field = lax.optimization_barrier(
         (blocks, target_first, target_field)
     )
     beside = jnp.concatenate(blocks, axis=0)
     model_parts = [smooth] + blocks[1:]
     model_parts += swapped(beside, beside)
-    target_second = sample(target_field, half, slots - half, "target_sample_b")
+    target_second = sample(target_field, part, slots - part, "target_sample_b")
     target_second, *model_parts = lax.optimization_barrier((target_second, *model_parts))
     *model_field, partial = call_at(
         functools.partial(model_kernel, lines),

time: 61.8 us -> 61.8 us (level)
  blocking collectives: 12.8 us -> 11.4 us
  starting transfers between devices: 15.1 us -> 16.4 us
    all_to_all x1, blocking collectives: 12.8 us -> 11.4 us  [shards(): lax.all_to_all(leaving, 'brick', split_axis=0, concat_axis=0, tiled=True)]
    ppermute x1, starting transfers between devices: 0.58 us -> 1.56 us  [relay_total(): lax.ppermute(moving, 'relay', [(i, (i + 1) % size) for i in range(size)])]
  transfers between devices with their start and end apart: 8 -> 8, of which waited for: 2 -> 3; matrix products, arithmetic and copies ran while one was open for 2% -> 2% of each run, Pallas kernels for 35% -> 35%
where the time goes in v9:
time: 61.8 us; the launch traced here: 61.5 us
  Pallas kernels  26.7 us (43%)
  starting transfers between devices  16.4 us (27%)
  blocking collectives  11.4 us (18%)
  waiting for transfers between devices  5.56 us (9%)
  local copies, waits for them, and re-layouts  1.11 us (2%)
    pallas_call x7, Pallas kernels, call(): pl.pallas_call(kernel, out_shape=out_shape, scratch_shapes=list(scratch),...  23.3 us
    all_to_all x1, blocking collectives, shards(): lax.all_to_all(leaving, 'brick', split_axis=0, concat_axis=0, tiled=True)  11.4 us
    all_to_all x1, starting transfers between devices, shards(): got = lax.all_to_all(sent, 'brick', split_axis=0, concat_axis=0, tiled=True)  7.38 us
    ppermute x4, starting transfers between devices, swapped(): lax.ppermute(value, 'brick', pairs + [(j, i) for i, j in pairs])  4.29 us
    pallas_call x2, Pallas kernels, call_at(): pl.pallas_call(kernel, out_shape=out_shape, grid_spec=pltpu.PrefetchScala...  3.4 us
    ppermute x2, starting transfers between devices, relay_blocks(): return [value, lax.ppermute(value, 'relay', [(0, 1), (1, 0)])]  3.15 us
    ppermute x2, waiting for transfers between devices, relay_blocks(): return [value, lax.ppermute(value, 'relay', [(0, 1), (1, 0)])]  2.97 us
    all_to_all x1, waiting for transfers between devices, shards(): got = lax.all_to_all(sent, 'brick', split_axis=0, concat_axis=0, tiled=True)  2.58 us
  transfers between devices with their start and end apart: 8, of which 3 were waited for; matrix products, arithmetic and copies ran while one was open for 2% of the time, Pallas kernels for 35%

profile of v9, /device:TPU:0, one launch (start us, length us, event | category | flops | bytes accessed | tf_op | source)
XLA Modules:
  0.0 61.5 jit_solution(4354931111588351132)
XLA Ops:
  0.0 2.2 %pack.1 = (s32[128,384]{1,0:T(8,128)}, s32[8,64]{1,0:T(8,128)}, s32[16,1664]{1,0:T(8,128)}) custom-call(s32[1,64]{1,0:T(1,128)} %bitcast.23, f32[3,64]{1,0:T(4,128)} %refs_1_.1, s32[64,128]{1,0:T(8,128)} %refs_2_.1, bf16[64,128]{1,0:T(8,128)(2,1)} %refs_3_.1, f32[3,64,128]{2,1,0:T(8,128)} %refs_4_.1, f32[32,1536]{1,0:T(8,128)} %bitcast.11), custom_call_target="tpu_custom_call" | custom-call | bytes 361472 | tf_op jit(solution)/shard_map/pack/pallas_call | solution.py:429
  2.2 7.4 %all-to-all-start = ((s32[16,8,384]{2,1,0:T(8,128)}), s32[16,8,384]{2,1,0:T(8,128)S(1)}, u32[]{:S(2)}, u32[]{:S(2)}) async-start(s32[16,8,384]{2,1,0:T(8,128)} %bitcast.21), calls=%async_computation | async-start | bytes 393216 | tf_op jit(solution)/shard_map/all_to_all | solution.py:579
  9.6 1.6 %collective-permute-start = (s32[16,1664]{1,0:T(8,128)}, s32[16,1664]{1,0:T(8,128)S(1)}, u32[]{:S(2)}, u32[]{:S(2)}) collective-permute-start(s32[16,1664]{1,0:T(8,128)} %get-tuple-element.31), channel_id=1, source_target_pairs={{0,1},{1,0},{2,3},{3,2},{4,5},{5,4},{6,7},{7,6},{8,9},{9,8},{10,11... | collective-permute-start | bytes 319496 | tf_op jit(solution)/shard_map/ppermute | solution.py:494
  11.2 1.0 %fusion.2 = (s32[2,4,1664]{2,1,0:T(4,128)S(1)}, s32[2,4,1664]{2,1,0:T(4,128)S(1)}) fusion(s32[2,8,1664]{2,1,0:T(8,128)} %bitcast.22), kind=kLoop, calls=%fused_computation.7 | loop fusion | bytes 212992 | tf_op jit(solution)/shard_map/slice | solution.py:571
  12.3 2.9 %collective-permute-done.refs_0_ = s32[16,1664]{1,0:T(8,128)S(1)} collective-permute-done((s32[16,1664]{1,0:T(8,128)}, s32[16,1664]{1,0:T(8,128)S(1)}, u32[]{:S(2)}, u32[]{:S(2)}) %collective-permute-start) | collective-permute-done | bytes 106528 | tf_op jit(solution)/shard_map/ppermute | solution.py:494
  15.3 0.1 collective-permute-start.1
  15.4 0.7 %collective-permute-start.2 = (s32[16,1664]{1,0:T(8,128)S(1)}, s32[16,1664]{1,0:T(8,128)S(1)}, u32[]{:S(2)}, u32[]{:S(2)}) collective-permute-start(s32[16,1664]{1,0:T(8,128)S(1)} %select_n.34), channel_id=1, source_target_pairs={{2,4},{6,8},{10,12},{14,16},{18,20},{22,24},{26,28},{4,2},{8,6},{1... | collective-permute-start | bytes 319496 | tf_op jit(solution)/shard_map/ppermute | solution.py:487
  16.0 2.6 %all-to-all-done = s32[16,8,384]{2,1,0:T(8,128)S(1)} async-done(((s32[16,8,384]{2,1,0:T(8,128)}), s32[16,8,384]{2,1,0:T(8,128)S(1)}, u32[]{:S(2)}, u32[]{:S(2)}) %all-to-all-start) | async-done | bytes 196640 | tf_op jit(solution)/shard_map/all_to_all | solution.py:579
  18.6 3.8 %splat.1 = (f32[32,1536]{1,0:T(8,128)S(1)}, s32[16,1664]{1,0:T(8,128)S(1)}) custom-call(s32[128,384]{1,0:T(8,128)S(1)} %bitcast.15), custom_call_target="tpu_custom_call" | custom-call | flops 1610612736 | bytes 196608 | tf_op jit(solution)/shard_map/splat/pallas_call | solution.py:429
  22.5 0.0 collective-permute-done.1.refs_1_
  22.5 0.0 collective-permute-done.2.refs_2_
  22.5 1.6 %collective-permute-start.3 = (s32[16,1664]{1,0:T(8,128)S(1)}, s32[16,1664]{1,0:T(8,128)S(1)}, u32[]{:S(2)}, u32[]{:S(2)}) collective-permute-start(s32[16,1664]{1,0:T(8,128)S(1)} %get-tuple-element.42), channel_id=1, source_target_pairs={{0,1},{1,0},{2,3},{3,2},{4,5},{5,4},{6,7},{7,6},{8,9},{9,8},{10,11... | collective-permute-start | bytes 319496 | tf_op jit(solution)/shard_map/ppermute | solution.py:494
  24.1 0.0 copy-done
  24.1 0.0 copy-done.2
  24.1 1.7 %target_fields.1 = (bf16[576,512]{1,0:T(8,128)(2,1)S(1)}, f32[96,1536]{1,0:T(8,128)S(1)}) custom-call(s32[1]{0:T(128)} %bitcast.6._, bf16[8,96,384]{2,1,0:T(8,128)(2,1)S(1)} %copy-done.2, f32[32,1536]{1,0:T(8,128)S(1)} %bitcast.12, s32[16,1664]{1,0:T(8,128)S(1)} %collective-permute-done.refs_0_, s32[16,1664]{1,0:T(8,128)S(1)} %collective-permute-done.1.refs_1_, ...), custom_call_target="tpu_custom_call" | custom-call | flops 113246208 | bytes 516096 | tf_op jit(solution)/shard_map/target_fields/pallas_call | solution.py:447
  25.7 2.1 %target_sample_a.1.refs_0_ = f32[32,128]{1,0:T(8,128)S(1)} custom-call(s32[128,384]{1,0:T(8,128)S(1)} %bitcast.16, bf16[576,512]{1,0:T(8,128)(2,1)S(1)} %get-tuple-element.38.field_ref, f32[96,1536]{1,0:T(8,128)S(1)} %get-tuple-element.39.exact_ref), custom_call_target="tpu_custom_call" | custom-call | flops 2415919104 | bytes 1966080 | tf_op jit(solution)/shard_map/target_sample_a/pallas_call | solution.py:429
  27.8 0.1 collective-permute-done.3.refs_0_
  27.9 0.0 copy-start.1
  27.9 1.0 %collective-permute-start.5 = (s32[32,1664]{1,0:T(8,128)S(1)}, s32[32,1664]{1,0:T(8,128)S(1)}, u32[]{:S(2)}, u32[]{:S(2)}) collective-permute-start(s32[32,1664]{1,0:T(8,128)S(1)} %constant_dynamic-update-slice_fusion), channel_id=1, source_target_pairs={{2,4},{6,8},{10,12},{14,16},{18,20},{22,24},{26,28},{4,2},{8,6},{1... | collective-permute-start | bytes 638984 | tf_op jit(solution)/shard_map/ppermute | solution.py:487
  28.9 2.6 %collective-permute-start.4 = (s32[32,1664]{1,0:T(8,128)S(1)}, s32[32,1664]{1,0:T(8,128)S(1)}, u32[]{:S(2)}, u32[]{:S(2)}) collective-permute-start(s32[32,1664]{1,0:T(8,128)S(1)} %constant_dynamic-update-slice_fusion), channel_id=1, source_target_pairs={{0,2},{4,6},{8,10},{12,14},{16,18},{20,22},{24,26},{28,30},{2,0},{... | collective-permute-start | bytes 638984 | tf_op jit(solution)/shard_map/ppermute | solution.py:487
  31.5 6.1 %target_sample_b.1.refs_1_ = f32[96,128]{1,0:T(8,128)S(1)} custom-call(s32[128,384]{1,0:T(8,128)S(1)} %bitcast.17, bf16[576,512]{1,0:T(8,128)(2,1)S(1)} %get-tuple-element.38.field_ref, f32[96,1536]{1,0:T(8,128)S(1)} %get-tuple-element.39.exact_ref), custom_call_target="tpu_custom_call" | custom-call | flops 7247757312 | bytes 1966080 | tf_op jit(solution)/shard_map/target_sample_b/pallas_call | solution.py:429
  37.6 0.0 collective-permute-done.5.refs_2_
  37.6 0.0 collective-permute-done.4.refs_1_
  37.6 0.0 copy-done.1
  37.7 1.7 %model_fields.1 = (bf16[576,512]{1,0:T(8,128)(2,1)S(1)}, f32[96,1536]{1,0:T(8,128)S(1)}, f32[8,128]{1,0:T(8,128)S(1)}) custom-call(s32[1]{0:T(128)} %bitcast.6._, bf16[8,128,576]{2,1,0:T(8,128)(2,1)S(1)} %copy-done.1, f32[32,1536]{1,0:T(8,128)S(1)} %bitcast.13, f32[32,1536]{1,0:T(8,128)S(1)} %get-tuple-element.44.own_ref, ...), custom_call_target="tpu_custom_call" | custom-call | bytes 925696 | tf_op jit(solution)/shard_map/model_fields/pallas_call | solution.py:447
  39.4 1.6 %collective-permute-start.6 = (f32[8,128]{1,0:T(8,128)S(1)}, f32[8,128]{1,0:T(8,128)S(1)}, u32[]{:S(2)}, u32[]{:S(2)}) collective-permute-start(f32[8,128]{1,0:T(8,128)S(1)} %get-tuple-element.50), channel_id=1, source_target_pairs={{0,1},{1,0},{2,3},{3,2},{4,5},{5,4},{6,7},{7,6},{8,9},{9,8},{10,11... | collective-permute-start | bytes 12296 | tf_op jit(solution)/shard_map/ppermute | solution.py:514
  41.0 8.1 %model_sample.1.refs_2_ = f32[128,128]{1,0:T(8,128)S(1)} custom-call(s32[128,384]{1,0:T(8,128)S(1)} %bitcast.18, bf16[576,512]{1,0:T(8,128)(2,1)S(1)} %get-tuple-element.48.field_ref, f32[96,1536]{1,0:T(8,128)S(1)} %get-tuple-element.49.exact_ref), custom_call_target="tpu_custom_call" | custom-call | flops 9663676416 | bytes 1966080 | tf_op jit(solution)/shard_map/model_sample/pallas_call | solution.py:429
  49.0 0.0 collective-permute-done.6
  49.1 0.2 join.1
  49.2 11.4 %all_to_all.22 = f32[16,1,128]{2,1,0:T(1,128)S(1)} all-to-all(f32[16,1,128]{2,1,0:T(1,128)S(1)} %bitcast.19), channel_id=1, replica_groups=mesh['brick'=16,'relay'=2] {'brick'}, dimensions={0} | all-to-all | bytes 16384 | tf_op jit(solution)/shard_map/all_to_all | solution.py:638
  60.6 0.0 copy-done.3
  60.6 0.9 %finish.1 = f32[6,64]{1,0:T(8,128)} custom-call(s32[8,64]{1,0:T(8,128)S(1)} %copy-done.3, f32[16,128]{1,0:T(8,128)S(1)} %bitcast.20), custom_call_target="tpu_custom_call" | custom-call | bytes 10240 | tf_op jit(solution)/shard_map/finish/pallas_call | solution.py:429
  (10 shorter events, 0.2 us)
Async XLA Ops:
  2.2 16.4 %all-to-all-start = ((s32[16,8,384]{2,1,0:T(8,128)}), s32[16,8,384]{2,1,0:T(8,128)S(1)}, u32[]{:S(2)}, u32[]{:S(2)}) async-start(s32[16,8,384]{2,1,0:T(8,128)} %bitcast.21), calls=%async_computation | async-start | bytes 393216 | tf_op jit(solution)/shard_map/all_to_all | solution.py:579
  9.6 5.5 %collective-permute-start = (s32[16,1664]{1,0:T(8,128)}, s32[16,1664]{1,0:T(8,128)S(1)}, u32[]{:S(2)}, u32[]{:S(2)}) collective-permute-start(s32[16,1664]{1,0:T(8,128)} %get-tuple-element.31), channel_id=1, source_target_pairs={{0,1},{1,0},{2,3},{3,2},{4,5},{5,4},{6,7},{7,6},{8,9},{9,8},{10,11... | collective-permute-start | bytes 319496 | tf_op jit(solution)/shard_map/ppermute | solution.py:494
  15.3 7.2 %collective-permute-start.1 = (s32[16,1664]{1,0:T(8,128)S(1)}, s32[16,1664]{1,0:T(8,128)S(1)}, u32[]{:S(2)}, u32[]{:S(2)}) collective-permute-start(s32[16,1664]{1,0:T(8,128)S(1)} %select_n.32), channel_id=1, source_target_pairs={{0,2},{4,6},{8,10},{12,14},{16,18},{20,22},{24,26},{28,30},{2,0},{... | collective-permute-start | bytes 319496 | tf_op jit(solution)/shard_map/ppermute | solution.py:487
  15.4 7.1 %collective-permute-start.2 = (s32[16,1664]{1,0:T(8,128)S(1)}, s32[16,1664]{1,0:T(8,128)S(1)}, u32[]{:S(2)}, u32[]{:S(2)}) collective-permute-start(s32[16,1664]{1,0:T(8,128)S(1)} %select_n.34), channel_id=1, source_target_pairs={{2,4},{6,8},{10,12},{14,16},{18,20},{22,24},{26,28},{4,2},{8,6},{1... | collective-permute-start | bytes 319496 | tf_op jit(solution)/shard_map/ppermute | solution.py:487
  18.6 5.4 %copy-start = (f32[4,8,1536]{2,1,0:T(8,128)S(1)}, f32[4,8,1536]{2,1,0:T(8,128)}, u32[]{:S(2)}) copy-start(f32[4,8,1536]{2,1,0:T(8,128)} %param.8) | copy-start | bytes 589828
  18.6 5.4 %copy-start.2 = (bf16[8,96,384]{2,1,0:T(8,128)(2,1)S(1)}, bf16[8,96,384]{2,1,0:T(8,128)(2,1)}, u32[]{:S(2)}) copy-start(bf16[8,96,384]{2,1,0:T(8,128)(2,1)} %constant.68.clone.table_ref) | copy-start | bytes 1769476
  22.5 5.4 %collective-permute-start.3 = (s32[16,1664]{1,0:T(8,128)S(1)}, s32[16,1664]{1,0:T(8,128)S(1)}, u32[]{:S(2)}, u32[]{:S(2)}) collective-permute-start(s32[16,1664]{1,0:T(8,128)S(1)} %get-tuple-element.42), channel_id=1, source_target_pairs={{0,1},{1,0},{2,3},{3,2},{4,5},{5,4},{6,7},{7,6},{8,9},{9,8},{10,11... | collective-permute-start | bytes 319496 | tf_op jit(solution)/shard_map/ppermute | solution.py:494
  27.9 9.7 %copy-start.1 = (bf16[8,128,576]{2,1,0:T(8,128)(2,1)S(1)}, bf16[8,128,576]{2,1,0:T(8,128)(2,1)}, u32[]{:S(2)}) copy-start(bf16[8,128,576]{2,1,0:T(8,128)(2,1)} %constant.69.clone.table_ref) | copy-start | bytes 3538948
  27.9 9.7 %collective-permute-start.5 = (s32[32,1664]{1,0:T(8,128)S(1)}, s32[32,1664]{1,0:T(8,128)S(1)}, u32[]{:S(2)}, u32[]{:S(2)}) collective-permute-start(s32[32,1664]{1,0:T(8,128)S(1)} %constant_dynamic-update-slice_fusion), channel_id=1, source_target_pairs={{2,4},{6,8},{10,12},{14,16},{18,20},{22,24},{26,28},{4,2},{8,6},{1... | collective-permute-start | bytes 638984 | tf_op jit(solution)/shard_map/ppermute | solution.py:487
  28.9 8.7 %collective-permute-start.4 = (s32[32,1664]{1,0:T(8,128)S(1)}, s32[32,1664]{1,0:T(8,128)S(1)}, u32[]{:S(2)}, u32[]{:S(2)}) collective-permute-start(s32[32,1664]{1,0:T(8,128)S(1)} %constant_dynamic-update-slice_fusion), channel_id=1, source_target_pairs={{0,2},{4,6},{8,10},{12,14},{16,18},{20,22},{24,26},{28,30},{2,0},{... | collective-permute-start | bytes 638984 | tf_op jit(solution)/shard_map/ppermute | solution.py:487
  39.4 9.6 %collective-permute-start.6 = (f32[8,128]{1,0:T(8,128)S(1)}, f32[8,128]{1,0:T(8,128)S(1)}, u32[]{:S(2)}, u32[]{:S(2)}) collective-permute-start(f32[8,128]{1,0:T(8,128)S(1)} %get-tuple-element.50), channel_id=1, source_target_pairs={{0,1},{1,0},{2,3},{3,2},{4,5},{5,4},{6,7},{7,6},{8,9},{9,8},{10,11... | collective-permute-start | bytes 12296 | tf_op jit(solution)/shard_map/ppermute | solution.py:514
  41.0 19.6 %copy-start.3 = (s32[8,64]{1,0:T(8,128)S(1)}, s32[8,64]{1,0:T(8,128)}, u32[]{:S(2)}) copy-start(s32[8,64]{1,0:T(8,128)} %get-tuple-element.28.place_ref) | copy-start | bytes 6148

commit v10 on v9

--- a/solution.py
+++ b/solution.py
@@ -63,12 +63,14 @@
     return np.concatenate([high, high, low], axis=-1)
 
 
-def weight_table(z_kinds, x_kinds, z_len, z_count, z_blocks, x_len, x_count, x_parts):
+def weight_table(
+    z_kinds, x_kinds, z_rows, z_len, z_count, z_blocks, x_len, x_count, x_parts
+):
     z_tables = []
     for r in range(z_count):
         wanted = np.concatenate([np.arange(z_len) + z_len * block for block in z_blocks(r)])
-        rows = np.arange(z_len) + z_len * r
-        z_tables.append(np.stack([columns_at(m, rows, wanted) for m in z_kinds]))
+        rows = [np.arange(z_len) + z_len * block for block in z_rows(r)]
+        z_tables.append(np.stack([columns_at(m, i, wanted) for m, i in zip(z_kinds, rows)]))
     x_tables = []
     for b in range(x_count):
         wanted = np.concatenate([x_len * b + part for part in x_parts(b)])
@@ -231,11 +233,11 @@
     return high, low
 
 
-def mix_lines(table_ref, parts):
+def mix_lines(index_ref, tables_ref, parts):
     value = jnp.concatenate(parts, axis=0)
     high, low = split(value)
     return jnp.dot(
-        table_ref[0], jnp.concatenate([high, low, high], axis=0), preferred_element_type=F32
+        tables_ref[index_ref[0]], jnp.concatenate([high, low, high], axis=0), preferred_element_type=F32
     )
 
 
@@ -259,20 +261,25 @@
     return lines
 
 
-def target_kernel(lines, _, table_ref, own_ref, *refs):
+def target_kernel(lines, index_ref, tables_ref, own_ref, *refs):
     *near_refs, first_ref, second_ref, out_ref, exact_ref = refs
-    mixed = mix_lines(table_ref, window_lines(own_ref, near_refs, first_ref, second_ref))
+    window = window_lines(own_ref, near_refs, first_ref, second_ref)
+    mixed = mix_lines(index_ref, tables_ref, window)
     grad_x = line_blur(mixed[0:lines], False)
     grad_y = line_blur(mixed[lines : 2 * lines], True)
     grad_z = line_blur(mixed[2 * lines : 3 * lines], False)
     store_fields([grad_x, grad_y, grad_z], lines, out_ref, exact_ref)
 
 
-def model_kernel(lines, _, table_ref, target_ref, own_ref, *refs):
-    *near_refs, first_ref, second_ref, out_ref, exact_ref, sum_ref = refs
-    smooth = mix_lines(table_ref, window_lines(own_ref, near_refs, first_ref, second_ref))
+def model_kernel(lines, near, index_ref, tables_ref, target_ref, *refs):
+    target = [target_ref[...]]
+    for ref in refs[: near - 1]:
+        target += decode(ref[...], 1)
+    target = jnp.concatenate(target, axis=0)
+    own_ref, *near_refs, first_ref, second_ref, out_ref, exact_ref, sum_ref = refs[near - 1 :]
+    window = window_lines(own_ref, near_refs, first_ref, second_ref)
+    smooth = mix_lines(index_ref, tables_ref, window)
     model = smooth[3 * lines :]
-    target = target_ref[...]
     sums = [jnp.sum(model * target), jnp.sum(model * model), jnp.sum(target * target)]
     lane = lax.broadcasted_iota(I32, sum_ref.shape, 1)
     total = jnp.zeros(sum_ref.shape, F32)
@@ -438,26 +445,15 @@
 
 
 def call_at(kernel, out_shape, index, table, *args, name=None, macs=0):
-    def whole(shape):
-        return pl.BlockSpec(shape, lambda i, s: (0,) * len(shape))
-
-    single = not isinstance(out_shape, list)
-    outs = [out_shape] if single else out_shape
-    specs = [whole(o.shape) for o in outs]
-    return pl.pallas_call(
+    vmem = pl.BlockSpec(memory_space=pltpu.VMEM)
+    return call(
         kernel,
-        out_shape=out_shape,
-        grid_spec=pltpu.PrefetchScalarGridSpec(
-            num_scalar_prefetch=1,
-            grid=(1,),
-            in_specs=[pl.BlockSpec((1,) + table.shape[1:], lambda i, s: (s[0], 0, 0))]
-            + [whole(a.shape) for a in args],
-            out_specs=specs[0] if single else specs,
-        ),
-        compiler_params=pltpu.CompilerParams(vmem_limit_bytes=VMEM_BYTES),
-        cost_estimate=cost(macs, 4 * sum(a.size for a in args)),
+        out_shape,
+        index, table, *args,
+        in_specs=[pl.BlockSpec(memory_space=pltpu.SMEM)] + [vmem] * (1 + len(args)),
         name=name,
-    )(index, table, *args)
+        macs=macs,
+    )
 
 
 def looked_up(values, position):
@@ -532,14 +528,16 @@
     z_total, x_total = relay_count * planes, brick_count * columns
     gz, dz = axis_matrix(z_total, False), axis_matrix(z_total, True)
     gx, dx = axis_matrix(x_total, False), axis_matrix(x_total, True)
+    near = 2 if relay_count == 2 else 1
     reach_one, reach_two = -(-KR // planes), -(-2 * KR // planes)
     target_table, tz, tx, tn = weight_table(
-        [gz, gz, dz], [dx, gx, gx], planes, relay_count, relay_order(relay_count, reach_one),
+        [gz, gz, dz], [dx, gx, gx], lambda r: [r] * 3, planes, relay_count, relay_order(relay_count, reach_one),
         columns, brick_count,
         paired(np.arange(columns), np.arange(-KR, 0), np.arange(columns, columns + KR)),
     )
     model_table, mz, mx, mn = weight_table(
-        [gz @ gz, gz @ gz, dz @ gz, gz], [dx @ gx, gx @ gx, gx @ gx, gx],
+        [gz @ gz, gz @ gz, dz @ gz] + [gz] * near, [dx @ gx, gx @ gx, gx @ gx] + [gx] * near,
+        lambda r: [r] * 4 + [1 - r] * (near - 1),
         planes, relay_count, relay_order(relay_count, reach_two), columns, brick_count,
         paired(np.arange(columns), np.arange(-columns, 0), np.arange(columns, 2 * columns)),
     )
@@ -622,12 +620,12 @@
     target_second = sample(target_field, part, slots - part, "target_sample_b")
     target_second, *model_parts = lax.optimization_barrier((target_second, *model_parts))
     *model_field, partial = call_at(
-        functools.partial(model_kernel, lines),
+        functools.partial(model_kernel, lines, near),
         field_shapes + [jax.ShapeDtypeStruct((8, 128), F32)],
-        model_index, jnp.asarray(model_table), target_lines, *model_parts,
+        model_index, jnp.asarray(model_table), target_lines, *target_blocks[1:near], *model_parts,
         name="model_fields",
     )
-    partials = relay_total(partial)
+    partials = partial if near == relay_count else relay_total(partial)
     model_sums = sample(model_field, 0, slots, "model_sample")
     leaving = call(
         functools.partial(join_kernel, most),

time: 61.8 us -> 60.6 us (0.981)
  starting transfers between devices: 16.4 us -> 14.8 us
    pallas_call x7 -> x9, Pallas kernels: 23.3 us -> 27 us  [call(): pl.pallas_call(kernel, out_shape=out_shape, scratch_shapes=list(scratch),...]
    pallas_call x2 -> x0, Pallas kernels: 3.4 us -> none  [call_at(): pl.pallas_call(kernel, out_shape=out_shape, grid_spec=pltpu.PrefetchScala...]
    ppermute x1 -> x0, starting transfers between devices: 1.56 us -> none  [relay_total(): lax.ppermute(moving, 'relay', [(i, (i + 1) % size) for i in range(size)])]
  transfers between devices with their start and end apart: 8 -> 7, of which waited for: 3 -> 3; matrix products, arithmetic and copies ran while one was open for 2% -> 2% of each run, Pallas kernels for 35% -> 23%
where the time goes in v10:
time: 60.6 us; the launch traced here: 60.3 us
  Pallas kernels  27 us (45%)
  starting transfers between devices  14.8 us (24%)
  blocking collectives  11.5 us (19%)
  waiting for transfers between devices  5.56 us (9%)
  local copies, waits for them, and re-layouts  1.12 us (2%)
    pallas_call x9, Pallas kernels, call(): pl.pallas_call(kernel, out_shape=out_shape, scratch_shapes=list(scratch),...  27 us
    all_to_all x1, blocking collectives, shards(): lax.all_to_all(leaving, 'brick', split_axis=0, concat_axis=0, tiled=True)  11.5 us
    all_to_all x1, starting transfers between devices, shards(): got = lax.all_to_all(sent, 'brick', split_axis=0, concat_axis=0, tiled=True)  7.38 us
    ppermute x4, starting transfers between devices, swapped(): lax.ppermute(value, 'brick', pairs + [(j, i) for i, j in pairs])  4.29 us
    ppermute x2, starting transfers between devices, relay_blocks(): return [value, lax.ppermute(value, 'relay', [(0, 1), (1, 0)])]  3.15 us
    ppermute x2, waiting for transfers between devices, relay_blocks(): return [value, lax.ppermute(value, 'relay', [(0, 1), (1, 0)])]  2.97 us
    all_to_all x1, waiting for transfers between devices, shards(): got = lax.all_to_all(sent, 'brick', split_axis=0, concat_axis=0, tiled=True)  2.58 us
  transfers between devices with their start and end apart: 7, of which 3 were waited for; matrix products, arithmetic and copies ran while one was open for 2% of the time, Pallas kernels for 23%

profile of v10, /device:TPU:0, one launch (start us, length us, event | category | flops | bytes accessed | tf_op | source)
XLA Modules:
  0.0 60.3 jit_solution(15975816138973472957)
XLA Ops:
  0.0 2.3 %pack.1 = (s32[128,384]{1,0:T(8,128)}, s32[8,64]{1,0:T(8,128)}, s32[16,1664]{1,0:T(8,128)}) custom-call(s32[1,64]{1,0:T(1,128)} %bitcast.23, f32[3,64]{1,0:T(4,128)} %refs_1_.1, s32[64,128]{1,0:T(8,128)} %refs_2_.1, bf16[64,128]{1,0:T(8,128)(2,1)} %refs_3_.1, f32[3,64,128]{2,1,0:T(8,128)} %refs_4_.1, f32[32,1536]{1,0:T(8,128)} %bitcast.11), custom_call_target="tpu_custom_call" | custom-call | bytes 361472 | tf_op jit(solution)/shard_map/pack/pallas_call | solution.py:436
  2.3 7.4 %all-to-all-start = ((s32[16,8,384]{2,1,0:T(8,128)}), s32[16,8,384]{2,1,0:T(8,128)S(1)}, u32[]{:S(2)}, u32[]{:S(2)}) async-start(s32[16,8,384]{2,1,0:T(8,128)} %bitcast.21), calls=%async_computation | async-start | bytes 393216 | tf_op jit(solution)/shard_map/all_to_all | solution.py:577
  9.6 1.6 %collective-permute-start = (s32[16,1664]{1,0:T(8,128)}, s32[16,1664]{1,0:T(8,128)S(1)}, u32[]{:S(2)}, u32[]{:S(2)}) collective-permute-start(s32[16,1664]{1,0:T(8,128)} %get-tuple-element.31), channel_id=1, source_target_pairs={{0,1},{1,0},{2,3},{3,2},{4,5},{5,4},{6,7},{7,6},{8,9},{9,8},{10,11... | collective-permute-start | bytes 319496 | tf_op jit(solution)/shard_map/ppermute | solution.py:490
  11.2 1.0 %fusion.2 = (s32[2,4,1664]{2,1,0:T(4,128)S(1)}, s32[2,4,1664]{2,1,0:T(4,128)S(1)}) fusion(s32[2,8,1664]{2,1,0:T(8,128)} %bitcast.22), kind=kLoop, calls=%fused_computation.6 | loop fusion | bytes 212992 | tf_op jit(solution)/shard_map/slice | solution.py:569
  12.3 2.9 %collective-permute-done.refs_0_ = s32[16,1664]{1,0:T(8,128)S(1)} collective-permute-done((s32[16,1664]{1,0:T(8,128)}, s32[16,1664]{1,0:T(8,128)S(1)}, u32[]{:S(2)}, u32[]{:S(2)}) %collective-permute-start) | collective-permute-done | bytes 106528 | tf_op jit(solution)/shard_map/ppermute | solution.py:490
  15.3 0.1 collective-permute-start.1
  15.4 0.7 %collective-permute-start.2 = (s32[16,1664]{1,0:T(8,128)S(1)}, s32[16,1664]{1,0:T(8,128)S(1)}, u32[]{:S(2)}, u32[]{:S(2)}) collective-permute-start(s32[16,1664]{1,0:T(8,128)S(1)} %select_n.34), channel_id=1, source_target_pairs={{2,4},{6,8},{10,12},{14,16},{18,20},{22,24},{26,28},{4,2},{8,6},{1... | collective-permute-start | bytes 319496 | tf_op jit(solution)/shard_map/ppermute | solution.py:483
  16.1 2.6 %all-to-all-done = s32[16,8,384]{2,1,0:T(8,128)S(1)} async-done(((s32[16,8,384]{2,1,0:T(8,128)}), s32[16,8,384]{2,1,0:T(8,128)S(1)}, u32[]{:S(2)}, u32[]{:S(2)}) %all-to-all-start) | async-done | bytes 196640 | tf_op jit(solution)/shard_map/all_to_all | solution.py:577
  18.6 0.0 copy-start
  18.6 3.8 %splat.1 = (f32[32,1536]{1,0:T(8,128)S(1)}, s32[16,1664]{1,0:T(8,128)S(1)}) custom-call(s32[128,384]{1,0:T(8,128)S(1)} %bitcast.15), custom_call_target="tpu_custom_call" | custom-call | flops 1610612736 | bytes 196608 | tf_op jit(solution)/shard_map/splat/pallas_call | solution.py:436
  22.5 0.0 collective-permute-done.1.refs_1_
  22.5 0.0 collective-permute-done.2.refs_2_
  22.5 1.6 %collective-permute-start.3 = (s32[16,1664]{1,0:T(8,128)S(1)}, s32[16,1664]{1,0:T(8,128)S(1)}, u32[]{:S(2)}, u32[]{:S(2)}) collective-permute-start(s32[16,1664]{1,0:T(8,128)S(1)} %get-tuple-element.42), channel_id=1, source_target_pairs={{0,1},{1,0},{2,3},{3,2},{4,5},{5,4},{6,7},{7,6},{8,9},{9,8},{10,11... | collective-permute-start | bytes 319496 | tf_op jit(solution)/shard_map/ppermute | solution.py:490
  24.1 0.0 copy-done
  24.1 0.0 copy-done.2
  24.1 1.7 %target_fields.1 = (bf16[576,512]{1,0:T(8,128)(2,1)S(1)}, f32[96,1536]{1,0:T(8,128)S(1)}) custom-call(s32[1]{0:T(128)} %bitcast.6.index_ref, bf16[8,96,384]{2,1,0:T(8,128)(2,1)S(1)} %copy-done.2, f32[32,1536]{1,0:T(8,128)S(1)} %bitcast.12, s32[16,1664]{1,0:T(8,128)S(1)} %collective-permute-done.refs_0_, s32[16,1664]{1,0:T(8,128)S(1)} %collective-permute-done.1.refs_1_, ...), custom_call_target="tpu_custom_call" | custom-call | flops 113246208 | bytes 1695748 | tf_op jit(solution)/shard_map/target_fields/pallas_call | solution.py:436
  25.7 2.1 %target_sample_a.1.refs_0_ = f32[32,128]{1,0:T(8,128)S(1)} custom-call(s32[128,384]{1,0:T(8,128)S(1)} %bitcast.16, bf16[576,512]{1,0:T(8,128)(2,1)S(1)} %get-tuple-element.38.field_ref, f32[96,1536]{1,0:T(8,128)S(1)} %get-tuple-element.39.exact_ref), custom_call_target="tpu_custom_call" | custom-call | flops 2415919104 | bytes 1966080 | tf_op jit(solution)/shard_map/target_sample_a/pallas_call | solution.py:436
  27.8 0.1 collective-permute-done.3.refs_2_
  27.9 0.0 copy-start.1
  27.9 1.0 %collective-permute-start.5 = (s32[32,1664]{1,0:T(8,128)S(1)}, s32[32,1664]{1,0:T(8,128)S(1)}, u32[]{:S(2)}, u32[]{:S(2)}) collective-permute-start(s32[32,1664]{1,0:T(8,128)S(1)} %constant_dynamic-update-slice_fusion), channel_id=1, source_target_pairs={{2,4},{6,8},{10,12},{14,16},{18,20},{22,24},{26,28},{4,2},{8,6},{1... | collective-permute-start | bytes 638984 | tf_op jit(solution)/shard_map/ppermute | solution.py:483
  28.9 2.6 %collective-permute-start.4 = (s32[32,1664]{1,0:T(8,128)S(1)}, s32[32,1664]{1,0:T(8,128)S(1)}, u32[]{:S(2)}, u32[]{:S(2)}) collective-permute-start(s32[32,1664]{1,0:T(8,128)S(1)} %constant_dynamic-update-slice_fusion), channel_id=1, source_target_pairs={{0,2},{4,6},{8,10},{12,14},{16,18},{20,22},{24,26},{28,30},{2,0},{... | collective-permute-start | bytes 638984 | tf_op jit(solution)/shard_map/ppermute | solution.py:483
  31.5 6.1 %target_sample_b.1.refs_1_ = f32[96,128]{1,0:T(8,128)S(1)} custom-call(s32[128,384]{1,0:T(8,128)S(1)} %bitcast.17, bf16[576,512]{1,0:T(8,128)(2,1)S(1)} %get-tuple-element.38.field_ref, f32[96,1536]{1,0:T(8,128)S(1)} %get-tuple-element.39.exact_ref), custom_call_target="tpu_custom_call" | custom-call | flops 7247757312 | bytes 1966080 | tf_op jit(solution)/shard_map/target_sample_b/pallas_call | solution.py:436
  37.6 0.0 collective-permute-done.5.refs_4_
  37.7 0.0 collective-permute-done.4.refs_3_
  37.7 0.0 copy-done.1
  37.7 1.8 %model_fields.1 = (bf16[576,512]{1,0:T(8,128)(2,1)S(1)}, f32[96,1536]{1,0:T(8,128)S(1)}, f32[8,128]{1,0:T(8,128)S(1)}) custom-call(s32[1]{0:T(128)} %bitcast.6.index_ref, bf16[8,160,576]{2,1,0:T(8,128)(2,1)S(1)} %copy-done.1, f32[32,1536]{1,0:T(8,128)S(1)} %bitcast.13, s32[16,1664]{1,0:T(8,128)S(1)} %collective-permute-done.refs_0_, ...), custom_call_target="tpu_custom_call" | custom-call | bytes 3981316 | tf_op jit(solution)/shard_map/model_fields/pallas_call | solution.py:436
  39.5 0.0 copy-start.3
  39.5 8.2 %model_sample.1.refs_2_ = f32[128,128]{1,0:T(8,128)S(1)} custom-call(s32[128,384]{1,0:T(8,128)S(1)} %bitcast.18, bf16[576,512]{1,0:T(8,128)(2,1)S(1)} %get-tuple-element.48.field_ref, f32[96,1536]{1,0:T(8,128)S(1)} %get-tuple-element.49.exact_ref), custom_call_target="tpu_custom_call" | custom-call | flops 9663676416 | bytes 1966080 | tf_op jit(solution)/shard_map/model_sample/pallas_call | solution.py:436
  47.7 0.2 join.1
  47.9 11.5 %all_to_all.22 = f32[16,1,128]{2,1,0:T(1,128)S(1)} all-to-all(f32[16,1,128]{2,1,0:T(1,128)S(1)} %bitcast.19), channel_id=1, replica_groups=mesh['brick'=16,'relay'=2] {'brick'}, dimensions={0} | all-to-all | bytes 16384 | tf_op jit(solution)/shard_map/all_to_all | solution.py:636
  59.4 0.0 copy-done.3
  59.4 0.9 %finish.1 = f32[6,64]{1,0:T(8,128)} custom-call(s32[8,64]{1,0:T(8,128)S(1)} %copy-done.3, f32[16,128]{1,0:T(8,128)S(1)} %bitcast.20), custom_call_target="tpu_custom_call" | custom-call | bytes 10240 | tf_op jit(solution)/shard_map/finish/pallas_call | solution.py:436
  (7 shorter events, 0.2 us)
Async XLA Ops:
  2.3 16.4 %all-to-all-start = ((s32[16,8,384]{2,1,0:T(8,128)}), s32[16,8,384]{2,1,0:T(8,128)S(1)}, u32[]{:S(2)}, u32[]{:S(2)}) async-start(s32[16,8,384]{2,1,0:T(8,128)} %bitcast.21), calls=%async_computation | async-start | bytes 393216 | tf_op jit(solution)/shard_map/all_to_all | solution.py:577
  9.6 5.5 %collective-permute-start = (s32[16,1664]{1,0:T(8,128)}, s32[16,1664]{1,0:T(8,128)S(1)}, u32[]{:S(2)}, u32[]{:S(2)}) collective-permute-start(s32[16,1664]{1,0:T(8,128)} %get-tuple-element.31), channel_id=1, source_target_pairs={{0,1},{1,0},{2,3},{3,2},{4,5},{5,4},{6,7},{7,6},{8,9},{9,8},{10,11... | collective-permute-start | bytes 319496 | tf_op jit(solution)/shard_map/ppermute | solution.py:490
  15.3 7.2 %collective-permute-start.1 = (s32[16,1664]{1,0:T(8,128)S(1)}, s32[16,1664]{1,0:T(8,128)S(1)}, u32[]{:S(2)}, u32[]{:S(2)}) collective-permute-start(s32[16,1664]{1,0:T(8,128)S(1)} %select_n.32), channel_id=1, source_target_pairs={{0,2},{4,6},{8,10},{12,14},{16,18},{20,22},{24,26},{28,30},{2,0},{... | collective-permute-start | bytes 319496 | tf_op jit(solution)/shard_map/ppermute | solution.py:483
  15.4 7.1 %collective-permute-start.2 = (s32[16,1664]{1,0:T(8,128)S(1)}, s32[16,1664]{1,0:T(8,128)S(1)}, u32[]{:S(2)}, u32[]{:S(2)}) collective-permute-start(s32[16,1664]{1,0:T(8,128)S(1)} %select_n.34), channel_id=1, source_target_pairs={{2,4},{6,8},{10,12},{14,16},{18,20},{22,24},{26,28},{4,2},{8,6},{1... | collective-permute-start | bytes 319496 | tf_op jit(solution)/shard_map/ppermute | solution.py:483
  18.6 5.4 %copy-start = (f32[4,8,1536]{2,1,0:T(8,128)S(1)}, f32[4,8,1536]{2,1,0:T(8,128)}, u32[]{:S(2)}) copy-start(f32[4,8,1536]{2,1,0:T(8,128)} %param.8) | copy-start | bytes 589828
  18.6 5.4 %copy-start.2 = (bf16[8,96,384]{2,1,0:T(8,128)(2,1)S(1)}, bf16[8,96,384]{2,1,0:T(8,128)(2,1)}, u32[]{:S(2)}) copy-start(bf16[8,96,384]{2,1,0:T(8,128)(2,1)} %constant.68.clone.tables_ref) | copy-start | bytes 1769476
  22.5 5.4 %collective-permute-start.3 = (s32[16,1664]{1,0:T(8,128)S(1)}, s32[16,1664]{1,0:T(8,128)S(1)}, u32[]{:S(2)}, u32[]{:S(2)}) collective-permute-start(s32[16,1664]{1,0:T(8,128)S(1)} %get-tuple-element.42), channel_id=1, source_target_pairs={{0,1},{1,0},{2,3},{3,2},{4,5},{5,4},{6,7},{7,6},{8,9},{9,8},{10,11... | collective-permute-start | bytes 319496 | tf_op jit(solution)/shard_map/ppermute | solution.py:490
  27.9 9.7 %copy-start.1 = (bf16[8,160,576]{2,1,0:T(8,128)(2,1)S(1)}, bf16[8,160,576]{2,1,0:T(8,128)(2,1)}, u32[]{:S(2)}) copy-start(bf16[8,160,576]{2,1,0:T(8,128)(2,1)} %constant.69.clone.tables_ref) | copy-start | bytes 4423684
  27.9 9.7 %collective-permute-start.5 = (s32[32,1664]{1,0:T(8,128)S(1)}, s32[32,1664]{1,0:T(8,128)S(1)}, u32[]{:S(2)}, u32[]{:S(2)}) collective-permute-start(s32[32,1664]{1,0:T(8,128)S(1)} %constant_dynamic-update-slice_fusion), channel_id=1, source_target_pairs={{2,4},{6,8},{10,12},{14,16},{18,20},{22,24},{26,28},{4,2},{8,6},{1... | collective-permute-start | bytes 638984 | tf_op jit(solution)/shard_map/ppermute | solution.py:483
  28.9 8.7 %collective-permute-start.4 = (s32[32,1664]{1,0:T(8,128)S(1)}, s32[32,1664]{1,0:T(8,128)S(1)}, u32[]{:S(2)}, u32[]{:S(2)}) collective-permute-start(s32[32,1664]{1,0:T(8,128)S(1)} %constant_dynamic-update-slice_fusion), channel_id=1, source_target_pairs={{0,2},{4,6},{8,10},{12,14},{16,18},{20,22},{24,26},{28,30},{2,0},{... | collective-permute-start | bytes 638984 | tf_op jit(solution)/shard_map/ppermute | solution.py:483
  39.5 20.0 %copy-start.3 = (s32[8,64]{1,0:T(8,128)S(1)}, s32[8,64]{1,0:T(8,128)}, u32[]{:S(2)}) copy-start(s32[8,64]{1,0:T(8,128)} %get-tuple-element.28.place_ref) | copy-start | bytes 6148

commit v11 on v10

--- a/solution.py
+++ b/solution.py
@@ -13,10 +13,13 @@
 EPSILON = 1e-06
 HIGHEST = lax.Precision.HIGHEST
 LO = 256
+BY_LANES = 14
 FIELDS = 16
 WEIGHT_SCALE = 512.0
 LEVER_SCALE = 32768.0
 LEVER_BIAS = 1 << 20
+FIELD_TOP = 1048575.0
+TINY = 1e-30
 CODE_TOP = 65535
 SCALE_UNIT = 512.0
 SCALE_LANES = 128
@@ -154,10 +157,10 @@
     placed = jnp.dot(place, payload, precision=HIGHEST, preferred_element_type=F32)
     placed = placed.astype(I32)
     code, weight, lx, ly, lz = [placed[:, k * beads : (k + 1) * beads] for k in range(5)]
-    lz = lz + LEVER_BIAS
+    one, two = pack_three(lx, ly, lz)
     out_ref[:, 0:beads] = code | (weight << 16)
-    out_ref[:, beads : 2 * beads] = (lx << 11) | (lz >> 10)
-    out_ref[:, 2 * beads : 3 * beads] = (ly << 11) | (lz & 1023)
+    out_ref[:, beads : 2 * beads] = one
+    out_ref[:, 2 * beads : 3 * beads] = two
 
 
 def line_blur(value, derivative):
@@ -241,10 +244,24 @@
     )
 
 
-def store_fields(fields, lines, out_ref, exact_ref):
+def pack_three(first, second, third):
+    third = third + LEVER_BIAS
+    return (first << 11) | (third >> 10), (second << 11) | (third & 1023)
+
+
+def unpack_three(one, two):
+    return one >> 11, two >> 11, (((one & 2047) << 10) | (two & 1023)) - LEVER_BIAS
+
+
+def store_fields(fields, lines, out_ref, word_ref, scale_ref):
+    top = jnp.maximum(jnp.max(jnp.abs(jnp.concatenate(fields, axis=0))), TINY)
+    scale_ref[...] = jnp.full(scale_ref.shape, top * (1.0 / FIELD_TOP), F32)
+    up = FIELD_TOP / jnp.full((1, fields[0].shape[1]), top, F32)
+    one, two = pack_three(*[jnp.round(field * up).astype(I32) for field in fields])
+    word_ref[:lines, :] = one
+    word_ref[lines:, :] = two
     his = fields[0].shape[1] // LO * lines
     for k, field in enumerate(fields):
-        exact_ref[k * lines : (k + 1) * lines, :] = field
         for yh in range(field.shape[1] // LO):
             high, low = split(field[:, yh * LO : (yh + 1) * LO])
             rows = slice(k * his + yh * lines, k * his + (yh + 1) * lines)
@@ -262,13 +279,13 @@
 
 
 def target_kernel(lines, index_ref, tables_ref, own_ref, *refs):
-    *near_refs, first_ref, second_ref, out_ref, exact_ref = refs
+    *near_refs, first_ref, second_ref, out_ref, word_ref, scale_ref = refs
     window = window_lines(own_ref, near_refs, first_ref, second_ref)
     mixed = mix_lines(index_ref, tables_ref, window)
     grad_x = line_blur(mixed[0:lines], False)
     grad_y = line_blur(mixed[lines : 2 * lines], True)
     grad_z = line_blur(mixed[2 * lines : 3 * lines], False)
-    store_fields([grad_x, grad_y, grad_z], lines, out_ref, exact_ref)
+    store_fields([grad_x, grad_y, grad_z], lines, out_ref, word_ref, scale_ref)
 
 
 def model_kernel(lines, near, index_ref, tables_ref, target_ref, *refs):
@@ -276,7 +293,7 @@
     for ref in refs[: near - 1]:
         target += decode(ref[...], 1)
     target = jnp.concatenate(target, axis=0)
-    own_ref, *near_refs, first_ref, second_ref, out_ref, exact_ref, sum_ref = refs[near - 1 :]
+    own_ref, *near_refs, first_ref, second_ref, out_ref, word_ref, scale_ref, sum_ref = refs[near - 1 :]
     window = window_lines(own_ref, near_refs, first_ref, second_ref)
     smooth = mix_lines(index_ref, tables_ref, window)
     model = smooth[3 * lines :]
@@ -289,7 +306,7 @@
     grad_x = line_blur(smooth[0:lines], False)
     grad_y = line_blur(smooth[lines : 2 * lines], True)
     grad_z = line_blur(smooth[2 * lines : 3 * lines], False)
-    store_fields([grad_x, grad_y, grad_z], lines, out_ref, exact_ref)
+    store_fields([grad_x, grad_y, grad_z], lines, out_ref, word_ref, scale_ref)
 
 
 def sample_by_matmul(word, field_ref, his, store):
@@ -319,30 +336,32 @@
     return finish
 
 
-def sample_by_lanes(word, exact_ref, lines, store):
+def sample_by_lanes(word, word_ref, scale_ref, lines, store):
     count, beads = word.shape
-    tiles = exact_ref.shape[1] // 128
+    tiles = word_ref.shape[1] // 128
     line_shift, lo_shift = lines.bit_length() - 1, LO.bit_length() - 1
     sub_iota = lax.broadcasted_iota(I32, (8, beads), 0)
+    scale = scale_ref[0:1, :]
     for q in range(count):
         own = jnp.broadcast_to(word[q : q + 1], (8, beads))
         lo, hi = own & (LO - 1), (own >> lo_shift) & 255
         line = hi & (lines - 1)
         group = (line >> 3) * tiles + (hi >> line_shift) * (LO // 128) + (lo >> 7)
         within, lane = (line & 7) == sub_iota, lo & 127
-        found = [jnp.zeros((8, beads), F32)] * 3
+        found = [jnp.zeros((8, beads), I32)] * 2
         for j in range(lines // 8 * tiles):
             here = group == j
             first, tile = j // tiles * 8, j % tiles * 128
-            for k in range(3):
-                table = exact_ref[k * lines + first : k * lines + first + 8, tile : tile + 128]
+            for k in range(2):
+                table = word_ref[k * lines + first : k * lines + first + 8, tile : tile + 128]
                 part = jnp.take_along_axis(table, lane, axis=1, mode="promise_in_bounds")
                 found[k] = jnp.where(here, part, found[k])
-        store(q, [jnp.sum(jnp.where(within, v, 0.0), axis=0, keepdims=True) for v in found])
+        one, two = [jnp.sum(jnp.where(within, v, 0), axis=0, keepdims=True) for v in found]
+        store(q, [v.astype(F32) * scale for v in unpack_three(one, two)])
 
 
 def sample_kernel(
-    lines, his, rb, by_lanes, start, got_ref, field_ref, exact_ref, out_ref, force_ref
+    lines, his, rb, by_lanes, start, got_ref, field_ref, word_ref, scale_ref, out_ref, force_ref
 ):
     slots = out_ref.shape[0]
     beads = got_ref.shape[1] // 3
@@ -358,7 +377,8 @@
 
         word = got_ref[pl.ds(start + i * rb, rb), 0:beads]
         finish = sample_by_matmul(word[:by_matmul], field_ref, his, store_from(0))
-        sample_by_lanes(word[by_matmul:], exact_ref, lines, store_from(by_matmul))
+        rest = word[by_matmul:]
+        sample_by_lanes(rest, word_ref, scale_ref, lines, store_from(by_matmul))
         finish()
         return carry
 
@@ -366,10 +386,7 @@
     rows = slice(start, start + slots)
     first, second = got_ref[rows, beads : 2 * beads], got_ref[rows, 2 * beads : 3 * beads]
     weight = (got_ref[rows, 0:beads] >> 16).astype(F32) * (1.0 / WEIGHT_SCALE)
-    lever_z = (((first & 2047) << 10) | (second & 1023)) - LEVER_BIAS
-    levers = [
-        v.astype(F32) * (1.0 / LEVER_SCALE) for v in (first >> 11, second >> 11, lever_z)
-    ]
+    levers = [v.astype(F32) * (1.0 / LEVER_SCALE) for v in unpack_three(first, second)]
     force = [force_ref[k] * weight for k in range(3)]
     terms = force + [
         levers[1] * force[2] - levers[2] * force[1],
@@ -588,7 +605,8 @@
     blocks = relay_blocks(coded, reach_two)
     field_shapes = [
         jax.ShapeDtypeStruct((3 * his, 2 * LO), BF16),
-        jax.ShapeDtypeStruct((3 * lines, rows), F32),
+        jax.ShapeDtypeStruct((2 * lines, rows), I32),
+        jax.ShapeDtypeStruct((8, 128), F32),
     ]
     target_field = call_at(
         functools.partial(target_kernel, lines),
@@ -601,7 +619,7 @@
     def sample(field, start, count, name):
         rb = min(32, count)
         return call(
-            functools.partial(sample_kernel, lines, his, rb, rb * 5 // 16, start),
+            functools.partial(sample_kernel, lines, his, rb, rb * BY_LANES // 32, start),
             jax.ShapeDtypeStruct((count, 128), F32),
             got, *field,
             scratch=[pltpu.VMEM((3, count, beads), F32)],

time: 60.6 us -> 58.7 us (0.969)
  Pallas kernels: 27 us -> 24.9 us
    pallas_call x9, Pallas kernels: 27 us -> 24.9 us  [call(): pl.pallas_call(kernel, out_shape=out_shape, scratch_shapes=list(scratch),...]
  transfers between devices with their start and end apart: 7 -> 7, of which waited for: 3 -> 3; matrix products, arithmetic and copies ran while one was open for 2% -> 2% of each run, Pallas kernels for 23% -> 22%
where the time goes in v11:
time: 58.7 us; the launch traced here: 58.4 us
  Pallas kernels  24.9 us (42%)
  starting transfers between devices  14.8 us (25%)
  blocking collectives  11.7 us (20%)
  waiting for transfers between devices  5.6 us (10%)
  local copies, waits for them, and re-layouts  1.12 us (2%)
    pallas_call x9, Pallas kernels, call(): pl.pallas_call(kernel, out_shape=out_shape, scratch_shapes=list(scratch),...  24.9 us
    all_to_all x1, blocking collectives, shards(): lax.all_to_all(leaving, 'brick', split_axis=0, concat_axis=0, tiled=True)  11.7 us
    all_to_all x1, starting transfers between devices, shards(): got = lax.all_to_all(sent, 'brick', split_axis=0, concat_axis=0, tiled=True)  7.38 us
    ppermute x4, starting transfers between devices, swapped(): lax.ppermute(value, 'brick', pairs + [(j, i) for i, j in pairs])  4.29 us
    ppermute x2, starting transfers between devices, relay_blocks(): return [value, lax.ppermute(value, 'relay', [(0, 1), (1, 0)])]  3.15 us
    ppermute x2, waiting for transfers between devices, relay_blocks(): return [value, lax.ppermute(value, 'relay', [(0, 1), (1, 0)])]  3.01 us
    all_to_all x1, waiting for transfers between devices, shards(): got = lax.all_to_all(sent, 'brick', split_axis=0, concat_axis=0, tiled=True)  2.58 us
  transfers between devices with their start and end apart: 7, of which 3 were waited for; matrix products, arithmetic and copies ran while one was open for 2% of the time, Pallas kernels for 22%

profile of v11, /device:TPU:0, one launch (start us, length us, event | category | flops | bytes accessed | tf_op | source)
XLA Modules:
  0.0 58.4 jit_solution(4257448876710249017)
XLA Ops:
  0.0 2.3 %pack.1 = (s32[128,384]{1,0:T(8,128)}, s32[8,64]{1,0:T(8,128)}, s32[16,1664]{1,0:T(8,128)}) custom-call(s32[1,64]{1,0:T(1,128)} %bitcast.23, f32[3,64]{1,0:T(4,128)} %refs_1_.1, s32[64,128]{1,0:T(8,128)} %refs_2_.1, bf16[64,128]{1,0:T(8,128)(2,1)} %refs_3_.1, f32[3,64,128]{2,1,0:T(8,128)} %refs_4_.1, f32[32,1536]{1,0:T(8,128)} %bitcast.11), custom_call_target="tpu_custom_call" | custom-call | bytes 361472 | tf_op jit(solution)/shard_map/pack/pallas_call | solution.py:453
  2.3 7.4 %all-to-all-start = ((s32[16,8,384]{2,1,0:T(8,128)}), s32[16,8,384]{2,1,0:T(8,128)S(1)}, u32[]{:S(2)}, u32[]{:S(2)}) async-start(s32[16,8,384]{2,1,0:T(8,128)} %bitcast.21), calls=%async_computation | async-start | bytes 393216 | tf_op jit(solution)/shard_map/all_to_all | solution.py:594
  9.6 1.6 %collective-permute-start = (s32[16,1664]{1,0:T(8,128)}, s32[16,1664]{1,0:T(8,128)S(1)}, u32[]{:S(2)}, u32[]{:S(2)}) collective-permute-start(s32[16,1664]{1,0:T(8,128)} %get-tuple-element.34), channel_id=1, source_target_pairs={{0,1},{1,0},{2,3},{3,2},{4,5},{5,4},{6,7},{7,6},{8,9},{9,8},{10,11... | collective-permute-start | bytes 319496 | tf_op jit(solution)/shard_map/ppermute | solution.py:507
  11.2 1.0 %fusion.2 = (s32[2,4,1664]{2,1,0:T(4,128)S(1)}, s32[2,4,1664]{2,1,0:T(4,128)S(1)}) fusion(s32[2,8,1664]{2,1,0:T(8,128)} %bitcast.22), kind=kLoop, calls=%fused_computation.6 | loop fusion | bytes 212992 | tf_op jit(solution)/shard_map/slice | solution.py:586
  12.3 2.9 %collective-permute-done.refs_0_ = s32[16,1664]{1,0:T(8,128)S(1)} collective-permute-done((s32[16,1664]{1,0:T(8,128)}, s32[16,1664]{1,0:T(8,128)S(1)}, u32[]{:S(2)}, u32[]{:S(2)}) %collective-permute-start) | collective-permute-done | bytes 106528 | tf_op jit(solution)/shard_map/ppermute | solution.py:507
  15.3 0.1 collective-permute-start.1
  15.4 0.7 %collective-permute-start.2 = (s32[16,1664]{1,0:T(8,128)S(1)}, s32[16,1664]{1,0:T(8,128)S(1)}, u32[]{:S(2)}, u32[]{:S(2)}) collective-permute-start(s32[16,1664]{1,0:T(8,128)S(1)} %select_n.34), channel_id=1, source_target_pairs={{2,4},{6,8},{10,12},{14,16},{18,20},{22,24},{26,28},{4,2},{8,6},{1... | collective-permute-start | bytes 319496 | tf_op jit(solution)/shard_map/ppermute | solution.py:500
  16.1 2.6 %all-to-all-done = s32[16,8,384]{2,1,0:T(8,128)S(1)} async-done(((s32[16,8,384]{2,1,0:T(8,128)}), s32[16,8,384]{2,1,0:T(8,128)S(1)}, u32[]{:S(2)}, u32[]{:S(2)}) %all-to-all-start) | async-done | bytes 196640 | tf_op jit(solution)/shard_map/all_to_all | solution.py:594
  18.6 0.0 copy-start
  18.6 3.8 %splat.1 = (f32[32,1536]{1,0:T(8,128)S(1)}, s32[16,1664]{1,0:T(8,128)S(1)}) custom-call(s32[128,384]{1,0:T(8,128)S(1)} %bitcast.15), custom_call_target="tpu_custom_call" | custom-call | flops 1610612736 | bytes 196608 | tf_op jit(solution)/shard_map/splat/pallas_call | solution.py:453
  22.5 0.0 collective-permute-done.1.refs_1_
  22.5 0.0 collective-permute-done.2.refs_2_
  22.5 1.6 %collective-permute-start.3 = (s32[16,1664]{1,0:T(8,128)S(1)}, s32[16,1664]{1,0:T(8,128)S(1)}, u32[]{:S(2)}, u32[]{:S(2)}) collective-permute-start(s32[16,1664]{1,0:T(8,128)S(1)} %get-tuple-element.47), channel_id=1, source_target_pairs={{0,1},{1,0},{2,3},{3,2},{4,5},{5,4},{6,7},{7,6},{8,9},{9,8},{10,11... | collective-permute-start | bytes 319496 | tf_op jit(solution)/shard_map/ppermute | solution.py:507
  24.1 0.0 copy-done
  24.1 0.0 copy-done.2
  24.1 1.9 %target_fields.1 = (bf16[576,512]{1,0:T(8,128)(2,1)S(1)}, s32[64,1536]{1,0:T(8,128)S(1)}, f32[8,128]{1,0:T(8,128)S(1)}) custom-call(s32[1]{0:T(128)} %bitcast.6.index_ref, bf16[8,96,384]{2,1,0:T(8,128)(2,1)S(1)} %copy-done.2, f32[32,1536]{1,0:T(8,128)S(1)} %bitcast.12, s32[16,1664]{1,0:T(8,128)S(1)} %collective-permute-done.refs_0_, ...), custom_call_target="tpu_custom_call" | custom-call | flops 113246208 | bytes 1695748 | tf_op jit(solution)/shard_map/target_fields/pallas_call | solution.py:453
  26.0 1.8 %target_sample_a.1.refs_0_ = f32[32,128]{1,0:T(8,128)S(1)} custom-call(s32[128,384]{1,0:T(8,128)S(1)} %bitcast.16, bf16[576,512]{1,0:T(8,128)(2,1)S(1)} %get-tuple-element.42.field_ref, s32[64,1536]{1,0:T(8,128)S(1)} %get-tuple-element.43.word_ref, f32[8,128]{1,0:T(8,128)S(1)} %get-tuple-element.44.scale_ref), custom_call_target="tpu_custom_call" | custom-call | flops 2415919104 | bytes 1773568 | tf_op jit(solution)/shard_map/target_sample_a/pallas_call | solution.py:453
  27.8 0.1 collective-permute-done.3.refs_2_
  27.9 0.0 copy-start.1
  27.9 1.0 %collective-permute-start.5 = (s32[32,1664]{1,0:T(8,128)S(1)}, s32[32,1664]{1,0:T(8,128)S(1)}, u32[]{:S(2)}, u32[]{:S(2)}) collective-permute-start(s32[32,1664]{1,0:T(8,128)S(1)} %constant_dynamic-update-slice_fusion), channel_id=1, source_target_pairs={{2,4},{6,8},{10,12},{14,16},{18,20},{22,24},{26,28},{4,2},{8,6},{1... | collective-permute-start | bytes 638984 | tf_op jit(solution)/shard_map/ppermute | solution.py:500
  28.9 2.6 %collective-permute-start.4 = (s32[32,1664]{1,0:T(8,128)S(1)}, s32[32,1664]{1,0:T(8,128)S(1)}, u32[]{:S(2)}, u32[]{:S(2)}) collective-permute-start(s32[32,1664]{1,0:T(8,128)S(1)} %constant_dynamic-update-slice_fusion), channel_id=1, source_target_pairs={{0,2},{4,6},{8,10},{12,14},{16,18},{20,22},{24,26},{28,30},{2,0},{... | collective-permute-start | bytes 638984 | tf_op jit(solution)/shard_map/ppermute | solution.py:500
  31.5 5.2 %target_sample_b.1.refs_1_ = f32[96,128]{1,0:T(8,128)S(1)} custom-call(s32[128,384]{1,0:T(8,128)S(1)} %bitcast.17, bf16[576,512]{1,0:T(8,128)(2,1)S(1)} %get-tuple-element.42.field_ref, s32[64,1536]{1,0:T(8,128)S(1)} %get-tuple-element.43.word_ref, f32[8,128]{1,0:T(8,128)S(1)} %get-tuple-element.44.scale_ref), custom_call_target="tpu_custom_call" | custom-call | flops 7247757312 | bytes 1773568 | tf_op jit(solution)/shard_map/target_sample_b/pallas_call | solution.py:453
  36.7 0.0 collective-permute-done.5.refs_4_
  36.7 0.0 collective-permute-done.4.refs_3_
  36.7 0.0 copy-done.1
  36.7 2.0 %model_fields.1 = (bf16[576,512]{1,0:T(8,128)(2,1)S(1)}, s32[64,1536]{1,0:T(8,128)S(1)}, f32[8,128]{1,0:T(8,128)S(1)}, f32[8,128]{1,0:T(8,128)S(1)}) custom-call(s32[1]{0:T(128)} %bitcast.6.index_ref, bf16[8,160,576]{2,1,0:T(8,128)(2,1)S(1)} %copy-done.1, f32[32,1536]{1,0:T(8,128)S(1)} %bitcast.13, s32[16,1664]{1,0:T(8,128)S(1)} %collective-permute-done.refs_0_, ...), custom_call_target="tpu_custom_call" | custom-call | bytes 3981316 | tf_op jit(solution)/shard_map/model_fields/pallas_call | solution.py:453
  38.7 0.0 copy-start.3
  38.8 6.9 %model_sample.1.refs_2_ = f32[128,128]{1,0:T(8,128)S(1)} custom-call(s32[128,384]{1,0:T(8,128)S(1)} %bitcast.18, bf16[576,512]{1,0:T(8,128)(2,1)S(1)} %get-tuple-element.53.field_ref, s32[64,1536]{1,0:T(8,128)S(1)} %get-tuple-element.54.word_ref, f32[8,128]{1,0:T(8,128)S(1)} %get-tuple-element.55.scale_ref), custom_call_target="tpu_custom_call" | custom-call | flops 9663676416 | bytes 1773568 | tf_op jit(solution)/shard_map/model_sample/pallas_call | solution.py:453
  45.7 0.2 join.1
  45.9 11.7 %all_to_all.22 = f32[16,1,128]{2,1,0:T(1,128)S(1)} all-to-all(f32[16,1,128]{2,1,0:T(1,128)S(1)} %bitcast.19), channel_id=1, replica_groups=mesh['brick'=16,'relay'=2] {'brick'}, dimensions={0} | all-to-all | bytes 16384 | tf_op jit(solution)/shard_map/all_to_all | solution.py:654
  57.5 0.0 copy-done.3
  57.5 0.9 %finish.1 = f32[6,64]{1,0:T(8,128)} custom-call(s32[8,64]{1,0:T(8,128)S(1)} %copy-done.3, f32[16,128]{1,0:T(8,128)S(1)} %bitcast.20), custom_call_target="tpu_custom_call" | custom-call | bytes 10240 | tf_op jit(solution)/shard_map/finish/pallas_call | solution.py:453
  (7 shorter events, 0.2 us)
Async XLA Ops:
  2.3 16.4 %all-to-all-start = ((s32[16,8,384]{2,1,0:T(8,128)}), s32[16,8,384]{2,1,0:T(8,128)S(1)}, u32[]{:S(2)}, u32[]{:S(2)}) async-start(s32[16,8,384]{2,1,0:T(8,128)} %bitcast.21), calls=%async_computation | async-start | bytes 393216 | tf_op jit(solution)/shard_map/all_to_all | solution.py:594
  9.6 5.5 %collective-permute-start = (s32[16,1664]{1,0:T(8,128)}, s32[16,1664]{1,0:T(8,128)S(1)}, u32[]{:S(2)}, u32[]{:S(2)}) collective-permute-start(s32[16,1664]{1,0:T(8,128)} %get-tuple-element.34), channel_id=1, source_target_pairs={{0,1},{1,0},{2,3},{3,2},{4,5},{5,4},{6,7},{7,6},{8,9},{9,8},{10,11... | collective-permute-start | bytes 319496 | tf_op jit(solution)/shard_map/ppermute | solution.py:507
  15.3 7.2 %collective-permute-start.1 = (s32[16,1664]{1,0:T(8,128)S(1)}, s32[16,1664]{1,0:T(8,128)S(1)}, u32[]{:S(2)}, u32[]{:S(2)}) collective-permute-start(s32[16,1664]{1,0:T(8,128)S(1)} %select_n.32), channel_id=1, source_target_pairs={{0,2},{4,6},{8,10},{12,14},{16,18},{20,22},{24,26},{28,30},{2,0},{... | collective-permute-start | bytes 319496 | tf_op jit(solution)/shard_map/ppermute | solution.py:500
  15.4 7.1 %collective-permute-start.2 = (s32[16,1664]{1,0:T(8,128)S(1)}, s32[16,1664]{1,0:T(8,128)S(1)}, u32[]{:S(2)}, u32[]{:S(2)}) collective-permute-start(s32[16,1664]{1,0:T(8,128)S(1)} %select_n.34), channel_id=1, source_target_pairs={{2,4},{6,8},{10,12},{14,16},{18,20},{22,24},{26,28},{4,2},{8,6},{1... | collective-permute-start | bytes 319496 | tf_op jit(solution)/shard_map/ppermute | solution.py:500
  18.6 5.4 %copy-start = (f32[4,8,1536]{2,1,0:T(8,128)S(1)}, f32[4,8,1536]{2,1,0:T(8,128)}, u32[]{:S(2)}) copy-start(f32[4,8,1536]{2,1,0:T(8,128)} %param.8) | copy-start | bytes 589828
  18.6 5.4 %copy-start.2 = (bf16[8,96,384]{2,1,0:T(8,128)(2,1)S(1)}, bf16[8,96,384]{2,1,0:T(8,128)(2,1)}, u32[]{:S(2)}) copy-start(bf16[8,96,384]{2,1,0:T(8,128)(2,1)} %constant.68.clone.tables_ref) | copy-start | bytes 1769476
  22.5 5.4 %collective-permute-start.3 = (s32[16,1664]{1,0:T(8,128)S(1)}, s32[16,1664]{1,0:T(8,128)S(1)}, u32[]{:S(2)}, u32[]{:S(2)}) collective-permute-start(s32[16,1664]{1,0:T(8,128)S(1)} %get-tuple-element.47), channel_id=1, source_target_pairs={{0,1},{1,0},{2,3},{3,2},{4,5},{5,4},{6,7},{7,6},{8,9},{9,8},{10,11... | collective-permute-start | bytes 319496 | tf_op jit(solution)/shard_map/ppermute | solution.py:507
  27.9 8.8 %copy-start.1 = (bf16[8,160,576]{2,1,0:T(8,128)(2,1)S(1)}, bf16[8,160,576]{2,1,0:T(8,128)(2,1)}, u32[]{:S(2)}) copy-start(bf16[8,160,576]{2,1,0:T(8,128)(2,1)} %constant.69.clone.tables_ref) | copy-start | bytes 4423684
  27.9 8.7 %collective-permute-start.5 = (s32[32,1664]{1,0:T(8,128)S(1)}, s32[32,1664]{1,0:T(8,128)S(1)}, u32[]{:S(2)}, u32[]{:S(2)}) collective-permute-start(s32[32,1664]{1,0:T(8,128)S(1)} %constant_dynamic-update-slice_fusion), channel_id=1, source_target_pairs={{2,4},{6,8},{10,12},{14,16},{18,20},{22,24},{26,28},{4,2},{8,6},{1... | collective-permute-start | bytes 638984 | tf_op jit(solution)/shard_map/ppermute | solution.py:500
  28.9 7.8 %collective-permute-start.4 = (s32[32,1664]{1,0:T(8,128)S(1)}, s32[32,1664]{1,0:T(8,128)S(1)}, u32[]{:S(2)}, u32[]{:S(2)}) collective-permute-start(s32[32,1664]{1,0:T(8,128)S(1)} %constant_dynamic-update-slice_fusion), channel_id=1, source_target_pairs={{0,2},{4,6},{8,10},{12,14},{16,18},{20,22},{24,26},{28,30},{2,0},{... | collective-permute-start | bytes 638984 | tf_op jit(solution)/shard_map/ppermute | solution.py:500
  38.7 18.8 %copy-start.3 = (s32[8,64]{1,0:T(8,128)S(1)}, s32[8,64]{1,0:T(8,128)}, u32[]{:S(2)}) copy-start(s32[8,64]{1,0:T(8,128)} %get-tuple-element.31.place_ref) | copy-start | bytes 6148

commit v12 on v11

--- a/solution.py
+++ b/solution.py
@@ -124,7 +124,7 @@
     row = brick_ref[...]
     rank, eye = slot_row(row, most)
     slot = row * most + rank
-    place = jnp.where(lax.broadcasted_iota(I32, (slots, frags), 0) == slot, 1.0, 0.0).astype(F32)
+    place = jnp.where(lax.broadcasted_iota(I32, (slots, frags), 0) == slot, 1.0, 0.0).astype(BF16)
 
     angles = angle_ref[...]
     cos, sin = jnp.cos(angles), jnp.sin(angles)
@@ -146,17 +146,24 @@
         total = turn[i][0] * arm_ref[0]
         for j in (1, 2):
             total = total + turn[i][j] * arm_ref[j]
-        levers.append(jnp.round(total * LEVER_SCALE))
+        lever = jnp.round(total * LEVER_SCALE).astype(I32)
+        levers += [lever >> 14, (lever >> 7) & 127, lever & 127]
 
     cell = cell_ref[...]
     line = ((cell.astype(F32) + 0.5) * (1.0 / row_count)).astype(I32)
     y = cell - line * row_count
-    code = (((y // LO) * lines + line) * LO + (y % LO)).astype(F32)
     weight = weight_ref[...].astype(F32) * WEIGHT_SCALE
-    payload = jnp.concatenate([code, weight] + levers, axis=1)
-    placed = jnp.dot(place, payload, precision=HIGHEST, preferred_element_type=F32)
-    placed = placed.astype(I32)
-    code, weight, lx, ly, lz = [placed[:, k * beads : (k + 1) * beads] for k in range(5)]
+    pieces = [(y // LO) * lines + line, y % LO] + levers
+    pieces = [weight.astype(BF16)] + [v.astype(F32).astype(BF16) for v in pieces]
+    payload = jnp.concatenate(pieces, axis=1)
+    placed = jnp.dot(place, payload, preferred_element_type=F32).astype(I32)
+    weight, hi, lo, *levers = [
+        placed[:, k * beads : (k + 1) * beads] for k in range(len(pieces))
+    ]
+    code = (hi << 8) | lo
+    lx, ly, lz = [
+        (levers[k] << 14) + (levers[k + 1] << 7) + levers[k + 2] for k in (0, 3, 6)
+    ]
     one, two = pack_three(lx, ly, lz)
     out_ref[:, 0:beads] = code | (weight << 16)
     out_ref[:, beads : 2 * beads] = one

time: 58.7 us -> 58.6 us (level)
  no operation moved by 1% of the time
where the time goes in v12:
time: 58.6 us; the launch traced here: 58.3 us
  Pallas kernels  24.8 us (42%)
  starting transfers between devices  14.8 us (25%)
  blocking collectives  11.7 us (20%)
  waiting for transfers between devices  5.58 us (10%)
  local copies, waits for them, and re-layouts  1.12 us (2%)
    pallas_call x9, Pallas kernels, call(): pl.pallas_call(kernel, out_shape=out_shape, scratch_shapes=list(scratch),...  24.8 us
    all_to_all x1, blocking collectives, shards(): lax.all_to_all(leaving, 'brick', split_axis=0, concat_axis=0, tiled=True)  11.7 us
    all_to_all x1, starting transfers between devices, shards(): got = lax.all_to_all(sent, 'brick', split_axis=0, concat_axis=0, tiled=True)  7.37 us
    ppermute x4, starting transfers between devices, swapped(): lax.ppermute(value, 'brick', pairs + [(j, i) for i, j in pairs])  4.29 us
    ppermute x2, starting transfers between devices, relay_blocks(): return [value, lax.ppermute(value, 'relay', [(0, 1), (1, 0)])]  3.17 us
    ppermute x2, waiting for transfers between devices, relay_blocks(): return [value, lax.ppermute(value, 'relay', [(0, 1), (1, 0)])]  2.99 us
    all_to_all x1, waiting for transfers between devices, shards(): got = lax.all_to_all(sent, 'brick', split_axis=0, concat_axis=0, tiled=True)  2.58 us
  transfers between devices with their start and end apart: 7, of which 3 were waited for; matrix products, arithmetic and copies ran while one was open for 2% of the time, Pallas kernels for 22%

profile of v12, /device:TPU:0, one launch (start us, length us, event | category | flops | bytes accessed | tf_op | source)
XLA Modules:
  0.0 58.3 jit_solution(12087551705540866894)
XLA Ops:
  0.0 2.2 %pack.1 = (s32[128,384]{1,0:T(8,128)}, s32[8,64]{1,0:T(8,128)}, s32[16,1664]{1,0:T(8,128)}) custom-call(s32[1,64]{1,0:T(1,128)} %bitcast.23, f32[3,64]{1,0:T(4,128)} %refs_1_.1, s32[64,128]{1,0:T(8,128)} %refs_2_.1, bf16[64,128]{1,0:T(8,128)(2,1)} %refs_3_.1, f32[3,64,128]{2,1,0:T(8,128)} %refs_4_.1, f32[32,1536]{1,0:T(8,128)} %bitcast.11), custom_call_target="tpu_custom_call" | custom-call | bytes 361472 | tf_op jit(solution)/shard_map/pack/pallas_call | solution.py:460
  2.2 7.4 %all-to-all-start = ((s32[16,8,384]{2,1,0:T(8,128)}), s32[16,8,384]{2,1,0:T(8,128)S(1)}, u32[]{:S(2)}, u32[]{:S(2)}) async-start(s32[16,8,384]{2,1,0:T(8,128)} %bitcast.21), calls=%async_computation | async-start | bytes 393216 | tf_op jit(solution)/shard_map/all_to_all | solution.py:601
  9.6 1.6 %collective-permute-start = (s32[16,1664]{1,0:T(8,128)}, s32[16,1664]{1,0:T(8,128)S(1)}, u32[]{:S(2)}, u32[]{:S(2)}) collective-permute-start(s32[16,1664]{1,0:T(8,128)} %get-tuple-element.34), channel_id=1, source_target_pairs={{0,1},{1,0},{2,3},{3,2},{4,5},{5,4},{6,7},{7,6},{8,9},{9,8},{10,11... | collective-permute-start | bytes 319496 | tf_op jit(solution)/shard_map/ppermute | solution.py:514
  11.1 1.0 %fusion.2 = (s32[2,4,1664]{2,1,0:T(4,128)S(1)}, s32[2,4,1664]{2,1,0:T(4,128)S(1)}) fusion(s32[2,8,1664]{2,1,0:T(8,128)} %bitcast.22), kind=kLoop, calls=%fused_computation.6 | loop fusion | bytes 212992 | tf_op jit(solution)/shard_map/slice | solution.py:593
  12.2 2.9 %collective-permute-done.refs_0_ = s32[16,1664]{1,0:T(8,128)S(1)} collective-permute-done((s32[16,1664]{1,0:T(8,128)}, s32[16,1664]{1,0:T(8,128)S(1)}, u32[]{:S(2)}, u32[]{:S(2)}) %collective-permute-start) | collective-permute-done | bytes 106528 | tf_op jit(solution)/shard_map/ppermute | solution.py:514
  15.2 0.1 collective-permute-start.1
  15.3 0.7 %collective-permute-start.2 = (s32[16,1664]{1,0:T(8,128)S(1)}, s32[16,1664]{1,0:T(8,128)S(1)}, u32[]{:S(2)}, u32[]{:S(2)}) collective-permute-start(s32[16,1664]{1,0:T(8,128)S(1)} %select_n.34), channel_id=1, source_target_pairs={{2,4},{6,8},{10,12},{14,16},{18,20},{22,24},{26,28},{4,2},{8,6},{1... | collective-permute-start | bytes 319496 | tf_op jit(solution)/shard_map/ppermute | solution.py:507
  16.0 2.6 %all-to-all-done = s32[16,8,384]{2,1,0:T(8,128)S(1)} async-done(((s32[16,8,384]{2,1,0:T(8,128)}), s32[16,8,384]{2,1,0:T(8,128)S(1)}, u32[]{:S(2)}, u32[]{:S(2)}) %all-to-all-start) | async-done | bytes 196640 | tf_op jit(solution)/shard_map/all_to_all | solution.py:601
  18.6 0.0 copy-start
  18.6 3.8 %splat.1 = (f32[32,1536]{1,0:T(8,128)S(1)}, s32[16,1664]{1,0:T(8,128)S(1)}) custom-call(s32[128,384]{1,0:T(8,128)S(1)} %bitcast.15), custom_call_target="tpu_custom_call" | custom-call | flops 1610612736 | bytes 196608 | tf_op jit(solution)/shard_map/splat/pallas_call | solution.py:460
  22.4 0.0 collective-permute-done.1.refs_1_
  22.4 0.0 collective-permute-done.2.refs_2_
  22.4 1.6 %collective-permute-start.3 = (s32[16,1664]{1,0:T(8,128)S(1)}, s32[16,1664]{1,0:T(8,128)S(1)}, u32[]{:S(2)}, u32[]{:S(2)}) collective-permute-start(s32[16,1664]{1,0:T(8,128)S(1)} %get-tuple-element.47), channel_id=1, source_target_pairs={{0,1},{1,0},{2,3},{3,2},{4,5},{5,4},{6,7},{7,6},{8,9},{9,8},{10,11... | collective-permute-start | bytes 319496 | tf_op jit(solution)/shard_map/ppermute | solution.py:514
  24.0 0.0 copy-done
  24.0 0.0 copy-done.2
  24.0 1.9 %target_fields.1 = (bf16[576,512]{1,0:T(8,128)(2,1)S(1)}, s32[64,1536]{1,0:T(8,128)S(1)}, f32[8,128]{1,0:T(8,128)S(1)}) custom-call(s32[1]{0:T(128)} %bitcast.6.index_ref, bf16[8,96,384]{2,1,0:T(8,128)(2,1)S(1)} %copy-done.2, f32[32,1536]{1,0:T(8,128)S(1)} %bitcast.12, s32[16,1664]{1,0:T(8,128)S(1)} %collective-permute-done.refs_0_, ...), custom_call_target="tpu_custom_call" | custom-call | flops 113246208 | bytes 1695748 | tf_op jit(solution)/shard_map/target_fields/pallas_call | solution.py:460
  25.9 1.8 %target_sample_a.1.refs_0_ = f32[32,128]{1,0:T(8,128)S(1)} custom-call(s32[128,384]{1,0:T(8,128)S(1)} %bitcast.16, bf16[576,512]{1,0:T(8,128)(2,1)S(1)} %get-tuple-element.42.field_ref, s32[64,1536]{1,0:T(8,128)S(1)} %get-tuple-element.43.word_ref, f32[8,128]{1,0:T(8,128)S(1)} %get-tuple-element.44.scale_ref), custom_call_target="tpu_custom_call" | custom-call | flops 2415919104 | bytes 1773568 | tf_op jit(solution)/shard_map/target_sample_a/pallas_call | solution.py:460
  27.7 0.1 collective-permute-done.3.refs_2_
  27.8 0.0 copy-start.1
  27.9 1.0 %collective-permute-start.5 = (s32[32,1664]{1,0:T(8,128)S(1)}, s32[32,1664]{1,0:T(8,128)S(1)}, u32[]{:S(2)}, u32[]{:S(2)}) collective-permute-start(s32[32,1664]{1,0:T(8,128)S(1)} %constant_dynamic-update-slice_fusion), channel_id=1, source_target_pairs={{2,4},{6,8},{10,12},{14,16},{18,20},{22,24},{26,28},{4,2},{8,6},{1... | collective-permute-start | bytes 638984 | tf_op jit(solution)/shard_map/ppermute | solution.py:507
  28.9 2.6 %collective-permute-start.4 = (s32[32,1664]{1,0:T(8,128)S(1)}, s32[32,1664]{1,0:T(8,128)S(1)}, u32[]{:S(2)}, u32[]{:S(2)}) collective-permute-start(s32[32,1664]{1,0:T(8,128)S(1)} %constant_dynamic-update-slice_fusion), channel_id=1, source_target_pairs={{0,2},{4,6},{8,10},{12,14},{16,18},{20,22},{24,26},{28,30},{2,0},{... | collective-permute-start | bytes 638984 | tf_op jit(solution)/shard_map/ppermute | solution.py:507
  31.4 5.2 %target_sample_b.1.refs_1_ = f32[96,128]{1,0:T(8,128)S(1)} custom-call(s32[128,384]{1,0:T(8,128)S(1)} %bitcast.17, bf16[576,512]{1,0:T(8,128)(2,1)S(1)} %get-tuple-element.42.field_ref, s32[64,1536]{1,0:T(8,128)S(1)} %get-tuple-element.43.word_ref, f32[8,128]{1,0:T(8,128)S(1)} %get-tuple-element.44.scale_ref), custom_call_target="tpu_custom_call" | custom-call | flops 7247757312 | bytes 1773568 | tf_op jit(solution)/shard_map/target_sample_b/pallas_call | solution.py:460
  36.6 0.0 collective-permute-done.5.refs_4_
  36.6 0.0 collective-permute-done.4.refs_3_
  36.6 0.0 copy-done.1
  36.6 2.0 %model_fields.1 = (bf16[576,512]{1,0:T(8,128)(2,1)S(1)}, s32[64,1536]{1,0:T(8,128)S(1)}, f32[8,128]{1,0:T(8,128)S(1)}, f32[8,128]{1,0:T(8,128)S(1)}) custom-call(s32[1]{0:T(128)} %bitcast.6.index_ref, bf16[8,160,576]{2,1,0:T(8,128)(2,1)S(1)} %copy-done.1, f32[32,1536]{1,0:T(8,128)S(1)} %bitcast.13, s32[16,1664]{1,0:T(8,128)S(1)} %collective-permute-done.refs_0_, ...), custom_call_target="tpu_custom_call" | custom-call | bytes 3981316 | tf_op jit(solution)/shard_map/model_fields/pallas_call | solution.py:460
  38.7 0.0 copy-start.3
  38.7 6.9 %model_sample.1.refs_2_ = f32[128,128]{1,0:T(8,128)S(1)} custom-call(s32[128,384]{1,0:T(8,128)S(1)} %bitcast.18, bf16[576,512]{1,0:T(8,128)(2,1)S(1)} %get-tuple-element.53.field_ref, s32[64,1536]{1,0:T(8,128)S(1)} %get-tuple-element.54.word_ref, f32[8,128]{1,0:T(8,128)S(1)} %get-tuple-element.55.scale_ref), custom_call_target="tpu_custom_call" | custom-call | flops 9663676416 | bytes 1773568 | tf_op jit(solution)/shard_map/model_sample/pallas_call | solution.py:460
  45.6 0.2 join.1
  45.8 11.7 %all_to_all.22 = f32[16,1,128]{2,1,0:T(1,128)S(1)} all-to-all(f32[16,1,128]{2,1,0:T(1,128)S(1)} %bitcast.19), channel_id=1, replica_groups=mesh['brick'=16,'relay'=2] {'brick'}, dimensions={0} | all-to-all | bytes 16384 | tf_op jit(solution)/shard_map/all_to_all | solution.py:661
  57.4 0.0 copy-done.3
  57.4 0.9 %finish.1 = f32[6,64]{1,0:T(8,128)} custom-call(s32[8,64]{1,0:T(8,128)S(1)} %copy-done.3, f32[16,128]{1,0:T(8,128)S(1)} %bitcast.20), custom_call_target="tpu_custom_call" | custom-call | bytes 10240 | tf_op jit(solution)/shard_map/finish/pallas_call | solution.py:460
  (7 shorter events, 0.2 us)
Async XLA Ops:
  2.2 16.4 %all-to-all-start = ((s32[16,8,384]{2,1,0:T(8,128)}), s32[16,8,384]{2,1,0:T(8,128)S(1)}, u32[]{:S(2)}, u32[]{:S(2)}) async-start(s32[16,8,384]{2,1,0:T(8,128)} %bitcast.21), calls=%async_computation | async-start | bytes 393216 | tf_op jit(solution)/shard_map/all_to_all | solution.py:601
  9.6 5.5 %collective-permute-start = (s32[16,1664]{1,0:T(8,128)}, s32[16,1664]{1,0:T(8,128)S(1)}, u32[]{:S(2)}, u32[]{:S(2)}) collective-permute-start(s32[16,1664]{1,0:T(8,128)} %get-tuple-element.34), channel_id=1, source_target_pairs={{0,1},{1,0},{2,3},{3,2},{4,5},{5,4},{6,7},{7,6},{8,9},{9,8},{10,11... | collective-permute-start | bytes 319496 | tf_op jit(solution)/shard_map/ppermute | solution.py:514
  15.2 7.2 %collective-permute-start.1 = (s32[16,1664]{1,0:T(8,128)S(1)}, s32[16,1664]{1,0:T(8,128)S(1)}, u32[]{:S(2)}, u32[]{:S(2)}) collective-permute-start(s32[16,1664]{1,0:T(8,128)S(1)} %select_n.32), channel_id=1, source_target_pairs={{0,2},{4,6},{8,10},{12,14},{16,18},{20,22},{24,26},{28,30},{2,0},{... | collective-permute-start | bytes 319496 | tf_op jit(solution)/shard_map/ppermute | solution.py:507
  15.3 7.1 %collective-permute-start.2 = (s32[16,1664]{1,0:T(8,128)S(1)}, s32[16,1664]{1,0:T(8,128)S(1)}, u32[]{:S(2)}, u32[]{:S(2)}) collective-permute-start(s32[16,1664]{1,0:T(8,128)S(1)} %select_n.34), channel_id=1, source_target_pairs={{2,4},{6,8},{10,12},{14,16},{18,20},{22,24},{26,28},{4,2},{8,6},{1... | collective-permute-start | bytes 319496 | tf_op jit(solution)/shard_map/ppermute | solution.py:507
  18.6 5.4 %copy-start = (f32[4,8,1536]{2,1,0:T(8,128)S(1)}, f32[4,8,1536]{2,1,0:T(8,128)}, u32[]{:S(2)}) copy-start(f32[4,8,1536]{2,1,0:T(8,128)} %param.8) | copy-start | bytes 589828
  18.6 5.4 %copy-start.2 = (bf16[8,96,384]{2,1,0:T(8,128)(2,1)S(1)}, bf16[8,96,384]{2,1,0:T(8,128)(2,1)}, u32[]{:S(2)}) copy-start(bf16[8,96,384]{2,1,0:T(8,128)(2,1)} %constant.68.clone.tables_ref) | copy-start | bytes 1769476
  22.4 5.4 %collective-permute-start.3 = (s32[16,1664]{1,0:T(8,128)S(1)}, s32[16,1664]{1,0:T(8,128)S(1)}, u32[]{:S(2)}, u32[]{:S(2)}) collective-permute-start(s32[16,1664]{1,0:T(8,128)S(1)} %get-tuple-element.47), channel_id=1, source_target_pairs={{0,1},{1,0},{2,3},{3,2},{4,5},{5,4},{6,7},{7,6},{8,9},{9,8},{10,11... | collective-permute-start | bytes 319496 | tf_op jit(solution)/shard_map/ppermute | solution.py:514
  27.8 8.8 %copy-start.1 = (bf16[8,160,576]{2,1,0:T(8,128)(2,1)S(1)}, bf16[8,160,576]{2,1,0:T(8,128)(2,1)}, u32[]{:S(2)}) copy-start(bf16[8,160,576]{2,1,0:T(8,128)(2,1)} %constant.69.clone.tables_ref) | copy-start | bytes 4423684
  27.9 8.7 %collective-permute-start.5 = (s32[32,1664]{1,0:T(8,128)S(1)}, s32[32,1664]{1,0:T(8,128)S(1)}, u32[]{:S(2)}, u32[]{:S(2)}) collective-permute-start(s32[32,1664]{1,0:T(8,128)S(1)} %constant_dynamic-update-slice_fusion), channel_id=1, source_target_pairs={{2,4},{6,8},{10,12},{14,16},{18,20},{22,24},{26,28},{4,2},{8,6},{1... | collective-permute-start | bytes 638984 | tf_op jit(solution)/shard_map/ppermute | solution.py:507
  28.9 7.7 %collective-permute-start.4 = (s32[32,1664]{1,0:T(8,128)S(1)}, s32[32,1664]{1,0:T(8,128)S(1)}, u32[]{:S(2)}, u32[]{:S(2)}) collective-permute-start(s32[32,1664]{1,0:T(8,128)S(1)} %constant_dynamic-update-slice_fusion), channel_id=1, source_target_pairs={{0,2},{4,6},{8,10},{12,14},{16,18},{20,22},{24,26},{28,30},{2,0},{... | collective-permute-start | bytes 638984 | tf_op jit(solution)/shard_map/ppermute | solution.py:507
  38.7 18.8 %copy-start.3 = (s32[8,64]{1,0:T(8,128)S(1)}, s32[8,64]{1,0:T(8,128)}, u32[]{:S(2)}) copy-start(s32[8,64]{1,0:T(8,128)} %get-tuple-element.31.place_ref) | copy-start | bytes 6148

commit v13 on v12

--- a/solution.py
+++ b/solution.py
@@ -138,9 +138,8 @@
     turn = [[eye_column(value, eye) for value in values] for values in turn]
     place_ref[0:1, :] = row
     place_ref[1:2, :] = rank
-    for copy in copies[2:]:
+    for copy in copies[2:5]:
         copy.wait()
-    encode(target_ref[...], code_ref)
     levers = []
     for i in range(3):
         total = turn[i][0] * arm_ref[0]
@@ -168,6 +167,8 @@
     out_ref[:, 0:beads] = code | (weight << 16)
     out_ref[:, beads : 2 * beads] = one
     out_ref[:, 2 * beads : 3 * beads] = two
+    copies[5].wait()
+    encode(target_ref[...], code_ref)
 
 
 def line_blur(value, derivative):

time: 58.6 us -> 58.6 us (level)
  no operation moved by 1% of the time
where the time goes in v13:
time: 58.6 us; the launch traced here: 58.3 us
  Pallas kernels  24.8 us (42%)
  starting transfers between devices  14.8 us (25%)
  blocking collectives  11.7 us (20%)
  waiting for transfers between devices  5.6 us (10%)
  local copies, waits for them, and re-layouts  1.12 us (2%)
    pallas_call x9, Pallas kernels, call(): pl.pallas_call(kernel, out_shape=out_shape, scratch_shapes=list(scratch),...  24.8 us
    all_to_all x1, blocking collectives, shards(): lax.all_to_all(leaving, 'brick', split_axis=0, concat_axis=0, tiled=True)  11.7 us
    all_to_all x1, starting transfers between devices, shards(): got = lax.all_to_all(sent, 'brick', split_axis=0, concat_axis=0, tiled=True)  7.38 us
    ppermute x4, starting transfers between devices, swapped(): lax.ppermute(value, 'brick', pairs + [(j, i) for i, j in pairs])  4.29 us
    ppermute x2, starting transfers between devices, relay_blocks(): return [value, lax.ppermute(value, 'relay', [(0, 1), (1, 0)])]  3.15 us
    ppermute x2, waiting for transfers between devices, relay_blocks(): return [value, lax.ppermute(value, 'relay', [(0, 1), (1, 0)])]  3.01 us
    all_to_all x1, waiting for transfers between devices, shards(): got = lax.all_to_all(sent, 'brick', split_axis=0, concat_axis=0, tiled=True)  2.58 us
  transfers between devices with their start and end apart: 7, of which 3 were waited for; matrix products, arithmetic and copies ran while one was open for 2% of the time, Pallas kernels for 22%

profile of v13, /device:TPU:0, one launch (start us, length us, event | category | flops | bytes accessed | tf_op | source)
XLA Modules:
  0.0 58.3 jit_solution(3024836774879668766)
XLA Ops:
  0.0 2.2 %pack.1 = (s32[128,384]{1,0:T(8,128)}, s32[8,64]{1,0:T(8,128)}, s32[16,1664]{1,0:T(8,128)}) custom-call(s32[1,64]{1,0:T(1,128)} %bitcast.23, f32[3,64]{1,0:T(4,128)} %refs_1_.1, s32[64,128]{1,0:T(8,128)} %refs_2_.1, bf16[64,128]{1,0:T(8,128)(2,1)} %refs_3_.1, f32[3,64,128]{2,1,0:T(8,128)} %refs_4_.1, f32[32,1536]{1,0:T(8,128)} %bitcast.11), custom_call_target="tpu_custom_call" | custom-call | bytes 361472 | tf_op jit(solution)/shard_map/pack/pallas_call | solution.py:461
  2.2 7.4 %all-to-all-start = ((s32[16,8,384]{2,1,0:T(8,128)}), s32[16,8,384]{2,1,0:T(8,128)S(1)}, u32[]{:S(2)}, u32[]{:S(2)}) async-start(s32[16,8,384]{2,1,0:T(8,128)} %bitcast.21), calls=%async_computation | async-start | bytes 393216 | tf_op jit(solution)/shard_map/all_to_all | solution.py:602
  9.6 1.6 %collective-permute-start = (s32[16,1664]{1,0:T(8,128)}, s32[16,1664]{1,0:T(8,128)S(1)}, u32[]{:S(2)}, u32[]{:S(2)}) collective-permute-start(s32[16,1664]{1,0:T(8,128)} %get-tuple-element.34), channel_id=1, source_target_pairs={{0,1},{1,0},{2,3},{3,2},{4,5},{5,4},{6,7},{7,6},{8,9},{9,8},{10,11... | collective-permute-start | bytes 319496 | tf_op jit(solution)/shard_map/ppermute | solution.py:515
  11.2 1.0 %fusion.2 = (s32[2,4,1664]{2,1,0:T(4,128)S(1)}, s32[2,4,1664]{2,1,0:T(4,128)S(1)}) fusion(s32[2,8,1664]{2,1,0:T(8,128)} %bitcast.22), kind=kLoop, calls=%fused_computation.6 | loop fusion | bytes 212992 | tf_op jit(solution)/shard_map/slice | solution.py:594
  12.2 2.9 %collective-permute-done.refs_0_ = s32[16,1664]{1,0:T(8,128)S(1)} collective-permute-done((s32[16,1664]{1,0:T(8,128)}, s32[16,1664]{1,0:T(8,128)S(1)}, u32[]{:S(2)}, u32[]{:S(2)}) %collective-permute-start) | collective-permute-done | bytes 106528 | tf_op jit(solution)/shard_map/ppermute | solution.py:515
  15.2 0.1 collective-permute-start.1
  15.3 0.7 %collective-permute-start.2 = (s32[16,1664]{1,0:T(8,128)S(1)}, s32[16,1664]{1,0:T(8,128)S(1)}, u32[]{:S(2)}, u32[]{:S(2)}) collective-permute-start(s32[16,1664]{1,0:T(8,128)S(1)} %select_n.34), channel_id=1, source_target_pairs={{2,4},{6,8},{10,12},{14,16},{18,20},{22,24},{26,28},{4,2},{8,6},{1... | collective-permute-start | bytes 319496 | tf_op jit(solution)/shard_map/ppermute | solution.py:508
  16.0 2.6 %all-to-all-done = s32[16,8,384]{2,1,0:T(8,128)S(1)} async-done(((s32[16,8,384]{2,1,0:T(8,128)}), s32[16,8,384]{2,1,0:T(8,128)S(1)}, u32[]{:S(2)}, u32[]{:S(2)}) %all-to-all-start) | async-done | bytes 196640 | tf_op jit(solution)/shard_map/all_to_all | solution.py:602
  18.6 0.0 copy-start
  18.6 3.8 %splat.1 = (f32[32,1536]{1,0:T(8,128)S(1)}, s32[16,1664]{1,0:T(8,128)S(1)}) custom-call(s32[128,384]{1,0:T(8,128)S(1)} %bitcast.15), custom_call_target="tpu_custom_call" | custom-call | flops 1610612736 | bytes 196608 | tf_op jit(solution)/shard_map/splat/pallas_call | solution.py:461
  22.4 0.0 collective-permute-done.1.refs_1_
  22.4 0.0 collective-permute-done.2.refs_2_
  22.4 1.6 %collective-permute-start.3 = (s32[16,1664]{1,0:T(8,128)S(1)}, s32[16,1664]{1,0:T(8,128)S(1)}, u32[]{:S(2)}, u32[]{:S(2)}) collective-permute-start(s32[16,1664]{1,0:T(8,128)S(1)} %get-tuple-element.47), channel_id=1, source_target_pairs={{0,1},{1,0},{2,3},{3,2},{4,5},{5,4},{6,7},{7,6},{8,9},{9,8},{10,11... | collective-permute-start | bytes 319496 | tf_op jit(solution)/shard_map/ppermute | solution.py:515
  24.0 0.0 copy-done
  24.0 0.0 copy-done.2
  24.0 1.9 %target_fields.1 = (bf16[576,512]{1,0:T(8,128)(2,1)S(1)}, s32[64,1536]{1,0:T(8,128)S(1)}, f32[8,128]{1,0:T(8,128)S(1)}) custom-call(s32[1]{0:T(128)} %bitcast.6.index_ref, bf16[8,96,384]{2,1,0:T(8,128)(2,1)S(1)} %copy-done.2, f32[32,1536]{1,0:T(8,128)S(1)} %bitcast.12, s32[16,1664]{1,0:T(8,128)S(1)} %collective-permute-done.refs_0_, ...), custom_call_target="tpu_custom_call" | custom-call | flops 113246208 | bytes 1695748 | tf_op jit(solution)/shard_map/target_fields/pallas_call | solution.py:461
  25.9 1.8 %target_sample_a.1.refs_0_ = f32[32,128]{1,0:T(8,128)S(1)} custom-call(s32[128,384]{1,0:T(8,128)S(1)} %bitcast.16, bf16[576,512]{1,0:T(8,128)(2,1)S(1)} %get-tuple-element.42.field_ref, s32[64,1536]{1,0:T(8,128)S(1)} %get-tuple-element.43.word_ref, f32[8,128]{1,0:T(8,128)S(1)} %get-tuple-element.44.scale_ref), custom_call_target="tpu_custom_call" | custom-call | flops 2415919104 | bytes 1773568 | tf_op jit(solution)/shard_map/target_sample_a/pallas_call | solution.py:461
  27.7 0.1 collective-permute-done.3.refs_2_
  27.9 0.0 copy-start.1
  27.9 1.0 %collective-permute-start.5 = (s32[32,1664]{1,0:T(8,128)S(1)}, s32[32,1664]{1,0:T(8,128)S(1)}, u32[]{:S(2)}, u32[]{:S(2)}) collective-permute-start(s32[32,1664]{1,0:T(8,128)S(1)} %constant_dynamic-update-slice_fusion), channel_id=1, source_target_pairs={{2,4},{6,8},{10,12},{14,16},{18,20},{22,24},{26,28},{4,2},{8,6},{1... | collective-permute-start | bytes 638984 | tf_op jit(solution)/shard_map/ppermute | solution.py:508
  28.9 2.6 %collective-permute-start.4 = (s32[32,1664]{1,0:T(8,128)S(1)}, s32[32,1664]{1,0:T(8,128)S(1)}, u32[]{:S(2)}, u32[]{:S(2)}) collective-permute-start(s32[32,1664]{1,0:T(8,128)S(1)} %constant_dynamic-update-slice_fusion), channel_id=1, source_target_pairs={{0,2},{4,6},{8,10},{12,14},{16,18},{20,22},{24,26},{28,30},{2,0},{... | collective-permute-start | bytes 638984 | tf_op jit(solution)/shard_map/ppermute | solution.py:508
  31.4 5.2 %target_sample_b.1.refs_1_ = f32[96,128]{1,0:T(8,128)S(1)} custom-call(s32[128,384]{1,0:T(8,128)S(1)} %bitcast.17, bf16[576,512]{1,0:T(8,128)(2,1)S(1)} %get-tuple-element.42.field_ref, s32[64,1536]{1,0:T(8,128)S(1)} %get-tuple-element.43.word_ref, f32[8,128]{1,0:T(8,128)S(1)} %get-tuple-element.44.scale_ref), custom_call_target="tpu_custom_call" | custom-call | flops 7247757312 | bytes 1773568 | tf_op jit(solution)/shard_map/target_sample_b/pallas_call | solution.py:461
  36.6 0.0 collective-permute-done.5.refs_4_
  36.6 0.0 collective-permute-done.4.refs_3_
  36.6 0.0 copy-done.1
  36.6 2.0 %model_fields.1 = (bf16[576,512]{1,0:T(8,128)(2,1)S(1)}, s32[64,1536]{1,0:T(8,128)S(1)}, f32[8,128]{1,0:T(8,128)S(1)}, f32[8,128]{1,0:T(8,128)S(1)}) custom-call(s32[1]{0:T(128)} %bitcast.6.index_ref, bf16[8,160,576]{2,1,0:T(8,128)(2,1)S(1)} %copy-done.1, f32[32,1536]{1,0:T(8,128)S(1)} %bitcast.13, s32[16,1664]{1,0:T(8,128)S(1)} %collective-permute-done.refs_0_, ...), custom_call_target="tpu_custom_call" | custom-call | bytes 3981316 | tf_op jit(solution)/shard_map/model_fields/pallas_call | solution.py:461
  38.7 0.0 copy-start.3
  38.7 6.9 %model_sample.1.refs_2_ = f32[128,128]{1,0:T(8,128)S(1)} custom-call(s32[128,384]{1,0:T(8,128)S(1)} %bitcast.18, bf16[576,512]{1,0:T(8,128)(2,1)S(1)} %get-tuple-element.53.field_ref, s32[64,1536]{1,0:T(8,128)S(1)} %get-tuple-element.54.word_ref, f32[8,128]{1,0:T(8,128)S(1)} %get-tuple-element.55.scale_ref), custom_call_target="tpu_custom_call" | custom-call | flops 9663676416 | bytes 1773568 | tf_op jit(solution)/shard_map/model_sample/pallas_call | solution.py:461
  45.7 0.2 join.1
  45.8 11.7 %all_to_all.22 = f32[16,1,128]{2,1,0:T(1,128)S(1)} all-to-all(f32[16,1,128]{2,1,0:T(1,128)S(1)} %bitcast.19), channel_id=1, replica_groups=mesh['brick'=16,'relay'=2] {'brick'}, dimensions={0} | all-to-all | bytes 16384 | tf_op jit(solution)/shard_map/all_to_all | solution.py:662
  57.5 0.0 copy-done.3
  57.5 0.9 %finish.1 = f32[6,64]{1,0:T(8,128)} custom-call(s32[8,64]{1,0:T(8,128)S(1)} %copy-done.3, f32[16,128]{1,0:T(8,128)S(1)} %bitcast.20), custom_call_target="tpu_custom_call" | custom-call | bytes 10240 | tf_op jit(solution)/shard_map/finish/pallas_call | solution.py:461
  (7 shorter events, 0.2 us)
Async XLA Ops:
  2.2 16.4 %all-to-all-start = ((s32[16,8,384]{2,1,0:T(8,128)}), s32[16,8,384]{2,1,0:T(8,128)S(1)}, u32[]{:S(2)}, u32[]{:S(2)}) async-start(s32[16,8,384]{2,1,0:T(8,128)} %bitcast.21), calls=%async_computation | async-start | bytes 393216 | tf_op jit(solution)/shard_map/all_to_all | solution.py:602
  9.6 5.5 %collective-permute-start = (s32[16,1664]{1,0:T(8,128)}, s32[16,1664]{1,0:T(8,128)S(1)}, u32[]{:S(2)}, u32[]{:S(2)}) collective-permute-start(s32[16,1664]{1,0:T(8,128)} %get-tuple-element.34), channel_id=1, source_target_pairs={{0,1},{1,0},{2,3},{3,2},{4,5},{5,4},{6,7},{7,6},{8,9},{9,8},{10,11... | collective-permute-start | bytes 319496 | tf_op jit(solution)/shard_map/ppermute | solution.py:515
  15.2 7.2 %collective-permute-start.1 = (s32[16,1664]{1,0:T(8,128)S(1)}, s32[16,1664]{1,0:T(8,128)S(1)}, u32[]{:S(2)}, u32[]{:S(2)}) collective-permute-start(s32[16,1664]{1,0:T(8,128)S(1)} %select_n.32), channel_id=1, source_target_pairs={{0,2},{4,6},{8,10},{12,14},{16,18},{20,22},{24,26},{28,30},{2,0},{... | collective-permute-start | bytes 319496 | tf_op jit(solution)/shard_map/ppermute | solution.py:508
  15.3 7.1 %collective-permute-start.2 = (s32[16,1664]{1,0:T(8,128)S(1)}, s32[16,1664]{1,0:T(8,128)S(1)}, u32[]{:S(2)}, u32[]{:S(2)}) collective-permute-start(s32[16,1664]{1,0:T(8,128)S(1)} %select_n.34), channel_id=1, source_target_pairs={{2,4},{6,8},{10,12},{14,16},{18,20},{22,24},{26,28},{4,2},{8,6},{1... | collective-permute-start | bytes 319496 | tf_op jit(solution)/shard_map/ppermute | solution.py:508
  18.6 5.4 %copy-start = (f32[4,8,1536]{2,1,0:T(8,128)S(1)}, f32[4,8,1536]{2,1,0:T(8,128)}, u32[]{:S(2)}) copy-start(f32[4,8,1536]{2,1,0:T(8,128)} %param.8) | copy-start | bytes 589828
  18.6 5.4 %copy-start.2 = (bf16[8,96,384]{2,1,0:T(8,128)(2,1)S(1)}, bf16[8,96,384]{2,1,0:T(8,128)(2,1)}, u32[]{:S(2)}) copy-start(bf16[8,96,384]{2,1,0:T(8,128)(2,1)} %constant.68.clone.tables_ref) | copy-start | bytes 1769476
  22.4 5.4 %collective-permute-start.3 = (s32[16,1664]{1,0:T(8,128)S(1)}, s32[16,1664]{1,0:T(8,128)S(1)}, u32[]{:S(2)}, u32[]{:S(2)}) collective-permute-start(s32[16,1664]{1,0:T(8,128)S(1)} %get-tuple-element.47), channel_id=1, source_target_pairs={{0,1},{1,0},{2,3},{3,2},{4,5},{5,4},{6,7},{7,6},{8,9},{9,8},{10,11... | collective-permute-start | bytes 319496 | tf_op jit(solution)/shard_map/ppermute | solution.py:515
  27.9 8.8 %copy-start.1 = (bf16[8,160,576]{2,1,0:T(8,128)(2,1)S(1)}, bf16[8,160,576]{2,1,0:T(8,128)(2,1)}, u32[]{:S(2)}) copy-start(bf16[8,160,576]{2,1,0:T(8,128)(2,1)} %constant.69.clone.tables_ref) | copy-start | bytes 4423684
  27.9 8.7 %collective-permute-start.5 = (s32[32,1664]{1,0:T(8,128)S(1)}, s32[32,1664]{1,0:T(8,128)S(1)}, u32[]{:S(2)}, u32[]{:S(2)}) collective-permute-start(s32[32,1664]{1,0:T(8,128)S(1)} %constant_dynamic-update-slice_fusion), channel_id=1, source_target_pairs={{2,4},{6,8},{10,12},{14,16},{18,20},{22,24},{26,28},{4,2},{8,6},{1... | collective-permute-start | bytes 638984 | tf_op jit(solution)/shard_map/ppermute | solution.py:508
  28.9 7.8 %collective-permute-start.4 = (s32[32,1664]{1,0:T(8,128)S(1)}, s32[32,1664]{1,0:T(8,128)S(1)}, u32[]{:S(2)}, u32[]{:S(2)}) collective-permute-start(s32[32,1664]{1,0:T(8,128)S(1)} %constant_dynamic-update-slice_fusion), channel_id=1, source_target_pairs={{0,2},{4,6},{8,10},{12,14},{16,18},{20,22},{24,26},{28,30},{2,0},{... | collective-permute-start | bytes 638984 | tf_op jit(solution)/shard_map/ppermute | solution.py:508
  38.7 18.8 %copy-start.3 = (s32[8,64]{1,0:T(8,128)S(1)}, s32[8,64]{1,0:T(8,128)}, u32[]{:S(2)}) copy-start(s32[8,64]{1,0:T(8,128)} %get-tuple-element.31.place_ref) | copy-start | bytes 6148
